TPU v7x, 32 devices: a whole 2x2x4 slice. The times are simulated.
32 devices in a mesh: dp: 16 (over z, y, core), mp: 2 (over x).
Axes of the slice: x: 2, y: 2, z: 4, core: 2. Of those that a mesh axis runs over, the one named last changes fastest.
Arguments:
- patches: bfloat16 [16384, 4096], P('dp', 'mp'), may hold values from -6 to 6
- labels: int32 [32, 4096], P(('dp', 'mp')), may hold values from 0 to 13
- batch_ids: int32 [32], P(('dp', 'mp')), may hold values from 0 to 3
- blocks: float32 [16, 2, 24, 128, 128], P('dp', 'mp'), may hold values from -0.21875 to 0.21875
- statistics: float32 [2, 16, 2, 24, 128, 128], P(None, 'dp', 'mp'), as said below
- roots: float32 [2, 16, 2, 24, 128, 128], P(None, 'dp', 'mp'), as said below
- moments: float32 [16, 2, 24, 128, 128], P('dp', 'mp'), may hold values from -1.9073486e-05 to 1.9073486e-05
- velocity: float32 [16, 2, 24, 128, 128], P('dp', 'mp'), may hold values from 1.9169148e-15 to 7.667659e-15
- aux: float32 [458878], replicated
- aux_moment: float32 [458878], replicated, may hold values from -1.1444092e-05 to 1.1444092e-05
- aux_velocity: float32 [458878], replicated, may hold values from 4.792287e-14 to 1.9169148e-13
Outputs:
- loss: float32 [], replicated
- grad_norm: float32 [], replicated
- new_blocks: float32 [16, 2, 24, 128, 128], P('dp', 'mp')
- new_statistics: float32 [2, 16, 2, 24, 128, 128], P(None, 'dp', 'mp')
- new_moments: float32 [16, 2, 24, 128, 128], P('dp', 'mp')
- new_velocity: float32 [16, 2, 24, 128, 128], P('dp', 'mp')
- new_aux: float32 [458878], replicated
- new_aux_moment: float32 [458878], replicated
- new_aux_velocity: float32 [458878], replicated
Inputs may be any that keep to these rules, and one draw needn't show every extreme that they name: `statistics`: symmetric in the last two dimensions. `roots`: symmetric in the last two dimensions, diagonal entries positive.
All inputs are finite; a program needn't handle non-finite values.
Results may differ from a plain program's by a relative error of at most 0.00045.
The roundings to bfloat16 on the way count: a program that leaves them out, or rounds other values in their place, can miss the bound.
Values may be sent and summed in bfloat16 or wider, within the bound.
A program may use at most 320 MiB of HBM per device.

v0:
```python
import math

import jax
import jax.numpy as jnp
from jax import lax
from jax.sharding import PartitionSpec as P

D = 768
HDIM = 64
FF = 3072
PV = 4096
DEC = 128
CF = 16
NCLS = 14
GS = 8
MB = 4
STEP = 10
BS = 128
NTOK = 512
CELLS = 4096


HIGHEST = lax.Precision.HIGHEST
beta_one = 0.9
beta_two = 0.999
beta_stat = 0.95
learn_rate = 0.02
decay_rate = 0.01
clip_value = 0.005


def product(operand, factor):
    return jnp.dot(operand, factor, preferred_element_type=jnp.float32)


def inner_rows(operand, factor):
    return lax.dot_general(
        operand, factor, (((0,), (0,)), ((), ())), preferred_element_type=jnp.float32
    )


def product_t(operand, factor):
    return lax.dot_general(
        operand, factor, (((1,), (1,)), ((), ())), preferred_element_type=jnp.float32
    )


def layer_norm(values, norm_gain, norm_shift):
    center = values - jnp.mean(values, -1, keepdims=True)
    spread = jnp.mean(center * center, -1, keepdims=True)
    return center * lax.rsqrt(spread + 1e-06) * norm_gain + norm_shift


def gelu(values):
    return jax.nn.gelu(values, approximate=False)


def aux_layout():
    return [
        ("positions", (NTOK, D)),
        ("embed_bias", (D,)),
        ("norm_gain", (2, D)),
        ("norm_bias", (2, D)),
        ("qv_bias", (2, D)),
        ("proj_bias", (D,)),
        ("up_bias", (FF,)),
        ("down_bias", (D,)),
        ("deconv_bias", (DEC,)),
        ("conv_weight", (27 * DEC, CF)),
        ("conv_bias", (CF,)),
        ("head_weight", (CF, NCLS)),
        ("head_bias", (NCLS,)),
    ]


def split_aux(vector):
    pieces = {}
    offset = 0
    for section_name, section_shape in aux_layout():
        length = math.prod(section_shape)
        pieces[section_name] = vector[offset : offset + length].reshape(section_shape)
        offset += length
    return pieces


def local_shapes(mp_count):
    return [
        (PV // mp_count, D),
        (D, 3 * D // mp_count),
        (D // mp_count, D),
        (D, FF // mp_count),
        (FF // mp_count, D),
        (3 * D // mp_count, 8 * DEC),
    ]


def from_blocks(blocks, shapes):
    matrices = []
    offset = 0
    for height, breadth in shapes:
        number = height * breadth // (BS * BS)
        piece = blocks[offset : offset + number]
        matrices.append(
            piece.reshape(height // BS, breadth // BS, BS, BS)
            .transpose(0, 2, 1, 3)
            .reshape(height, breadth)
        )
        offset += number
    return matrices


def to_blocks(matrices):
    return jnp.concatenate(
        [
            matrix.reshape(matrix.shape[0] // BS, BS, matrix.shape[1] // BS, BS)
            .transpose(0, 2, 1, 3)
            .reshape(-1, BS, BS)
            for matrix in matrices
        ],
        0,
    )


def fetch_weights(blocks, mp_count):
    gathered = lax.all_gather(blocks.astype(jnp.bfloat16), "dp", axis=0, tiled=True)
    return from_blocks(gathered.reshape(-1, BS, BS), local_shapes(mp_count))


def to_grid(flat):
    volumes = flat.shape[0]
    shaped = flat.reshape(volumes, GS, GS, GS, 2, 2, 2, DEC).transpose(0, 1, 4, 2, 5, 3, 6, 7)
    return shaped.reshape(volumes, 2 * GS, 2 * GS, 2 * GS, DEC)


def from_grid(volume):
    volumes = volume.shape[0]
    shaped = volume.reshape(volumes, GS, 2, GS, 2, GS, 2, DEC).transpose(0, 1, 3, 5, 2, 4, 6, 7)
    return shaped.reshape(volumes, NTOK, 8 * DEC)


def offset_list():
    return [
        (depth_at, row_at, col_at)
        for depth_at in range(3)
        for row_at in range(3)
        for col_at in range(3)
    ]


def im2col(volume):
    extent = volume.shape[1]
    padded = jnp.pad(volume, ((0, 0), (1, 1), (1, 1), (1, 1), (0, 0)))
    slabs = [
        padded[
            :, depth_at : depth_at + extent, row_at : row_at + extent, col_at : col_at + extent, :
        ]
        for depth_at, row_at, col_at in offset_list()
    ]
    return jnp.concatenate(slabs, -1).reshape(-1, 27 * volume.shape[-1])


def col2im(columns, volumes):
    extent = 2 * GS
    channels = columns.shape[-1] // 27
    shaped = columns.reshape(volumes, extent, extent, extent, 27, channels)
    padded = jnp.zeros((volumes, extent + 2, extent + 2, extent + 2, channels), jnp.float32)
    for position, (depth_at, row_at, col_at) in enumerate(offset_list()):
        padded = padded.at[
            :, depth_at : depth_at + extent, row_at : row_at + extent, col_at : col_at + extent, :
        ].add(shaped[:, :, :, :, position, :])
    return padded[:, 1:-1, 1:-1, 1:-1, :]


def split_heads(tensor, crops_here):
    return tensor.reshape(crops_here, NTOK, -1, HDIM).transpose(0, 2, 1, 3)


def merge_heads(tensor):
    return tensor.transpose(0, 2, 1, 3).reshape(tensor.shape[0] * NTOK, -1)


def score_heads(queries, key_rows):
    return (
        jnp.einsum("chqd,chkd->chqk", queries, key_rows, preferred_element_type=jnp.float32) * 0.125
    )


def shampoo_step(blocks, grads, stat_pair, root_pair, moment, veloc):
    stat_left = beta_stat * stat_pair[0] + (1 - beta_stat) * jnp.einsum(
        "abcij,abckj->abcik", grads, grads, precision=HIGHEST
    )
    stat_right = beta_stat * stat_pair[1] + (1 - beta_stat) * jnp.einsum(
        "abcji,abcjk->abcik", grads, grads, precision=HIGHEST
    )
    moment_new = beta_one * moment + (1 - beta_one) * grads
    veloc_new = beta_two * veloc + (1 - beta_two) * grads * grads
    moment_hat = moment_new / (1 - beta_one**STEP)
    adam_dir = moment_hat / (jnp.sqrt(veloc_new / (1 - beta_two**STEP)) + 1e-08)
    left_side = jnp.einsum("abcij,abcjk->abcik", root_pair[0], moment_hat, precision=HIGHEST)
    precond = jnp.einsum("abcij,abcjk->abcik", left_side, root_pair[1], precision=HIGHEST)
    ratio = jnp.sqrt(
        (jnp.mean(adam_dir * adam_dir, (-2, -1), keepdims=True) + 1e-06)
        / (jnp.mean(precond * precond, (-2, -1), keepdims=True) + 1e-06)
    )
    block_new = blocks - learn_rate * (precond * ratio + decay_rate * blocks)
    return (block_new, jnp.stack([stat_left, stat_right]), moment_new, veloc_new)


def adam_step(param, grads, moment, veloc):
    moment_new = beta_one * moment + (1 - beta_one) * grads
    veloc_new = beta_two * veloc + (1 - beta_two) * grads * grads
    direction = (
        moment_new / (1 - beta_one**STEP) / (jnp.sqrt(veloc_new / (1 - beta_two**STEP)) + 1e-08)
    )
    return (param - learn_rate * direction, moment_new, veloc_new)


def local(
    patches,
    labels,
    batch_ids,
    blocks,
    statistics,
    roots,
    moments,
    velocity,
    aux,
    aux_moment,
    aux_velocity,
):
    mp_count = lax.axis_size("mp")
    part_index = lax.axis_index("mp")
    width_here = D // mp_count
    hidden_here = FF // mp_count
    total_rows = patches.shape[0]
    crops_here = total_rows // NTOK
    own_crops = crops_here // mp_count
    all_crops = crops_here * lax.axis_size("dp")
    pieces = split_aux(aux)
    norm_gain = pieces["norm_gain"]
    norm_shift = pieces["norm_bias"]
    w_embed, w_qkv, w_proj, w_up, w_down, w_deconv = fetch_weights(blocks, mp_count)
    query_bias = lax.dynamic_slice_in_dim(pieces["qv_bias"][0], part_index * width_here, width_here)
    value_bias = lax.dynamic_slice_in_dim(pieces["qv_bias"][1], part_index * width_here, width_here)
    up_bias = lax.dynamic_slice_in_dim(pieces["up_bias"], part_index * hidden_here, hidden_here)
    embedded = lax.psum(product(patches, w_embed), "mp")
    stream_zero = (
        embedded.reshape(crops_here, NTOK, D) + pieces["positions"] + pieces["embed_bias"]
    ).reshape(total_rows, D)
    normed_one = layer_norm(stream_zero, norm_gain[0], norm_shift[0]).astype(jnp.bfloat16)
    projected = product(normed_one, w_qkv)
    queries = split_heads((projected[:, :width_here] + query_bias).astype(jnp.bfloat16), crops_here)
    key_rows = split_heads(
        projected[:, width_here : 2 * width_here].astype(jnp.bfloat16), crops_here
    )
    value_rows = split_heads(
        (projected[:, 2 * width_here :] + value_bias).astype(jnp.bfloat16), crops_here
    )
    scores = score_heads(queries, key_rows)
    row_max = jnp.max(scores, -1, keepdims=True)
    log_total = row_max + jnp.log(jnp.sum(jnp.exp(scores - row_max), -1, keepdims=True))
    attention = jnp.exp(scores - log_total)
    mixed_heads = merge_heads(
        jnp.einsum(
            "chqk,chkd->chqd",
            attention.astype(jnp.bfloat16),
            value_rows,
            preferred_element_type=jnp.float32,
        ).astype(jnp.bfloat16)
    )
    stream_one = stream_zero + lax.psum(product(mixed_heads, w_proj), "mp") + pieces["proj_bias"]
    normed_two = layer_norm(stream_one, norm_gain[1], norm_shift[1]).astype(jnp.bfloat16)
    hidden = product(normed_two, w_up) + up_bias
    active = gelu(hidden).astype(jnp.bfloat16)
    stream_two = stream_one + lax.psum(product(active, w_down), "mp") + pieces["down_bias"]
    column_parts = [
        lax.dynamic_slice_in_dim(
            stream.astype(jnp.bfloat16), part_index * width_here, width_here, 1
        )
        for stream in (stream_zero, stream_one, stream_two)
    ]
    deconv_rows = w_deconv.reshape(3, width_here, 8 * DEC)
    partial_value = (
        product(column_parts[0], deconv_rows[0])
        + product(column_parts[1], deconv_rows[1])
        + product(column_parts[2], deconv_rows[2])
    )
    upsampled = lax.psum_scatter(
        partial_value.reshape(crops_here, NTOK, 8 * DEC), "mp", scatter_dimension=0, tiled=True
    )
    cell_grid = to_grid(upsampled) + pieces["deconv_bias"]
    conv_in = gelu(cell_grid).astype(jnp.bfloat16)
    columns = im2col(conv_in)
    conv_weight = pieces["conv_weight"].astype(jnp.bfloat16)
    conved = product(columns, conv_weight) + pieces["conv_bias"]
    features = gelu(conved).astype(jnp.bfloat16)
    head_weight = pieces["head_weight"].astype(jnp.bfloat16)
    logits = (product(features, head_weight) + pieces["head_bias"]).reshape(own_crops, CELLS, NCLS)
    target = (labels[:, :, None] == jnp.arange(NCLS, dtype=jnp.int32)).astype(jnp.float32)
    batch_onehot = (batch_ids[:, None] == jnp.arange(MB, dtype=jnp.int32)).astype(jnp.float32)

    def tail_terms(logit_values):
        log_prob = jax.nn.log_softmax(logit_values, -1)
        chance = jnp.exp(log_prob)
        intersection = jnp.einsum(
            "cm,ck->mk", batch_onehot, jnp.sum(chance * target, 1), precision=HIGHEST
        )
        predicted = jnp.einsum("cm,ck->mk", batch_onehot, jnp.sum(chance, 1), precision=HIGHEST)
        return (intersection, predicted, -jnp.sum(log_prob * target))

    local_terms, tail_back = jax.vjp(tail_terms, logits)
    truth_local = jnp.einsum("cm,ck->mk", batch_onehot, jnp.sum(target, 1), precision=HIGHEST)
    intersection_all, predicted_all, entropy_all, truth_all = lax.psum(
        (local_terms[0], local_terms[1], local_terms[2], truth_local), ("dp", "mp")
    )

    def total_loss(intersection_sum, predicted_sum, entropy_sum):
        dice_ratio = (2 * intersection_sum + 1) / (predicted_sum + truth_all + 1)
        return entropy_sum / (all_crops * CELLS) + jnp.mean(1 - jnp.mean(dice_ratio, 1))

    loss_value, loss_grads = jax.value_and_grad(total_loss, (0, 1, 2))(
        intersection_all, predicted_all, entropy_all
    )
    grad_logits = tail_back(loss_grads)[0].reshape(own_crops * CELLS, NCLS)
    grad_head_bias = jnp.sum(grad_logits, 0)
    logits_low = grad_logits.astype(jnp.bfloat16)
    grad_head_weight = inner_rows(features, logits_low)
    _, conved_back = jax.vjp(gelu, conved)
    back_conved = conved_back(product_t(logits_low, head_weight))[0]
    grad_conv_bias = jnp.sum(back_conved, 0)
    conved_low = back_conved.astype(jnp.bfloat16)
    grad_conv_weight = inner_rows(columns, conved_low)
    back_conv_in = col2im(product_t(conved_low, conv_weight), own_crops)
    _, grid_back = jax.vjp(gelu, cell_grid)
    back_grid = grid_back(back_conv_in)[0]
    grad_deconv_bias = jnp.sum(back_grid, (0, 1, 2, 3))
    back_up = from_grid(back_grid).astype(jnp.bfloat16)
    every_up = lax.all_gather(back_up, "mp", axis=0, tiled=True).reshape(total_rows, 8 * DEC)
    grad_deconv = jnp.concatenate(
        [inner_rows(column_parts[which], every_up) for which in range(3)], 0
    )
    half_backs = jnp.stack([product_t(every_up, deconv_rows[which]) for which in range(3)])
    stream_backs = lax.all_gather(half_backs.astype(jnp.bfloat16), "mp", axis=2, tiled=True).astype(
        half_backs.dtype
    )
    back_two = stream_backs[2]
    grad_down_bias = jnp.sum(back_two, 0)
    two_low = back_two.astype(jnp.bfloat16)
    grad_down = inner_rows(active, two_low)
    _, hidden_back = jax.vjp(gelu, hidden)
    back_hidden = hidden_back(product_t(two_low, w_down))[0].astype(jnp.bfloat16)
    grad_up_bias = jnp.sum(back_hidden.astype(jnp.float32), 0)
    grad_up = inner_rows(normed_two, back_hidden)
    back_normed_two = lax.psum(product_t(back_hidden, w_up).astype(jnp.bfloat16), "mp").astype(
        jnp.float32
    )
    _, second_back = jax.vjp(layer_norm, stream_one, norm_gain[1], norm_shift[1])
    back_norm_two, grad_gain_two, grad_shift_two = second_back(back_normed_two)
    back_one = back_two + stream_backs[1] + back_norm_two
    grad_proj_bias = jnp.sum(back_one, 0)
    one_low = back_one.astype(jnp.bfloat16)
    grad_proj = inner_rows(mixed_heads, one_low)
    back_mixed = split_heads(product_t(one_low, w_proj).astype(jnp.bfloat16), crops_here)
    attention = jnp.exp(score_heads(queries, key_rows) - log_total)
    back_attention = jnp.einsum(
        "chqd,chkd->chqk", back_mixed, value_rows, preferred_element_type=jnp.float32
    )
    back_values = jnp.einsum(
        "chqk,chqd->chkd",
        attention.astype(jnp.bfloat16),
        back_mixed,
        preferred_element_type=jnp.float32,
    ).astype(jnp.bfloat16)
    back_scores = (
        attention * (back_attention - jnp.sum(back_attention * attention, -1, keepdims=True))
    ).astype(jnp.bfloat16)
    back_queries = (
        jnp.einsum("chqk,chkd->chqd", back_scores, key_rows, preferred_element_type=jnp.float32)
        * 0.125
    ).astype(jnp.bfloat16)
    back_keys = (
        jnp.einsum("chqk,chqd->chkd", back_scores, queries, preferred_element_type=jnp.float32)
        * 0.125
    ).astype(jnp.bfloat16)
    query_flat = merge_heads(back_queries)
    value_flat = merge_heads(back_values)
    back_projected = jnp.concatenate([query_flat, merge_heads(back_keys), value_flat], 1)
    grad_qkv = inner_rows(normed_one, back_projected)
    grad_query_bias = jnp.sum(query_flat.astype(jnp.float32), 0)
    grad_value_bias = jnp.sum(value_flat.astype(jnp.float32), 0)
    back_normed_one = lax.psum(product_t(back_projected, w_qkv).astype(jnp.bfloat16), "mp").astype(
        jnp.float32
    )
    _, first_back = jax.vjp(layer_norm, stream_zero, norm_gain[0], norm_shift[0])
    back_norm_one, grad_gain_one, grad_shift_one = first_back(back_normed_one)
    back_zero = back_one + stream_backs[0] + back_norm_one
    grad_embed_bias = jnp.sum(back_zero, 0)
    grad_positions = jnp.sum(back_zero.reshape(crops_here, NTOK, D), 0)
    grad_embed = inner_rows(patches, back_zero.astype(jnp.bfloat16))
    inverse = 1.0 / mp_count
    query_full = lax.dynamic_update_slice_in_dim(
        jnp.zeros((D,), jnp.float32), grad_query_bias, part_index * width_here, 0
    )
    value_full = lax.dynamic_update_slice_in_dim(
        jnp.zeros((D,), jnp.float32), grad_value_bias, part_index * width_here, 0
    )
    up_full = lax.dynamic_update_slice_in_dim(
        jnp.zeros((FF,), jnp.float32), grad_up_bias, part_index * hidden_here, 0
    )
    grad_aux = jnp.concatenate(
        [
            grad_positions.reshape(-1) * inverse,
            grad_embed_bias * inverse,
            jnp.concatenate([grad_gain_one, grad_gain_two]) * inverse,
            jnp.concatenate([grad_shift_one, grad_shift_two]) * inverse,
            query_full,
            value_full,
            grad_proj_bias * inverse,
            up_full,
            grad_down_bias * inverse,
            grad_deconv_bias,
            grad_conv_weight.reshape(-1),
            grad_conv_bias,
            grad_head_weight.reshape(-1),
            grad_head_bias,
        ]
    )
    grad_local = to_blocks([grad_embed, grad_qkv, grad_proj, grad_up, grad_down, grad_deconv])
    aux_total = lax.psum(grad_aux, ("dp", "mp"))
    owned = lax.psum_scatter(
        grad_local.reshape(lax.axis_size("dp"), 1, -1, BS, BS),
        "dp",
        scatter_dimension=0,
        tiled=True,
    )
    block_square = lax.psum(jnp.sum(owned * owned), ("dp", "mp"))
    grad_norm = jnp.sqrt(block_square + jnp.sum(aux_total * aux_total))
    clip_scale = clip_value / jnp.maximum(grad_norm, clip_value)
    block_new, stat_new, moment_new, veloc_new = shampoo_step(
        blocks, owned * clip_scale, statistics, roots, moments, velocity
    )
    aux_new, aux_moment_new, aux_veloc_new = adam_step(
        aux, aux_total * clip_scale, aux_moment, aux_velocity
    )
    return (
        loss_value,
        grad_norm,
        block_new,
        stat_new,
        moment_new,
        veloc_new,
        aux_new,
        aux_moment_new,
        aux_veloc_new,
    )


def solution(mesh):
    placed = (
        P("dp", "mp"),
        P(("dp", "mp"), None),
        P(("dp", "mp")),
        P("dp", "mp", None, None, None),
        P(None, "dp", "mp", None, None, None),
        P(None, "dp", "mp", None, None, None),
        P("dp", "mp", None, None, None),
        P("dp", "mp", None, None, None),
        P(),
        P(),
        P(),
    )
    return jax.shard_map(
        local,
        mesh=mesh,
        in_specs=placed,
        out_specs=(
            P(),
            P(),
            P("dp", "mp", None, None, None),
            P(None, "dp", "mp", None, None, None),
            P("dp", "mp", None, None, None),
            P("dp", "mp", None, None, None),
            P(),
            P(),
            P(),
        ),
        check_vma=False,
    )
```

profile of v0, /device:TPU:0, one launch (start us, length us, event | category | flops | bytes accessed | tf_op | source)
XLA Modules:
  0.0 1817.0 jit_solution(7773721581910772968)
XLA Ops:
  9.7 104.6 %all-gather.4.cloned.1.call-done = bf16[16,1,24,128,128]{4,3,2,1,0:T(8,128)(2,1)} async-done(((bf16[1,1,24,128,128]{4,3,2,1,0:T(8,128)(2,1)}), bf16[16,1,24,128,128]{4,3,2,1,0:T(8,128)(2,1)}) %all-gather.4.cloned.1.call-update) | async-done | bytes 12582928 | tf_op jit(solution)/shard_map/all_gather | solution.py:125
  119.3 8.3 fusion.33
  137.8 74.0 %all-reduce.11.cloned.1.call-done = f32[1024,768]{1,0:T(8,128)} async-done(((f32[1024,768]{1,0:T(8,128)}), f32[1024,768]{1,0:T(8,128)}) %all-reduce.11.cloned.1.call-update) | async-done | bytes 3145744 | tf_op jit(solution)/shard_map/psum | solution.py:246
  246.9 7.0 fusion.145
  272.3 72.1 %all-reduce.13.cloned.1.call-done = f32[1024,768]{1,0:T(8,128)} async-done(((f32[1024,768]{1,0:T(8,128)}), f32[1024,768]{1,0:T(8,128)}) %all-reduce.13.cloned.1.call-update) | async-done | bytes 3145744 | tf_op jit(solution)/shard_map/psum | solution.py:271
  349.8 15.4 fusion.1
  386.8 73.2 %all-reduce.15.cloned.1.call-done = f32[1024,768]{1,0:T(8,128)} async-done(((f32[1024,768]{1,0:T(8,128)}), f32[1024,768]{1,0:T(8,128)}) %all-reduce.15.cloned.1.call-update) | async-done | bytes 3145744 | tf_op jit(solution)/shard_map/psum | solution.py:275
  461.7 7.0 add_add_fusion.2
  475.2 48.1 %reduce-scatter.3.cloned.1.call-done = f32[1,512,1024]{2,1,0:T(8,128)} async-done(((f32[2,512,1024]{2,1,0:T(8,128)}), f32[1,512,1024]{2,1,0:T(8,128)}) %reduce-scatter.3.cloned.1.call-update) | async-done | bytes 2097168 | tf_op jit(solution)/shard_map/reduce_scatter | solution.py:288
  536.1 6.7 pad_slice_fusion
  580.2 14.3 multiply_convert_fusion.6
  595.2 39.5 %all-reduce.3 = (f32[4,14]{1,0:T(4,128)S(1)}, f32[4,14]{1,0:T(4,128)S(1)}) all-reduce(f32[4,14]{1,0:T(4,128)S(1)} %get-tuple-element.422, f32[4,14]{1,0:T(4,128)S(1)} %get-tuple-element.421), channel_id=1, replica_groups=mesh['dp'=16,'mp'=2] {'dp','mp'}, use_global_device_ids=true, to_apply=%region_17.18 | all-reduce | flops 112 | bytes 896 | tf_op jit(solution)/shard_map/psum | solution.py:313
  639.3 22.9 %convolution_bitcast_fusion = f32[1,16,16,16,27,128]{5,3,4,2,1,0:T(8,128)} fusion(bf16[16,16,16,16,1]{3,2,4,1,0:T(8,128)(2,1)S(1)} %bitcast.636, bf16[27,128,16]{2,1,0:T(8,128)(2,1)} %convert_element_type.214), kind=kOutput, calls=%fused_computation | convolution fusion | flops 452984832 | bytes 56864768 | tf_op jit(solution)/shard_map/dot_general | solution.py:43
  669.6 12.9 scatter-add.91
  686.7 12.9 scatter-add.94
  707.8 12.9 scatter-add.96
  726.8 14.8 scatter-add.99
  749.8 12.9 scatter-add.101
  766.9 12.9 scatter-add.104
  788.0 12.9 scatter-add.106
  805.1 13.1 scatter-add.109
  826.5 12.9 scatter-add.111
  843.6 12.9 scatter-add.114
  864.7 12.9 scatter-add.116
  881.8 12.9 scatter-add.119
  903.0 12.9 scatter-add.121
  920.1 12.9 scatter-add.124
  941.3 12.9 scatter-add.126
  958.4 12.9 scatter-add.129
  979.6 12.9 scatter-add.131
  996.8 12.9 scatter-add.134
  1015.6 33.6 %all-gather.6.cloned.1.call-done = bf16[2,512,1024]{2,1,0:T(8,128)(2,1)} async-done(((bf16[1,512,1024]{2,1,0:T(8,128)(2,1)}), bf16[2,512,1024]{2,1,0:T(8,128)(2,1)}) %all-gather.6.cloned.1.call-update) | async-done | bytes 2097168 | tf_op jit(solution)/shard_map/all_gather | solution.py:338
  1056.6 62.7 %all-gather.8.cloned.1.call-done = bf16[3,1024,768]{2,1,0:T(8,128)(2,1)} async-done(((bf16[3,1024,384]{2,1,0:T(8,128)(2,1)}), bf16[3,1024,768]{2,1,0:T(8,128)(2,1)}) %all-gather.8.cloned.1.call-update) | async-done | bytes 4718608 | tf_op jit(solution)/shard_map/all_gather | solution.py:343
  1122.5 11.7 convert_reduce_fusion
  1140.0 15.1 fusion.4
  1169.8 21.6 %all-reduce.17.cloned.1.call-done = bf16[1024,768]{1,0:T(8,128)(2,1)} async-done(((bf16[1024,768]{1,0:T(8,128)(2,1)}), bf16[1024,768]{1,0:T(8,128)(2,1)}) %all-reduce.17.cloned.1.call-update) | async-done | bytes 1572880 | tf_op jit(solution)/shard_map/psum | solution.py:354
  1211.5 8.7 convert_reduce_fusion.3
  1220.2 9.4 multiply_reduce_fusion
  1229.6 7.4 multiply_convert_fusion
  1249.0 7.9 fusion.244
  1257.0 6.8 reshape.2130
  1282.2 18.4 %all-reduce.19.cloned.1.call-done = bf16[1024,768]{1,0:T(8,128)(2,1)} async-done(((bf16[1024,768]{1,0:T(8,128)(2,1)}), bf16[1024,768]{1,0:T(8,128)(2,1)}) %all-reduce.19.cloned.1.call-update) | async-done | bytes 1572880 | tf_op jit(solution)/shard_map/psum | solution.py:391
  1323.4 6.6 copy.313
  1359.3 18.2 %fusion.269 = f32[3456,16]{1,0:T(8,128)} fusion(bf16[4096,3456]{1,0:T(8,128)(2,1)} %constant_dynamic-update-slice_fusion, bf16[4096,16]{0,1:T(8,128)(2,1)S(1)} %copy-done.77), kind=kOutput, calls=%fused_computation.485 | convolution fusion | flops 452984832 | bytes 28663808 | tf_op jit(solution)/shard_map/dot_general | solution.py:37
  1387.2 16.8 concatenate.207
  1406.0 195.6 %reduce-scatter.5.cloned.1.call-done = f32[1,1,24,128,128]{4,3,2,1,0:T(8,128)} async-done(((f32[16,1,24,128,128]{4,3,2,1,0:T(8,128)}), f32[1,1,24,128,128]{4,3,2,1,0:T(8,128)}) %reduce-scatter.5.cloned.1.call-update) | async-done | bytes 1572880 | tf_op jit(solution)/shard_map/reduce_scatter | solution.py:430
  1604.1 134.9 %all-reduce.21.cloned.1.call-done = f32[458878]{0:T(1024)} async-done(((f32[458878]{0:T(1024)}), f32[458878]{0:T(1024)}) %all-reduce.21.cloned.1.call-update) | async-done | bytes 1835528 | tf_op jit(solution)/shard_map/psum | solution.py:429
  1741.6 40.6 %all-reduce.2 = (f32[]{:T(128)}, f32[]{:T(128)}) all-reduce(f32[]{:T(128)S(6)} %neg.65, f32[]{:T(128)} %multiply_reduce_fusion.7), channel_id=1, replica_groups=mesh['dp'=16,'mp'=2] {'dp','mp'}, use_global_device_ids=true, to_apply=%region_13.14 | all-reduce | flops 2 | bytes 16 | tf_op jit(solution)/shard_map/psum | solution.py:313
  (498 shorter events, 451.6 us)
Async XLA Ops:
  7.2 107.2 %all-gather.4.cloned.1.call-start = ((), (), s32[]{:S(2)}) async-start(), calls=%async_computation.2 | async-start | bytes 13369344 | tf_op jit(solution)/shard_map/all_gather | solution.py:125
  9.7 202.0 %all-reduce.11.cloned.1.call-start = ((), (), s32[]{:S(2)}) async-start(), calls=%async_computation.3 | async-start | bytes 6291456 | tf_op jit(solution)/shard_map/psum | solution.py:246
  127.6 216.8 %all-reduce.13.cloned.1.call-start = ((), (), s32[]{:S(2)}) async-start(), calls=%async_computation.4 | async-start | bytes 6291456 | tf_op jit(solution)/shard_map/psum | solution.py:271
  130.4 84.6 %copy-start.82 = (f32[768]{0:T(1024)}, f32[768]{0:T(1024)S(1)}, u32[]{:S(2)}) copy-start(f32[768]{0:T(1024)S(1)} %get-tuple-element.388) | copy-start | bytes 9220
  130.5 84.6 %copy-start.96 = (f32[768]{0:T(1024)}, f32[768]{0:T(1024)S(1)}, u32[]{:S(2)}) copy-start(f32[768]{0:T(1024)S(1)} %get-tuple-element.387) | copy-start | bytes 9220
  130.5 216.8 %copy-start.84 = (f32[768]{0:T(1024)}, f32[768]{0:T(1024)S(1)}, u32[]{:S(2)}) copy-start(f32[768]{0:T(1024)S(1)} %get-tuple-element.383) | copy-start | bytes 9220
  130.5 216.8 %copy-start.104 = (f32[768]{0:T(1024)}, f32[768]{0:T(1024)S(1)}, u32[]{:S(2)}) copy-start(f32[768]{0:T(1024)S(1)} %get-tuple-element.382) | copy-start | bytes 9220
  214.5 164.2 %copy-start.1 = (f32[1024,768]{1,0:T(8,128)}, f32[1024,768]{1,0:T(8,128)S(1)}, u32[]{:S(2)}) copy-start(f32[1024,768]{1,0:T(8,128)S(1)} %get-tuple-element.370) | copy-start | bytes 9437188
  241.3 12.6 copy-start.72
  258.5 201.5 %all-reduce.15.cloned.1.call-start = ((), (), s32[]{:S(2)}) async-start(), calls=%async_computation.5 | async-start | bytes 6291456 | tf_op jit(solution)/shard_map/psum | solution.py:275
  259.1 106.1 %copy-start.94 = (f32[1536]{0:T(1024)}, f32[1536]{0:T(1024)S(1)}, u32[]{:S(2)}) copy-start(f32[1536]{0:T(1024)S(1)} %dynamic_slice.22) | copy-start | bytes 18436
  346.7 18.4 %copy-start.3 = (f32[1024,768]{1,0:T(8,128)}, f32[1024,768]{1,0:T(8,128)S(1)}, u32[]{:S(2)}) copy-start(f32[1024,768]{1,0:T(8,128)S(1)} %get-tuple-element.368) | copy-start | bytes 9437188
  346.7 18.4 %copy-start.80 = (f32[1024]{0:T(1024)}, f32[1024]{0:T(1024)S(1)}, u32[]{:S(2)}) copy-start(f32[1024]{0:T(1024)S(1)} %broadcast_multiply_fusion.4) | copy-start | bytes 12292
  347.3 17.9 copy-start.90
  347.3 17.9 copy-start.92
  349.8 20.0 %copy-start.56 = (bf16[12,6,128,128]{3,1,2,0:T(8,128)(2,1)S(1)}, bf16[12,6,128,128]{3,1,2,0:T(8,128)(2,1)}, u32[]{:S(2)}) copy-start(bf16[12,6,128,128]{3,1,2,0:T(8,128)(2,1)} %copy.271) | copy-start | bytes 7077892
  374.1 149.2 %reduce-scatter.3.cloned.1.call-start = ((), (), s32[]{:S(2)}) async-start(), calls=%async_computation.6 | async-start | bytes 6291456 | tf_op jit(solution)/shard_map/reduce_scatter | solution.py:288
  382.0 78.0 %copy-start.4 = (f32[1024,768]{1,0:T(8,128)S(1)}, f32[1024,768]{1,0:T(8,128)}, u32[]{:S(2)}) copy-start(f32[1024,768]{1,0:T(8,128)} %copy-done.3) | copy-start | bytes 9437188
  468.7 580.5 %all-gather.6.cloned.1.call-start = ((), (), s32[]{:S(2)}) async-start(), calls=%async_computation.7 | async-start | bytes 3145728 | tf_op jit(solution)/shard_map/all_gather | solution.py:338
  594.5 44.2 %copy-start.67 = (bf16[4096,16]{0,1:T(8,128)(2,1)}, bf16[4096,16]{0,1:T(8,128)(2,1)S(1)}, u32[]{:S(2)}) copy-start(bf16[4096,16]{0,1:T(8,128)(2,1)S(1)} %get-tuple-element.363) | copy-start | bytes 393220
  638.8 23.4 %copy-start.76 = (bf16[4096,16]{0,1:T(8,128)(2,1)}, bf16[4096,16]{0,1:T(8,128)(2,1)S(1)}, u32[]{:S(2)}) copy-start(bf16[4096,16]{0,1:T(8,128)(2,1)S(1)} %get-tuple-element.417) | copy-start | bytes 393220
  1013.9 35.3 %copy-start.61 = (bf16[3,128,8,128]{3,2,1,0:T(8,128)(2,1)S(1)}, bf16[3,128,8,128]{3,2,1,0:T(8,128)(2,1)}, u32[]{:S(2)}) copy-start(bf16[3,128,8,128]{3,2,1,0:T(8,128)(2,1)} %copy-done.60) | copy-start | bytes 2359300
  1015.2 104.2 %all-gather.8.cloned.1.call-start = ((), (), s32[]{:S(2)}) async-start(), calls=%async_computation.8 | async-start | bytes 7077888 | tf_op jit(solution)/shard_map/all_gather | solution.py:343
  1056.6 66.0 %copy-start.57 = (bf16[12,6,128,128]{3,1,2,0:T(8,128)(2,1)S(1)}, bf16[12,6,128,128]{3,1,2,0:T(8,128)(2,1)}, u32[]{:S(2)}) copy-start(bf16[12,6,128,128]{3,1,2,0:T(8,128)(2,1)} %copy.271) | copy-start | bytes 7077892
  1056.6 66.0 %copy-start.95 = (f32[1536]{0:T(1024)S(1)}, f32[1536]{0:T(1024)}, u32[]{:S(2)}) copy-start(f32[1536]{0:T(1024)} %copy-done.94) | copy-start | bytes 18436
  1056.6 134.8 %all-reduce.17.cloned.1.call-start = ((), (), s32[]{:S(2)}) async-start(), calls=%async_computation.9 | async-start | bytes 3145728 | tf_op jit(solution)/shard_map/psum | solution.py:354
  1122.5 11.7 copy-start.6
  1122.5 13.4 copy-start.55
  1139.7 160.9 %all-reduce.19.cloned.1.call-start = ((), (), s32[]{:S(2)}) async-start(), calls=%async_computation.10 | async-start | bytes 3145728 | tf_op jit(solution)/shard_map/psum | solution.py:391
  1166.8 24.5 %copy-start.81 = (f32[1024]{0:T(1024)S(1)}, f32[1024]{0:T(1024)}, u32[]{:S(2)}) copy-start(f32[1024]{0:T(1024)} %copy-done.80) | copy-start | bytes 12292
  1166.8 24.5 %copy-start.85 = (f32[768]{0:T(1024)S(1)}, f32[768]{0:T(1024)}, u32[]{:S(2)}) copy-start(f32[768]{0:T(1024)} %copy-done.84) | copy-start | bytes 9220
  1169.8 25.7 %copy-start.91 = (f32[1024]{0:T(1024)S(1)}, f32[1024]{0:T(1024)}, u32[]{:S(2)}) copy-start(f32[1024]{0:T(1024)} %copy-done.90) | copy-start | bytes 12292
  1169.8 25.7 %copy-start.93 = (f32[1024]{0:T(1024)S(1)}, f32[1024]{0:T(1024)}, u32[]{:S(2)}) copy-start(f32[1024]{0:T(1024)} %copy-done.92) | copy-start | bytes 12292
  1203.8 7.6 copy-start.73
  1211.5 8.7 copy-start.16
  1211.5 18.1 slice-start
  1211.5 18.1 slice-start.1
  1220.2 9.4 slice-start.2
  1249.0 352.6 %reduce-scatter.5.cloned.1.call-start = ((), (), s32[]{:S(2)}) async-start(), calls=%async_computation.11 | async-start | bytes 26738688 | tf_op jit(solution)/shard_map/reduce_scatter | solution.py:430
  1276.1 24.6 %copy-start.79 = (f32[1024]{0:T(1024)S(1)}, f32[1024]{0:T(1024)}, u32[]{:S(2)}) copy-start(f32[1024]{0:T(1024)} %copy-done.78) | copy-start | bytes 12292
  1276.1 24.6 %copy-start.83 = (f32[768]{0:T(1024)S(1)}, f32[768]{0:T(1024)}, u32[]{:S(2)}) copy-start(f32[768]{0:T(1024)} %copy-done.82) | copy-start | bytes 9220
  1282.2 21.5 %copy-start.89 = (f32[1024]{0:T(1024)S(1)}, f32[1024]{0:T(1024)}, u32[]{:S(2)}) copy-start(f32[1024]{0:T(1024)} %copy-done.88) | copy-start | bytes 12292
  1282.2 21.5 %copy-start.87 = (f32[1024]{0:T(1024)S(1)}, f32[1024]{0:T(1024)}, u32[]{:S(2)}) copy-start(f32[1024]{0:T(1024)} %copy-done.86) | copy-start | bytes 12292
  1357.5 381.5 %all-reduce.21.cloned.1.call-start = ((), (), s32[]{:S(2)}) async-start(), calls=%async_computation.12 | async-start | bytes 3678208 | tf_op jit(solution)/shard_map/psum | solution.py:429
  1359.3 20.5 %copy-start.103 = (f32[1536]{0:T(1024)S(1)}, f32[1536]{0:T(1024)}, u32[]{:S(2)}) copy-start(f32[1536]{0:T(1024)} %get-tuple-element.437) | copy-start | bytes 18436
  1387.1 17.6 copy-start.110
  1387.1 17.6 copy-start.112
  1601.6 182.0 %copy-start.10 = (f32[1,1,24,128,128]{4,3,2,1,0:T(8,128)S(1)}, f32[1,1,24,128,128]{4,3,2,1,0:T(8,128)}, u32[]{:S(2)}) copy-start(f32[1,1,24,128,128]{4,3,2,1,0:T(8,128)} %reduce-scatter.5.cloned.1.call-done) | copy-start | bytes 4718596
  (92 other events, 291.9 us)
Sparse Core Ops, SparseCore 0:
  10.9 103.4 all-gather.3
  127.7 83.9 all-reduce.10
  258.6 85.7 all-reduce.12
  374.2 85.7 all-reduce.14
  468.9 54.3 reduce-scatter.2
  1015.3 33.8 all-gather.5
  1056.7 62.6 all-gather.7
  1139.8 51.4 all-reduce.16
  1249.1 51.4 all-reduce.18
  1357.6 243.9 reduce-scatter.4
  1607.6 131.3 all-reduce.20
where the time goes:
time: 1830 us; the launch traced here: 1820 us
  waiting for transfers between devices  839 us (46%)
  local copies, waits for them, and re-layouts  454 us (25%)
  other arithmetic  215 us (12%)
  matrix products  205 us (11%)
  blocking collectives  80.1 us (4%)
  between operations  22 us (1%)
    scatter-add x19, local copies, waits for them, and re-layouts, col2im(): padded = padded.at[:, depth_at:depth_at + extent, row_at:row_at + extent,...  237 us
    reduce_scatter x1, waiting for transfers between devices, local(): lax.psum_scatter(grad_local.reshape(lax.axis_size('dp'), 1, -1, BS, BS),...  196 us
    psum x1, waiting for transfers between devices, local(): aux_total = lax.psum(grad_aux, ('dp', 'mp'))  135 us
    all_gather x1, waiting for transfers between devices, fetch_weights(): lax.all_gather(blocks.astype(jnp.bfloat16), 'dp', axis=0, tiled=True)  105 us
    psum x2, blocking collectives, local(): lax.psum((local_terms[0], local_terms[1], local_terms[2], truth_local), (...  80.1 us
    add x18, other arithmetic, col2im(): padded = padded.at[:, depth_at:depth_at + extent, row_at:row_at + extent,...  76.8 us
    unnamed x290, local copies, waits for them, and re-layouts  75 us
    psum x1, waiting for transfers between devices, local(): embedded = lax.psum(product(patches, w_embed), 'mp')  74 us
  transfers between devices with their start and end apart: 11, of which 11 were waited for; matrix products, arithmetic and copies ran while one was open for 8% of the time, Pallas kernels for 0%

commit v1 on v0

v1 whole, which is shorter than its diff:
```python
import functools
import math

import jax
import jax.numpy as jnp
from jax import lax
from jax.experimental import pallas as pl
from jax.experimental.pallas import tpu as pltpu
from jax.sharding import PartitionSpec as P

D = 768
HDIM = 64
FF = 3072
PV = 4096
DEC = 128
CF = 16
NCLS = 14
GS = 8
MB = 4
STEP = 10
BS = 128
NTOK = 512
CELLS = 4096
MP = 2
HALF = D // MP
E_BLOCKS = PV // MP * D // (BS * BS)

HIGHEST = lax.Precision.HIGHEST
MESH = pl.DeviceIdType.MESH
beta_one = 0.9
beta_two = 0.999
beta_stat = 0.95
learn_rate = 0.02
decay_rate = 0.01
clip_value = 0.005
MIB = 1024 * 1024

OFFSETS = [(a, b, c) for a in range(3) for b in range(3) for c in range(3)]
PARITIES = [(i, j, k) for i in range(2) for j in range(2) for k in range(2)]


def dot(a, b, dims):
    return lax.dot_general(a, b, (dims, ((), ())), preferred_element_type=jnp.float32)


def dot_nn(a, b):
    return dot(a, b, ((1,), (0,)))


def dot_nt(a, b):
    return dot(a, b, ((1,), (1,)))


def dot_tn(a, b):
    return dot(a, b, ((0,), (0,)))


def gelu_cdf(v):
    return 0.5 * (1.0 + lax.erf(v * (0.5**0.5)))


def gelu_and_slope(v):
    cdf = gelu_cdf(v)
    density = jnp.exp(-0.5 * v * v) * (1.0 / math.sqrt(2.0 * math.pi))
    return v * cdf, cdf + v * density


def aux_layout():
    return [
        ("positions", (NTOK, D)),
        ("embed_bias", (D,)),
        ("norm_gain", (2, D)),
        ("norm_bias", (2, D)),
        ("qv_bias", (2, D)),
        ("proj_bias", (D,)),
        ("up_bias", (FF,)),
        ("down_bias", (D,)),
        ("deconv_bias", (DEC,)),
        ("conv_weight", (27 * DEC, CF)),
        ("conv_bias", (CF,)),
        ("head_weight", (CF, NCLS)),
        ("head_bias", (NCLS,)),
    ]


NAUX = sum(math.prod(shape) for _, shape in aux_layout())


def split_aux(vector):
    pieces = {}
    offset = 0
    for section_name, section_shape in aux_layout():
        length = math.prod(section_shape)
        pieces[section_name] = vector[offset : offset + length].reshape(section_shape)
        offset += length
    return pieces


LOCAL_SHAPES = [
    (PV // MP, D),
    (D, 3 * HALF),
    (HALF, D),
    (D, FF // MP),
    (FF // MP, D),
    (3 * HALF, 8 * DEC),
]


def from_blocks(piece, height, breadth):
    return (
        piece.reshape(height // BS, breadth // BS, BS, BS)
        .transpose(0, 2, 1, 3)
        .reshape(height, breadth)
    )


def to_blocks(matrix):
    return (
        matrix.reshape(matrix.shape[0] // BS, BS, matrix.shape[1] // BS, BS)
        .transpose(0, 2, 1, 3)
        .reshape(-1, BS, BS)
    )


def attention_forward_kernel(qkv_q, qkv_k, qkv_v, mixed_ref, lse_ref):
    q, k, v = qkv_q[...], qkv_k[...], qkv_v[...]
    v_t = v.astype(jnp.float32).T.astype(jnp.bfloat16)
    outs = []
    for h in range(2):
        cols = slice(h * HDIM, (h + 1) * HDIM)
        scores = dot_nt(k[:, cols], q[:, cols]) * 0.125
        top = jnp.max(scores, 0, keepdims=True)
        weights = jnp.exp(scores - top)
        total = jnp.sum(weights, 0, keepdims=True)
        attention = (weights * (1.0 / total)).astype(jnp.bfloat16)
        outs.append(dot_nn(v_t[cols], attention))
        lse_ref[0, h : h + 1, :] = top + jnp.log(total)
    mixed_ref[...] = jnp.concatenate(outs, 0).T.astype(jnp.bfloat16)


def attention_backward_kernel(qkv_q, qkv_k, qkv_v, gm_ref, lse_ref, gq_ref, gk_ref, gv_ref):
    q, k, v, gm = qkv_q[...], qkv_k[...], qkv_v[...], gm_ref[...]
    k_t = k.astype(jnp.float32).T.astype(jnp.bfloat16)
    gq_t = []
    for h in range(2):
        cols = slice(h * HDIM, (h + 1) * HDIM)
        scores = dot_nt(k[:, cols], q[:, cols]) * 0.125
        attention = jnp.exp(scores - lse_ref[0, h : h + 1, :])
        back = dot_nt(v[:, cols], gm[:, cols])
        gv_ref[:, cols] = dot_nn(attention.astype(jnp.bfloat16), gm[:, cols]).astype(jnp.bfloat16)
        mean = jnp.sum(back * attention, 0, keepdims=True)
        gs = (attention * (back - mean)).astype(jnp.bfloat16)
        gk_ref[:, cols] = (dot_nn(gs, q[:, cols]) * 0.125).astype(jnp.bfloat16)
        gq_t.append(dot_nn(k_t[cols], gs) * 0.125)
    gq_ref[...] = jnp.concatenate(gq_t, 0).T.astype(jnp.bfloat16)


def qkv_spec(part):
    return pl.BlockSpec((NTOK, BS), lambda i, part=part: (0, (i // 3) * 9 + part * 3 + i % 3))


def attention_forward(qkv):
    return pl.pallas_call(
        attention_forward_kernel,
        grid=(6,),
        out_shape=(
            jax.ShapeDtypeStruct((NTOK, D), jnp.bfloat16),
            jax.ShapeDtypeStruct((6, 2, NTOK), jnp.float32),
        ),
        in_specs=[qkv_spec(0), qkv_spec(1), qkv_spec(2)],
        out_specs=(
            pl.BlockSpec((NTOK, BS), lambda i: (0, i)),
            pl.BlockSpec((1, 2, NTOK), lambda i: (i, 0, 0)),
        ),
        compiler_params=pltpu.CompilerParams(vmem_limit_bytes=32 * MIB),
        cost_estimate=pl.CostEstimate(
            flops=12 * 4 * NTOK * NTOK * HDIM,
            bytes_accessed=NTOK * D * 8,
            transcendentals=12 * NTOK * NTOK,
        ),
        name="attention_forward",
    )(qkv, qkv, qkv)


def attention_backward(qkv, gm, lse):
    pair = pl.BlockSpec((NTOK, BS), lambda i: (0, i))
    return pl.pallas_call(
        attention_backward_kernel,
        grid=(6,),
        out_shape=(jax.ShapeDtypeStruct((NTOK, D), jnp.bfloat16),) * 3,
        in_specs=[
            qkv_spec(0),
            qkv_spec(1),
            qkv_spec(2),
            pair,
            pl.BlockSpec((1, 2, NTOK), lambda i: (i, 0, 0)),
        ],
        out_specs=(pair,) * 3,
        compiler_params=pltpu.CompilerParams(vmem_limit_bytes=32 * MIB),
        cost_estimate=pl.CostEstimate(
            flops=12 * 10 * NTOK * NTOK * HDIM,
            bytes_accessed=NTOK * D * 14,
            transcendentals=12 * NTOK * NTOK,
        ),
        name="attention_backward",
    )(qkv, qkv, qkv, gm, lse)


def source_of(parity, step):
    at = parity + step
    if at < 0:
        return 1, -1
    if at > 1:
        return 0, 1
    return at, 0


def shift_plan(offset, parity, sign):
    found = [source_of(par, sign * (off - 1)) for off, par in zip(offset, parity)]
    bits = [f[0] for f in found]
    steps = [f[1] for f in found]
    return bits[0] * 4 + bits[1] * 2 + bits[2], steps


def token_masks(tokens):
    at = (tokens // (GS * GS), (tokens // GS) % GS, tokens % GS)
    masks = {}
    for axis in range(3):
        masks[axis, 1] = at[axis] < GS - 1
        masks[axis, -1] = at[axis] > 0
    return masks


def shifted(values, steps, masks):
    delta = steps[0] * GS * GS + steps[1] * GS + steps[2]
    if delta == 0 and not any(steps):
        return values
    moved = pltpu.roll(values, (-delta) % NTOK, 1)
    keep = None
    for axis in range(3):
        if steps[axis]:
            mask = masks[axis, steps[axis]]
            keep = mask if keep is None else keep & mask
    return jnp.where(keep, moved, 0.0)


def lanes(parity):
    return slice(parity * NTOK, (parity + 1) * NTOK)


def decoder_forward_kernel(
    up_ref,
    deconv_bias_ref,
    conv_ref,
    conv_bias_ref,
    head_ref,
    head_bias_ref,
    labels_ref,
    batch_ref,
    conv_in_ref,
    grid_slope_ref,
    conv_slope_ref,
    features_ref,
    chance_ref,
    sums_ref,
    conved_ref,
):
    tokens = lax.broadcasted_iota(jnp.int32, (CF, NTOK), 1)
    masks = token_masks(tokens)
    for parity in range(8):
        conved_ref[:, lanes(parity)] = jnp.broadcast_to(conv_bias_ref[...], (CF, NTOK))
    for parity in range(8):
        cell = up_ref[parity * DEC : (parity + 1) * DEC, :] + deconv_bias_ref[...]
        value, slope = gelu_and_slope(cell)
        low = value.astype(jnp.bfloat16)
        conv_in_ref[:, lanes(parity)] = low
        grid_slope_ref[:, lanes(parity)] = slope
        products = dot_nn(conv_ref[...], low)
        for at, offset in enumerate(OFFSETS):
            target, back_steps = shift_plan(offset, PARITIES[parity], -1)
            forward = [-s for s in back_steps]
            piece = shifted(products[at * CF : (at + 1) * CF, :], forward, masks)
            conved_ref[:, lanes(target)] += piece
    rows = lax.broadcasted_iota(jnp.int32, (CF, NTOK), 0)
    hit = jnp.zeros((CF, 1), jnp.float32)
    predicted = jnp.zeros((CF, 1), jnp.float32)
    truth = jnp.zeros((CF, 1), jnp.float32)
    entropy = jnp.zeros((CF, 1), jnp.float32)
    for parity in range(8):
        value, slope = gelu_and_slope(conved_ref[:, lanes(parity)])
        conv_slope_ref[:, lanes(parity)] = slope
        features = value.astype(jnp.bfloat16)
        features_ref[:, lanes(parity)] = features
        logits = dot_nn(head_ref[...], features) + head_bias_ref[...]
        logits = jnp.where(rows < NCLS, logits, -1e30)
        center = logits - jnp.max(logits, 0, keepdims=True)
        log_prob = center - jnp.log(jnp.sum(jnp.exp(center), 0, keepdims=True))
        chance = jnp.exp(log_prob)
        target = (rows == labels_ref[parity : parity + 1, :]).astype(jnp.float32)
        chance_ref[:, lanes(parity)] = chance
        hit += jnp.sum(chance * target, 1, keepdims=True)
        predicted += jnp.sum(chance, 1, keepdims=True)
        truth += jnp.sum(target, 1, keepdims=True)
        entropy -= jnp.sum(jnp.where(target > 0, log_prob, 0.0), 1, keepdims=True)
    lane = lax.broadcasted_iota(jnp.int32, (CF, BS), 1)
    base = batch_ref[...] * 3
    sums_ref[...] = (
        jnp.where(lane == base, hit, 0.0)
        + jnp.where(lane == base + 1, predicted, 0.0)
        + jnp.where(lane == base + 2, truth, 0.0)
        + jnp.where(lane == 3 * MB, entropy, 0.0)
    )


def decoder_backward_kernel(
    all_crops,
    sums_ref,
    batch_ref,
    labels_ref,
    chance_ref,
    features_ref,
    conv_slope_ref,
    grid_slope_ref,
    conv_in_ref,
    conv_t_ref,
    head_t_ref,
    gu_ref,
    conv_grad_ref,
    head_grad_ref,
    small_ref,
    deconv_grad_ref,
    spread_ref,
):
    sums = sums_ref[...]
    lane = lax.broadcasted_iota(jnp.int32, (CF, BS), 1)
    row = lax.broadcasted_iota(jnp.int32, (CF, BS), 0)
    live = (lane < 3 * MB) & (lane % 3 == 0) & (row < NCLS)
    under = pltpu.roll(sums, BS - 1, 1) + pltpu.roll(sums, BS - 2, 1) + 1.0
    under = jnp.where(live, under, 1.0)
    over = 2.0 * sums + 1.0
    dice = jnp.where(live, over / under, 0.0)
    mean_dice = jnp.sum(jnp.sum(dice, 1, keepdims=True), 0, keepdims=True) / (NCLS * MB)
    entropy_lane = jnp.where(lane == 3 * MB, sums, 0.0)
    entropy = jnp.sum(jnp.sum(entropy_lane, 1, keepdims=True), 0, keepdims=True)
    loss = entropy / (all_crops * CELLS) + (1.0 - mean_dice)
    own = live & (lane == batch_ref[...] * 3)
    d_hit = jnp.sum(jnp.where(own, -2.0 / (MB * NCLS) / under, 0.0), 1, keepdims=True)
    d_predicted = jnp.sum(
        jnp.where(own, (1.0 / (MB * NCLS)) * over / (under * under), 0.0), 1, keepdims=True
    )
    tokens = lax.broadcasted_iota(jnp.int32, (CF, NTOK), 1)
    masks = token_masks(tokens)
    rows = lax.broadcasted_iota(jnp.int32, (CF, NTOK), 0)
    head_bias = jnp.zeros((CF, 1), jnp.float32)
    conv_bias = jnp.zeros((CF, 1), jnp.float32)
    head_grad = jnp.zeros((CF, CF), jnp.float32)
    for parity in range(8):
        chance = chance_ref[:, lanes(parity)]
        target = (rows == labels_ref[parity : parity + 1, :]).astype(jnp.float32)
        back = (d_hit * target + d_predicted) * chance - target * (1.0 / (all_crops * CELLS))
        logits = back - chance * jnp.sum(back, 0, keepdims=True)
        head_bias += jnp.sum(logits, 1, keepdims=True)
        low = logits.astype(jnp.bfloat16)
        head_grad += dot_nt(features_ref[:, lanes(parity)], low)
        conved = conv_slope_ref[:, lanes(parity)] * dot_nn(head_t_ref[...], low)
        conv_bias += jnp.sum(conved, 1, keepdims=True)
        rounded = conved.astype(jnp.bfloat16).astype(jnp.float32)
        for at, offset in enumerate(OFFSETS):
            target_cell, steps = shift_plan(offset, PARITIES[parity], 1)
            piece = shifted(rounded, [-s for s in steps], masks)
            spread_ref[at * CF : (at + 1) * CF, lanes(target_cell)] = piece.astype(jnp.bfloat16)
    head_grad_ref[...] = head_grad
    small_ref[...] = (
        jnp.where(lane == 0, head_bias, 0.0)
        + jnp.where(lane == 1, conv_bias, 0.0)
        + jnp.where(lane == 2, loss, 0.0)
    )
    conv_grad = jnp.zeros((27 * CF, DEC), jnp.float32)
    deconv_grad = jnp.zeros((DEC, 1), jnp.float32)
    for parity in range(8):
        spread = spread_ref[:, lanes(parity)]
        conv_grad += dot_nt(spread, conv_in_ref[:, lanes(parity)])
        back = grid_slope_ref[:, lanes(parity)] * dot_nn(conv_t_ref[...], spread)
        deconv_grad += jnp.sum(back, 1, keepdims=True)
        gu_ref[parity * DEC : (parity + 1) * DEC, :] = back.astype(jnp.bfloat16)
    conv_grad_ref[...] = conv_grad
    deconv_grad_ref[...] = jnp.broadcast_to(deconv_grad, (DEC, BS))


def whole_specs(number):
    return [pl.BlockSpec(memory_space=pltpu.VMEM)] * number


def decoder_forward(up_t, deconv_bias, conv_low, conv_bias, head_low, head_bias, labels, batch):
    shapes = (
        jax.ShapeDtypeStruct((DEC, CELLS), jnp.bfloat16),
        jax.ShapeDtypeStruct((DEC, CELLS), jnp.float32),
        jax.ShapeDtypeStruct((CF, CELLS), jnp.float32),
        jax.ShapeDtypeStruct((CF, CELLS), jnp.bfloat16),
        jax.ShapeDtypeStruct((CF, CELLS), jnp.float32),
        jax.ShapeDtypeStruct((CF, BS), jnp.float32),
    )
    return pl.pallas_call(
        decoder_forward_kernel,
        out_shape=shapes,
        in_specs=whole_specs(8),
        out_specs=tuple(whole_specs(6)),
        scratch_shapes=[pltpu.VMEM((CF, CELLS), jnp.float32)],
        compiler_params=pltpu.CompilerParams(vmem_limit_bytes=40 * MIB),
        cost_estimate=pl.CostEstimate(
            flops=2 * 27 * CF * DEC * CELLS, bytes_accessed=6 * MIB, transcendentals=DEC * CELLS
        ),
        name="decoder_forward",
    )(up_t, deconv_bias, conv_low, conv_bias, head_low, head_bias, labels, batch)


def decoder_backward(
    all_crops, sums, batch, labels, chance, features, conv_slope, grid_slope, conv_in, conv_t, head_t
):
    shapes = (
        jax.ShapeDtypeStruct((8 * DEC, NTOK), jnp.bfloat16),
        jax.ShapeDtypeStruct((27 * CF, DEC), jnp.float32),
        jax.ShapeDtypeStruct((CF, CF), jnp.float32),
        jax.ShapeDtypeStruct((CF, BS), jnp.float32),
        jax.ShapeDtypeStruct((DEC, BS), jnp.float32),
    )
    return pl.pallas_call(
        functools.partial(decoder_backward_kernel, all_crops),
        out_shape=shapes,
        in_specs=whole_specs(10),
        out_specs=tuple(whole_specs(5)),
        scratch_shapes=[pltpu.VMEM((27 * CF, CELLS), jnp.bfloat16)],
        compiler_params=pltpu.CompilerParams(vmem_limit_bytes=40 * MIB),
        cost_estimate=pl.CostEstimate(
            flops=4 * 27 * CF * DEC * CELLS, bytes_accessed=6 * MIB, transcendentals=0
        ),
        name="decoder_backward",
    )(sums, batch, labels, chance, features, conv_slope, grid_slope, conv_in, conv_t, head_t)


def gather_weights(blocks):
    low = blocks.astype(jnp.bfloat16)[0]
    gathered = lax.all_gather(low, ("dp", "mp"), axis=0, tiled=True)
    return gathered.reshape(lax.axis_size("dp"), MP, -1, BS, BS)


def sum_small(values):
    return lax.psum(values, ("dp", "mp"))


def swap_mp(values):
    return lax.ppermute(values, "mp", [(0, 1), (1, 0)])


def reduce_blocks(embed_grad, block_grads):
    part = lax.axis_index("mp")
    own = (jnp.arange(MP) == part).astype(jnp.float32)
    first = embed_grad[None] * own[:, None, None, None]
    every = jnp.concatenate([first, block_grads], 1)
    dp = lax.axis_size("dp")
    every = every.reshape(MP, dp, -1, BS, BS).transpose(1, 0, 2, 3, 4)
    return lax.psum_scatter(
        every.reshape(dp * MP, -1, BS, BS), ("dp", "mp"), scatter_dimension=0, tiled=True
    )[0]


def layer_norm(values):
    center = values - jnp.mean(values, -1, keepdims=True)
    spread = jnp.mean(center * center, -1, keepdims=True)
    inverse = lax.rsqrt(spread + 1e-06)
    return center * inverse, inverse


def layer_norm_back(back, normal, inverse, gain):
    scaled = back * gain
    mean = jnp.mean(scaled, -1, keepdims=True)
    along = jnp.mean(scaled * normal, -1, keepdims=True)
    return inverse * (scaled - mean - normal * along)


def shampoo_step(blocks, grads, stat_pair, root_pair, moment, veloc):
    stat_left = beta_stat * stat_pair[0] + (1 - beta_stat) * jnp.einsum(
        "cij,ckj->cik", grads, grads, precision=HIGHEST
    )
    stat_right = beta_stat * stat_pair[1] + (1 - beta_stat) * jnp.einsum(
        "cji,cjk->cik", grads, grads, precision=HIGHEST
    )
    moment_new = beta_one * moment + (1 - beta_one) * grads
    veloc_new = beta_two * veloc + (1 - beta_two) * grads * grads
    moment_hat = moment_new / (1 - beta_one**STEP)
    adam_dir = moment_hat / (jnp.sqrt(veloc_new / (1 - beta_two**STEP)) + 1e-08)
    left_side = jnp.einsum("cij,cjk->cik", root_pair[0], moment_hat, precision=HIGHEST)
    precond = jnp.einsum("cij,cjk->cik", left_side, root_pair[1], precision=HIGHEST)
    ratio = jnp.sqrt(
        (jnp.mean(adam_dir * adam_dir, (-2, -1), keepdims=True) + 1e-06)
        / (jnp.mean(precond * precond, (-2, -1), keepdims=True) + 1e-06)
    )
    block_new = blocks - learn_rate * (precond * ratio + decay_rate * blocks)
    return (block_new, jnp.stack([stat_left, stat_right]), moment_new, veloc_new)


def adam_step(param, grads, moment, veloc):
    moment_new = beta_one * moment + (1 - beta_one) * grads
    veloc_new = beta_two * veloc + (1 - beta_two) * grads * grads
    direction = (
        moment_new / (1 - beta_one**STEP) / (jnp.sqrt(veloc_new / (1 - beta_two**STEP)) + 1e-08)
    )
    return (param - learn_rate * direction, moment_new, veloc_new)


def halves(matrix):
    return matrix[:, :HALF], matrix[:, HALF:]


def local(
    patches,
    labels,
    batch_ids,
    blocks,
    statistics,
    roots,
    moments,
    velocity,
    aux,
    aux_moment,
    aux_velocity,
):
    part = lax.axis_index("mp")
    all_crops = lax.axis_size("dp") * MP
    pieces = split_aux(aux)
    gain, shift = pieces["norm_gain"], pieces["norm_bias"]

    gathered = gather_weights(blocks)
    per_part = [gathered[:, m].reshape(-1, BS, BS) for m in range(MP)]
    starts = [0]
    for height, breadth in LOCAL_SHAPES:
        starts.append(starts[-1] + height * breadth // (BS * BS))

    def matrix_of(which, m):
        piece = per_part[m][starts[which] : starts[which + 1]]
        return from_blocks(piece, *LOCAL_SHAPES[which])

    own_embed = lax.dynamic_index_in_dim(gathered, part, 1, False).reshape(-1, BS, BS)
    w_embed = from_blocks(own_embed[:E_BLOCKS], *LOCAL_SHAPES[0])
    w_qkv = jnp.concatenate([matrix_of(1, m) for m in range(MP)], 1)
    w_proj = jnp.concatenate([matrix_of(2, m) for m in range(MP)], 0)
    w_up = jnp.concatenate([matrix_of(3, m) for m in range(MP)], 1)
    w_down = jnp.concatenate([matrix_of(4, m) for m in range(MP)], 0)
    w_deconv = jnp.concatenate([matrix_of(5, m) for m in range(MP)], 0)

    other_rows = lax.dynamic_slice_in_dim(patches, (1 - part) * NTOK, NTOK, 0)
    own_rows = lax.dynamic_slice_in_dim(patches, part * NTOK, NTOK, 0)
    received = swap_mp(dot_nn(other_rows, w_embed))
    stream_zero = (
        dot_nn(own_rows, w_embed) + received + pieces["positions"] + pieces["embed_bias"]
    )
    normal_one, inverse_one = layer_norm(stream_zero)
    normed_one = (normal_one * gain[0] + shift[0]).astype(jnp.bfloat16)
    q_bias, v_bias = pieces["qv_bias"][0], pieces["qv_bias"][1]
    nothing = jnp.zeros((HALF,), jnp.float32)
    qkv_bias = jnp.concatenate(
        [q_bias[:HALF], nothing, v_bias[:HALF], q_bias[HALF:], nothing, v_bias[HALF:]]
    )
    qkv = (dot_nn(normed_one, w_qkv) + qkv_bias).astype(jnp.bfloat16)
    mixed, lse = attention_forward(qkv)
    stream_one = stream_zero + dot_nn(mixed, w_proj) + pieces["proj_bias"]
    normal_two, inverse_two = layer_norm(stream_one)
    normed_two = (normal_two * gain[1] + shift[1]).astype(jnp.bfloat16)
    hidden = dot_nn(normed_two, w_up) + pieces["up_bias"]
    active_value, hidden_slope = gelu_and_slope(hidden)
    active = active_value.astype(jnp.bfloat16)
    stream_two = stream_one + dot_nn(active, w_down) + pieces["down_bias"]
    streams = [s.astype(jnp.bfloat16) for s in (stream_zero, stream_one, stream_two)]
    stacked = jnp.concatenate([halves(s)[m] for m in range(MP) for s in streams], 1)
    up_t = dot(w_deconv, stacked, ((0,), (1,)))

    conv_weight = pieces["conv_weight"].astype(jnp.bfloat16).reshape(27, DEC, CF)
    conv_low = conv_weight.transpose(0, 2, 1).reshape(27 * CF, DEC)
    conv_t = conv_weight.transpose(1, 0, 2).reshape(DEC, 27 * CF)
    head_weight = jnp.pad(pieces["head_weight"], ((0, 0), (0, CF - NCLS))).astype(jnp.bfloat16)
    head_bias = jnp.pad(pieces["head_bias"], (0, CF - NCLS)).reshape(CF, 1)
    grid_labels = (
        labels.reshape(GS, 2, GS, 2, GS, 2).transpose(1, 3, 5, 0, 2, 4).reshape(8, NTOK)
    )
    batch = jnp.broadcast_to(batch_ids.reshape(1, 1), (1, BS))
    conv_in, grid_slope, conv_slope, features, chance, sums = decoder_forward(
        up_t,
        pieces["deconv_bias"].reshape(DEC, 1),
        conv_low,
        pieces["conv_bias"].reshape(CF, 1),
        head_weight.T,
        head_bias,
        grid_labels,
        batch,
    )
    sums = sum_small(sums)
    gu_t, conv_grad, head_grad, small, deconv_bias_grad = decoder_backward(
        all_crops,
        sums,
        batch,
        grid_labels,
        chance,
        features,
        conv_slope,
        grid_slope,
        conv_in,
        conv_t,
        head_weight,
    )
    loss_value = small[0, 2]
    grad_head_bias = small[:NCLS, 0]
    grad_conv_bias = small[:, 1]
    grad_deconv_bias = deconv_bias_grad[:, 0]
    grad_conv_weight = conv_grad.reshape(27, CF, DEC).transpose(0, 2, 1)
    grad_head_weight = head_grad[:, :NCLS]

    grad_deconv = dot_tn(stacked, gu_t.T)
    stacked_back = dot(gu_t, w_deconv, ((0,), (1,)))
    back_zero_s, back_one_s, back_two = [
        jnp.concatenate([stacked_back[:, (3 * m + s) * HALF : (3 * m + s + 1) * HALF] for m in range(MP)], 1)
        for s in range(3)
    ]
    grad_down_bias = jnp.sum(back_two, 0)
    two_low = back_two.astype(jnp.bfloat16)
    back_hidden = (hidden_slope * dot_nt(two_low, w_down)).astype(jnp.bfloat16)
    grad_down = dot_tn(active, two_low)
    grad_up_bias = jnp.sum(back_hidden.astype(jnp.float32), 0)
    grad_up = dot_tn(normed_two, back_hidden)
    back_normed_two = dot_nt(back_hidden, w_up)
    grad_gain_two = jnp.sum(back_normed_two * normal_two, 0)
    grad_shift_two = jnp.sum(back_normed_two, 0)
    back_one = (
        back_two + back_one_s + layer_norm_back(back_normed_two, normal_two, inverse_two, gain[1])
    )
    grad_proj_bias = jnp.sum(back_one, 0)
    one_low = back_one.astype(jnp.bfloat16)
    grad_proj = dot_tn(mixed, one_low)
    back_mixed = dot_nt(one_low, w_proj).astype(jnp.bfloat16)
    back_q, back_k, back_v = attention_backward(qkv, back_mixed, lse)
    back_qkv = jnp.concatenate(
        [halves(piece)[m] for m in range(MP) for piece in (back_q, back_k, back_v)], 1
    )
    grad_qkv = dot_tn(normed_one, back_qkv)
    grad_query_bias = jnp.sum(back_q.astype(jnp.float32), 0)
    grad_value_bias = jnp.sum(back_v.astype(jnp.float32), 0)
    back_normed_one = dot_nt(back_qkv, w_qkv)
    grad_gain_one = jnp.sum(back_normed_one * normal_one, 0)
    grad_shift_one = jnp.sum(back_normed_one, 0)
    back_zero = (
        back_one + back_zero_s + layer_norm_back(back_normed_one, normal_one, inverse_one, gain[0])
    )
    zero_low = back_zero.astype(jnp.bfloat16)
    other_low = swap_mp(zero_low)
    grad_embed = dot_tn(own_rows, zero_low) + dot_tn(other_rows, other_low)

    block_grads = jnp.stack(
        [
            jnp.concatenate(
                [
                    to_blocks(grad_qkv[:, m * 3 * HALF : (m + 1) * 3 * HALF]),
                    to_blocks(grad_proj[m * HALF : (m + 1) * HALF]),
                    to_blocks(grad_up[:, m * FF // MP : (m + 1) * FF // MP]),
                    to_blocks(grad_down[m * FF // MP : (m + 1) * FF // MP]),
                    to_blocks(grad_deconv[m * 3 * HALF : (m + 1) * 3 * HALF]),
                ]
            )
            for m in range(MP)
        ]
    )
    owned = reduce_blocks(to_blocks(grad_embed), block_grads)
    late = jnp.stack(
        [
            grad_gain_one,
            grad_gain_two,
            grad_shift_one,
            grad_shift_two,
            grad_query_bias,
            grad_value_bias,
            grad_proj_bias,
        ]
    )
    rest = jnp.concatenate(
        [
            late.reshape(-1),
            grad_up_bias,
            grad_down_bias,
            grad_deconv_bias,
            grad_conv_weight.reshape(-1),
            grad_conv_bias,
            grad_head_weight.reshape(-1),
            grad_head_bias,
        ]
    )
    aux_sum = sum_small(jnp.concatenate([back_zero.reshape(-1), rest]))
    positions_sum = aux_sum[: NTOK * D]
    embed_bias_sum = jnp.sum(positions_sum.reshape(NTOK, D), 0)
    aux_total = jnp.concatenate([positions_sum, embed_bias_sum, aux_sum[NTOK * D :]])
    block_square = sum_small(jnp.sum(owned * owned))
    grad_norm = jnp.sqrt(block_square + jnp.sum(aux_total * aux_total))
    clip_scale = clip_value / jnp.maximum(grad_norm, clip_value)
    block_new, stat_new, moment_new, veloc_new = shampoo_step(
        blocks[0, 0],
        owned * clip_scale,
        statistics[:, 0, 0],
        roots[:, 0, 0],
        moments[0, 0],
        velocity[0, 0],
    )
    aux_new, aux_moment_new, aux_veloc_new = adam_step(
        aux, aux_total * clip_scale, aux_moment, aux_velocity
    )
    return (
        loss_value,
        grad_norm,
        block_new[None, None],
        stat_new[:, None, None],
        moment_new[None, None],
        veloc_new[None, None],
        aux_new,
        aux_moment_new,
        aux_veloc_new,
    )


def solution(mesh):
    block_spec = P("dp", "mp", None, None, None)
    pair_spec = P(None, "dp", "mp", None, None, None)
    placed = (
        P("dp", "mp"),
        P(("dp", "mp"), None),
        P(("dp", "mp")),
        block_spec,
        pair_spec,
        pair_spec,
        block_spec,
        block_spec,
        P(),
        P(),
        P(),
    )
    return jax.shard_map(
        local,
        mesh=mesh,
        in_specs=placed,
        out_specs=(P(), P(), block_spec, pair_spec, block_spec, block_spec, P(), P(), P()),
        check_vma=False,
    )
```

time: 1830 us -> 1190 us (0.65)
  waiting for transfers between devices: 839 us -> 576 us
  other arithmetic: 215 us -> 66.6 us
  local copies, waits for them, and re-layouts: 454 us -> 322 us
  matrix products: 205 us -> 87.1 us
  Pallas kernels: 0 us -> 28.4 us
    psum x6 -> x1, waiting for transfers between devices: 394 us -> 0.01 us  [sum_small(): return lax.psum(values, ('dp', 'mp'))]
    scatter-add x19 -> x0, local copies, waits for them, and re-layouts: 237 us -> none  [col2im(): padded = padded.at[:, depth_at:depth_at + extent, row_at:row_at + extent,...]
    reduce_scatter x2 -> x1, waiting for transfers between devices: 244 us -> 427 us  [reduce_blocks(): lax.psum_scatter(every.reshape(dp * MP, -1, BS, BS), ('dp', 'mp'), scatte...]
    dot_general x41 -> x23, matrix products: 205 us -> 87.1 us  [the longest x19 75.1 us: dot(): lax.dot_general(a, b, (dims, ((), ())), preferred_element_type=jnp.float32)]
    transpose x3 -> x25, local copies, waits for them, and re-layouts: 10.3 us -> 104 us  [the longest x9 44.5 us: to_blocks(): return matrix.reshape(matrix.shape[0] // BS, BS, matrix.shape[1] // BS, B...]
    add x19 -> x1, other arithmetic: 76.8 us -> 2.22 us  [shampoo_step(): veloc_new = beta_two * veloc + (1 - beta_two) * grads * grads]
    all_gather x3 -> x1, waiting for transfers between devices: 201 us -> 143 us  [gather_weights(): gathered = lax.all_gather(low, ('dp', 'mp'), axis=0, tiled=True)]
    slice x10 -> x20, local copies, waits for them, and re-layouts: 26.6 us -> 65.9 us  [the longest x5 16.6 us: matrix_of(): piece = per_part[m][starts[which]:starts[which + 1]]]
  transfers between devices with their start and end apart: 11 -> 5, of which waited for: 11 -> 3; matrix products, arithmetic and copies ran while one was open for 8% -> 24% of each run, Pallas kernels for 0% -> 0%
where the time goes in v1:
time: 1190 us; the launch traced here: 1180 us
  waiting for transfers between devices  576 us (48%)
  local copies, waits for them, and re-layouts  322 us (27%)
  matrix products  87.1 us (7%)
  blocking collectives  78.2 us (7%)
  other arithmetic  66.6 us (6%)
  Pallas kernels  28.4 us (2%)
  between operations  18.7 us (2%)
    reduce_scatter x1, waiting for transfers between devices, reduce_blocks(): lax.psum_scatter(every.reshape(dp * MP, -1, BS, BS), ('dp', 'mp'), scatte...  427 us
    all_gather x1, waiting for transfers between devices, gather_weights(): gathered = lax.all_gather(low, ('dp', 'mp'), axis=0, tiled=True)  143 us
    psum x2, blocking collectives, sum_small(): return lax.psum(values, ('dp', 'mp'))  78.2 us
    dot_general x19, matrix products, dot(): lax.dot_general(a, b, (dims, ((), ())), preferred_element_type=jnp.float32)  75.1 us
    unnamed x249, local copies, waits for them, and re-layouts  68.9 us
    reshape x10, local copies, waits for them, and re-layouts, to_blocks(): matrix.reshape(matrix.shape[0] // BS, BS, matrix.shape[1] // BS, BS)  45.8 us
    transpose x9, local copies, waits for them, and re-layouts, to_blocks(): return matrix.reshape(matrix.shape[0] // BS, BS, matrix.shape[1] // BS, B...  44.5 us
    transpose x1, local copies, waits for them, and re-layouts, reduce_blocks(): every = every.reshape(MP, dp, -1, BS, BS).transpose(1, 0, 2, 3, 4)  34.5 us
  transfers between devices with their start and end apart: 5, of which 3 were waited for; matrix products, arithmetic and copies ran while one was open for 24% of the time, Pallas kernels for 0%

profile of v1, /device:TPU:0, one launch (start us, length us, event | category | flops | bytes accessed | tf_op | source)
XLA Modules:
  0.0 1181.7 jit_solution(5284257703533614504)
XLA Ops:
  26.0 142.9 %all-gather.3.cloned.1.call-done = bf16[32,1,24,128,128]{4,3,2,1,0:T(8,128)(2,1)} async-done(((bf16[1,1,24,128,128]{4,3,2,1,0:T(8,128)(2,1)}), bf16[32,1,24,128,128]{4,3,2,1,0:T(8,128)(2,1)}) %all-gather.3.cloned.1.call-update) | async-done | bytes 25165840 | tf_op jit(solution)/shard_map/all_gather | solution.py:443
  168.9 12.1 %fusion.91 = (bf16[3,1,24,128,128]{4,3,2,1,0:T(8,128)(2,1)}, bf16[3,1,24,128,128]{4,3,2,1,0:T(8,128)(2,1)}, bf16[3,1,24,128,128]{4,3,2,1,0:T(8,128)(2,1)}, bf16[...) fusion(bf16[16,2,24,128,128]{4,3,2,1,0:T(8,128)(2,1)} %bitcast.263), kind=kLoop, calls=%fused_computation.180 | loop fusion | bytes 28311552 | tf_op jit(solution)/shard_map/slice | solution.py:540
  181.0 9.9 fusion.92
  200.9 5.6 fusion.7
  212.3 4.5 copy.175
  236.7 6.6 collective-permute-done
  243.3 3.5 fusion.100
  250.1 9.2 attention_forward.1
  260.8 5.9 multiply_convert_fusion
  272.4 4.3 decoder_forward.1
  280.7 38.8 %psum.21.sums_ref = f32[16,128]{1,0:T(8,128)} all-reduce(f32[16,128]{1,0:T(8,128)} %copy-done.24), channel_id=1, replica_groups=mesh['dp'=16,'mp'=2] {'dp','mp'}, use_global_device_ids=true, to_apply=%region_4.5 | all-reduce | flops 2048 | bytes 16384 | tf_op jit(solution)/shard_map/psum | solution.py:448
  328.6 5.1 fusion.103
  335.4 7.0 convert_reduce_fusion
  350.2 12.7 %attention_backward.1 = (bf16[512,768]{1,0:T(8,128)(2,1)S(1)}, bf16[512,768]{1,0:T(8,128)(2,1)S(1)}, bf16[512,768]{1,0:T(8,128)(2,1)S(1)}) custom-call(bf16[512,2304]{1,0:T(8,128)(2,1)S(1)} %fusion.6.qkv_q.qkv_k.qkv_v, bf16[512,2304]{1,0:T(8,128)(2,1)S(1)} %fusion.6.qkv_q.qkv_k.qkv_v, bf16[512,2304]{1,0:T(8,128)(2,1)S(1)} %fusion.6.qkv_q.qkv_k.qkv_v, ...), custom_call_target="tpu_custom_call" | custom-call | flops 2013265920 | bytes 5505024 | tf_op jit(solution)/shard_map/attention_backward/pallas_call | solution.py:187
  368.9 5.2 fusion.83
  374.1 5.5 fusion.84
  379.7 5.1 fusion.70
  384.7 5.2 fusion.104
  405.2 13.7 %concatenate.62 = f32[458110]{0:T(1024)} concatenate(f32[393216]{0:T(1024)S(1)} %reshape.417, f32[5376]{0:T(1024)S(1)} %reshape.418, f32[3072]{0:T(1024)S(1)} %get-tuple-element.158, f32[768]{0:T(1024)S(1)} %get-tuple-element.143, f32[128]{0:T(128)S(1)} %slice_reduce_fusion, f32[55296]{0:T(1024)S(1)} %reshape.420, f32[16]{0:T(128)S(1)} %slice_reduce_fusion.2, f32[224]{0:T(256)S(1)} %reshape.421, ...), dimensions={0} | concatenate | bytes 3664880 | tf_op jit(solution)/shard_map/concatenate | solution.py:694
  421.3 5.3 fusion.95
  426.5 5.2 copy.192
  431.7 4.8 reshape.395
  436.5 5.5 copy.193
  445.0 4.9 reshape.405
  449.9 5.5 copy.199
  455.4 8.2 fusion.94
  463.7 6.8 reshape.399
  470.5 6.5 copy.195
  477.0 8.1 fusion.93
  485.1 6.6 reshape.401
  491.7 5.7 copy.196
  497.4 6.6 reshape.411
  504.0 5.8 copy.202
  509.8 7.1 reshape.409
  516.9 6.4 copy.201
  523.2 4.8 slice_bitcast_fusion.1
  550.8 6.5 constant_dynamic-update-slice_fusion.3
  563.1 3.5 fusion.15
  569.6 5.8 convolution_add_fusion.1
  575.4 6.6 copy.190
  582.0 6.8 copy.224
  588.9 6.6 copy.191
  595.5 9.6 broadcast_multiply_fusion
  605.1 34.1 %maximum_maximum_fusion = f32[2,384,128,128]{3,2,1,0:T(8,128)} fusion(f32[1,288,128,128]{3,2,1,0:T(8,128)} %bitcast.267, f32[1,288,128,128]{3,2,1,0:T(8,128)} %bitcast.266, f32[2,96,128,128]{3,2,1,0:T(8,128)} %broadcast_multiply_fusion), kind=kLoop, calls=%fused_computation | loop fusion | flops 25165824 | bytes 100663296 | tf_op jit(solution)/shard_map/concatenate | solution.py:459
  639.2 34.5 %copy.204 = f32[16,2,24,128,128]{4,3,2,1,0:T(8,128)} copy(f32[16,2,24,128,128]{4,3,2,0,1:T(8,128)} %bitcast.262) | data formatting | bytes 100663296 | tf_op jit(solution)/shard_map/transpose | solution.py:461
  677.9 426.9 %reduce-scatter.2.cloned.1.call-done = f32[1,24,128,128]{3,2,1,0:T(8,128)} async-done(((f32[32,24,128,128]{3,2,1,0:T(8,128)}), f32[1,24,128,128]{3,2,1,0:T(8,128)}) %reduce-scatter.2.cloned.1.call-update) | async-done | bytes 1572880 | tf_op jit(solution)/shard_map/reduce_scatter | solution.py:462
  1108.4 39.3 %psum.22 = f32[]{:T(128)} all-reduce(f32[]{:T(128)} %multiply_reduce_fusion.4), channel_id=1, replica_groups=mesh['dp'=16,'mp'=2] {'dp','mp'}, use_global_device_ids=true, to_apply=%region_11.12 | all-reduce | flops 1 | bytes 8 | tf_op jit(solution)/shard_map/psum | solution.py:448
  1149.1 3.9 fusion.33
  (378 shorter events, 172.2 us)
Async XLA Ops:
  7.2 161.7 %all-gather.3.cloned.1.call-start = ((), (), s32[]{:S(2)}) async-start(), calls=%async_computation.3 | async-start | bytes 25952256 | tf_op jit(solution)/shard_map/all_gather | solution.py:443
  9.8 665.1 %all-reduce.4.cloned.1.call-start = ((), (), s32[]{:S(2)}) async-start(), calls=%async_computation.2 | async-start | bytes 3670016 | tf_op jit(solution)/shard_map/psum | solution.py:448
  10.0 250.8 %copy-start.89 = (f32[3072]{0:T(1024)}, f32[3072]{0:T(1024)S(1)}, u32[]{:S(2)}) copy-start(f32[3072]{0:T(1024)S(1)} %slice.286) | copy-start | bytes 36868
  10.2 6.6 copy-start.88
  26.0 221.3 %copy-start.86 = (f32[768]{0:T(1024)}, f32[768]{0:T(1024)S(1)}, u32[]{:S(2)}) copy-start(f32[768]{0:T(1024)S(1)} %get-tuple-element.139) | copy-start | bytes 9220
  26.0 221.3 %copy-start.97 = (f32[768]{0:T(1024)}, f32[768]{0:T(1024)S(1)}, u32[]{:S(2)}) copy-start(f32[768]{0:T(1024)S(1)} %get-tuple-element.138) | copy-start | bytes 9220
  26.0 234.7 %copy-start.84 = (f32[768]{0:T(1024)}, f32[768]{0:T(1024)S(1)}, u32[]{:S(2)}) copy-start(f32[768]{0:T(1024)S(1)} %get-tuple-element.136) | copy-start | bytes 9220
  26.0 234.7 %copy-start.95 = (f32[768]{0:T(1024)}, f32[768]{0:T(1024)S(1)}, u32[]{:S(2)}) copy-start(f32[768]{0:T(1024)S(1)} %get-tuple-element.135) | copy-start | bytes 9220
  200.9 7.0 copy-start.62
  206.4 36.9 %collective-permute-start = (f32[512,768]{1,0:T(8,128)}, f32[512,768]{1,0:T(8,128)}, u32[]{:S(2)}, u32[]{:S(2)}) collective-permute-start(f32[512,768]{1,0:T(8,128)} %fusion.7), channel_id=1, source_target_pairs={{0,1},{1,0},{2,3},{3,2},{4,5},{5,4},{6,7},{7,6},{8,9},{9,8},{10,11... | collective-permute-start | bytes 4718600 | tf_op jit(solution)/shard_map/ppermute | solution.py:452
  212.2 4.6 copy-start.42
  232.9 33.8 %copy-start.67 = (bf16[3072,768]{1,0:T(8,128)(2,1)}, bf16[3072,768]{1,0:T(8,128)(2,1)S(1)}, u32[]{:S(2)}) copy-start(bf16[3072,768]{1,0:T(8,128)(2,1)S(1)} %bitcast_dynamic-update-slice_fusion) | copy-start | bytes 14155780
  233.5 27.2 %copy-start.68 = (bf16[768,3072]{1,0:T(8,128)(2,1)}, bf16[768,3072]{1,0:T(8,128)(2,1)S(1)}, u32[]{:S(2)}) copy-start(bf16[768,3072]{1,0:T(8,128)(2,1)S(1)} %bitcast_dynamic-update-slice_fusion.2) | copy-start | bytes 14155780
  235.1 8.2 copy-start.69
  236.1 7.2 copy-start.60
  236.1 7.2 copy-start.65
  236.7 32.9 %copy-start.66 = (bf16[2304,1024]{1,0:T(8,128)(2,1)}, bf16[2304,1024]{1,0:T(8,128)(2,1)S(1)}, u32[]{:S(2)}) copy-start(bf16[2304,1024]{1,0:T(8,128)(2,1)S(1)} %bitcast_dynamic-update-slice_fusion.4) | copy-start | bytes 14155780
  243.3 4.6 copy-start.72
  246.9 12.5 %copy-start.48 = (f32[512,768]{1,0:T(8,128)}, f32[512,768]{1,0:T(8,128)S(1)}, u32[]{:S(2)}) copy-start(f32[512,768]{1,0:T(8,128)S(1)} %get-tuple-element.151) | copy-start | bytes 4718596
  250.1 9.3 copy-start.76
  260.3 6.4 copy-start.51
  260.3 6.4 copy-start.82
  260.6 6.0 copy-start.93
  326.0 9.3 slice-start.3
  326.0 9.3 slice-start.7
  328.2 5.5 copy-start.10
  328.2 5.5 copy-start.17
  328.2 5.5 copy-start.22
  328.5 6.7 slice-start.4
  328.6 6.7 slice-start.8
  333.8 8.6 slice-start.5
  335.3 7.0 copy-start.52
  335.3 7.0 slice-start.6
  335.3 7.0 copy-start.83
  335.4 7.0 copy-start.85
  335.4 7.0 copy-start.94
  368.9 5.2 copy-start.96
  374.1 5.5 copy-start.57
  379.7 5.1 copy-start.79
  384.7 5.3 copy-start.23
  384.7 5.5 copy-start.11
  418.9 685.9 %reduce-scatter.2.cloned.1.call-start = ((), (), s32[]{:S(2)}) async-start(), calls=%async_computation.1 | async-start | bytes 51904512 | tf_op jit(solution)/shard_map/reduce_scatter | solution.py:462
  418.9 150.7 %collective-permute-start.1 = (bf16[512,768]{1,0:T(8,128)(2,1)}, bf16[512,768]{1,0:T(8,128)(2,1)}, u32[]{:S(2)}, u32[]{:S(2)}) collective-permute-start(bf16[512,768]{1,0:T(8,128)(2,1)} %get-tuple-element.108), channel_id=1, source_target_pairs={{0,1},{1,0},{2,3},{3,2},{4,5},{5,4},{6,7},{7,6},{8,9},{9,8},{10,11... | collective-permute-start | bytes 2359304 | tf_op jit(solution)/shard_map/ppermute | solution.py:452
  548.5 8.8 copy-start.29
  550.8 9.6 slice-start
  563.1 6.5 copy-start.28
  588.9 6.6 copy-start.99
  1104.8 44.3 %copy-start.27 = (f32[1,24,128,128]{3,2,1,0:T(8,128)S(1)}, f32[1,24,128,128]{3,2,1,0:T(8,128)}, u32[]{:S(2)}) copy-start(f32[1,24,128,128]{3,2,1,0:T(8,128)} %reduce-scatter.2.cloned.1.call-done) | copy-start | bytes 4718596
  (66 other events, 133.3 us)
Sparse Core Ops, SparseCore 0:
  11.5 157.3 all-gather.2
  419.0 134.2 all-reduce.3
  673.8 430.9 reduce-scatter.1

commit v2 on v1

--- a/solution.py
+++ b/solution.py
@@ -438,13 +438,706 @@
     )(sums, batch, labels, chance, features, conv_slope, grid_slope, conv_in, conv_t, head_t)
 
 
+LAYERS = 4
+PIECES = 24
+ROWS_A = 272
+ROWS_B = 136
+ROWS_N = ROWS_A + ROWS_B
+ROWS_E = 128
+CHUNK = 8 * ROWS_N
+AUX_ROWS = CHUNK - 24 * BS
+LAG = 2
+HOP_LAG = 1
+CORE_SLOTS = 6
+SEND_SLOTS = 4
+KEEP = 8
+SUM_SLOTS = 12
+
+
+def remote(src, dst, send_sem, recv_sem, device):
+    return pltpu.make_async_remote_copy(
+        src_ref=src,
+        dst_ref=dst,
+        send_sem=send_sem,
+        recv_sem=recv_sem,
+        device_id=device,
+        device_id_type=MESH,
+    )
+
+
+def places():
+    dp, x = lax.axis_index("dp"), lax.axis_index("mp")
+    z, y, c = dp // 4, (dp // 2) % 2, dp % 2
+    return dict(
+        dp=dp,
+        x=x,
+        y=y,
+        z=z,
+        c=c,
+        at_core=(dp + 1 - 2 * c, x),
+        at_x=(dp, 1 - x),
+        at_y=(dp + 2 - 4 * y, x),
+        above=(lax.rem(dp + 4, 4 * LAYERS), x),
+        below=(lax.rem(dp + 4 * LAYERS - 4, 4 * LAYERS), x),
+    )
+
+
+def greet_neighbours(at):
+    barrier = pltpu.get_barrier_semaphore()
+    for name in ("at_core", "at_x", "at_y"):
+        pl.semaphore_signal(barrier, inc=1, device_id=at[name], device_id_type=MESH)
+
+    @pl.when(at["z"] < LAYERS - 1)
+    def _():
+        pl.semaphore_signal(barrier, inc=1, device_id=at["above"], device_id_type=MESH)
+
+    @pl.when(at["z"] > 0)
+    def _():
+        pl.semaphore_signal(barrier, inc=1, device_id=at["below"], device_id_type=MESH)
+
+    peers = 3 + jnp.minimum(at["z"], 1) + jnp.minimum(LAYERS - 1 - at["z"], 1)
+    pl.semaphore_wait(barrier, peers)
+
+
+def gather_kernel(rows, rows_a, skip, in_ref, out_ref, local_sem, up_sem, down_sem, z_recv, x_send, x_recv, y_send, y_recv, core_send, core_recv):
+    at = places()
+    x, y, z, c = at["x"], at["y"], at["z"], at["c"]
+    last = LAYERS - 1
+    every, a, b = pl.ds(0, rows), pl.ds(0, rows_a), pl.ds(rows_a, rows - rows_a)
+
+    def spot(l, y_at, c_at, x_at, part):
+        return out_ref.at[x_at, l * 4 + y_at * 2 + c_at, part]
+
+    def send(ref, send_sem, recv_sem, device):
+        return remote(ref, ref, send_sem, recv_sem, device)
+
+    def up(l):
+        return send(spot(l, y, c, x, every), up_sem.at[l], z_recv.at[l], at["above"])
+
+    def down(l):
+        return send(spot(l, y, c, x, every), down_sem.at[l], z_recv.at[l], at["below"])
+
+    def x_a(l, x_at):
+        return send(spot(l, y, c, x_at, a), x_send.at[l, 0], x_recv.at[l, 0], at["at_x"])
+
+    def x_b(l, x_at):
+        return send(spot(l, y, c, x_at, b), x_send.at[l, 1], x_recv.at[l, 1], at["at_x"])
+
+    def x_relay(l, x_at):
+        return send(spot(l, 1 - y, c, x_at, b), x_send.at[l, 2], x_recv.at[l, 2], at["at_x"])
+
+    def y_a(l, y_at):
+        return send(spot(l, y_at, c, x, a), y_send.at[l, 0], y_recv.at[l, 0], at["at_y"])
+
+    def y_b(l, y_at):
+        return send(spot(l, y_at, c, x, b), y_send.at[l, 1], y_recv.at[l, 1], at["at_y"])
+
+    def y_relay(l, y_at):
+        return send(spot(l, y_at, c, 1 - x, a), y_send.at[l, 2], y_recv.at[l, 2], at["at_y"])
+
+    def core(l, kind, c_at):
+        spots = (
+            spot(l, y, c_at, x, every),
+            spot(l, 1 - y, c_at, x, every),
+            spot(l, y, c_at, 1 - x, every),
+            spot(l, 1 - y, c_at, 1 - x, a),
+            spot(l, 1 - y, c_at, 1 - x, b),
+        )
+        return send(spots[kind], core_send.at[l, kind], core_recv.at[l, kind], at["at_core"])
+
+    def wide(l):
+        return (l > 0) if skip else (l >= 0)
+
+    own = pltpu.make_async_copy(in_ref, out_ref.at[x, at["dp"]], local_sem)
+    own.start()
+    greet_neighbours(at)
+    own.wait()
+
+    def arrive(l, came_up, came_down):
+        if not (came_up and came_down):
+            up(l).wait_recv()
+        if came_up:
+
+            @pl.when(z < last)
+            def _():
+                up(l).start()
+
+        if came_down:
+
+            @pl.when(z > 0)
+            def _():
+                down(l).start()
+
+        y_b(l, y).start()
+
+        @pl.when(wide(l))
+        def _():
+            x_a(l, x).start()
+            x_b(l, x).start()
+
+        y_a(l, y).start()
+        core(l, 0, c).start()
+
+    def relay(l):
+        y_b(l, 1 - y).wait_recv()
+
+        @pl.when(wide(l))
+        def _():
+            x_relay(l, x).start()
+            x_a(l, 1 - x).wait_recv()
+            y_relay(l, y).start()
+
+        y_a(l, 1 - y).wait_recv()
+        core(l, 1, c).start()
+
+        @pl.when(wide(l))
+        def _():
+            x_b(l, 1 - x).wait_recv()
+            core(l, 2, c).start()
+
+    def finish(l):
+        @pl.when(wide(l))
+        def _():
+            y_relay(l, 1 - y).wait_recv()
+            core(l, 3, c).start()
+            x_relay(l, 1 - x).wait_recv()
+            core(l, 4, c).start()
+
+    def both(r, run):
+        if r < 0 or r >= LAYERS:
+            return
+        if r == 0:
+            run(z, True, True)
+            return
+
+        @pl.when(z - r >= 0)
+        def _():
+            run(z - r, True, False)
+
+        @pl.when(z + r <= last)
+        def _():
+            run(z + r, False, True)
+
+    for r in range(LAYERS + 2):
+        both(r, arrive)
+        both(r - 1, lambda l, up_way, down_way: relay(l))
+        both(r - 2, lambda l, up_way, down_way: finish(l))
+
+    def settle(l, carry):
+        for kind in (0, 1):
+            core(l, kind, 1 - c).wait_recv()
+            core(l, kind, c).wait_send()
+        y_a(l, y).wait_send()
+        y_b(l, y).wait_send()
+
+        @pl.when(wide(l))
+        def _():
+            for kind in (2, 3, 4):
+                core(l, kind, 1 - c).wait_recv()
+                core(l, kind, c).wait_send()
+            for copy in (x_a(l, x), x_b(l, x), x_relay(l, x), y_relay(l, y)):
+                copy.wait_send()
+
+        @pl.when((l <= z) & (z < last))
+        def _():
+            up(l).wait_send()
+
+        @pl.when((l >= z) & (z > 0))
+        def _():
+            down(l).wait_send()
+
+        return carry
+
+    lax.fori_loop(0, LAYERS, settle, 0)
+
+
+def gather_all(values, rows_a, skip, collective_id, name, memory=pl.ANY):
+    rows = values.shape[0]
+
+    def sems(*shape):
+        return pltpu.SemaphoreType.DMA(shape)
+
+    return pl.pallas_call(
+        functools.partial(gather_kernel, rows, rows_a, skip),
+        out_shape=jax.ShapeDtypeStruct((MP, 4 * LAYERS, rows, BS), values.dtype),
+        in_specs=[pl.BlockSpec(memory_space=memory)],
+        out_specs=pl.BlockSpec(memory_space=memory),
+        scratch_shapes=[
+            pltpu.SemaphoreType.DMA,
+            sems(LAYERS),
+            sems(LAYERS),
+            sems(LAYERS),
+            sems(LAYERS, 3),
+            sems(LAYERS, 3),
+            sems(LAYERS, 3),
+            sems(LAYERS, 3),
+            sems(LAYERS, 5),
+            sems(LAYERS, 5),
+        ],
+        compiler_params=pltpu.CompilerParams(
+            collective_id=collective_id, has_side_effects=True, vmem_limit_bytes=32 * MIB
+        ),
+        cost_estimate=pl.CostEstimate(flops=0, bytes_accessed=32 * rows * BS * 4, transcendentals=0),
+        name=name,
+    )(values)
+
+
+def reduce_kernel(
+    n_ref,
+    e_ref,
+    out_ref,
+    own_n,
+    own_e,
+    core_n,
+    core_e,
+    keep_own,
+    keep_a,
+    keep_b,
+    keep_e,
+    xs_a,
+    xs_b,
+    ys_b,
+    ys_a,
+    ys_e,
+    xr_a,
+    xr_b,
+    yr_b,
+    yr_a,
+    yr_e,
+    sum_n,
+    sum_e,
+    up_n,
+    down_n,
+    down_e,
+    own_sem,
+    core_send,
+    core_recv,
+    credit,
+    xs_a_sem,
+    xs_b_sem,
+    ys_b_sem,
+    ys_a_sem,
+    ys_e_sem,
+    xr_a_sem,
+    xr_b_sem,
+    yr_b_sem,
+    yr_a_sem,
+    yr_e_sem,
+    z_n_sem,
+    z_e_sem,
+    up_n_sem,
+    down_n_sem,
+    down_e_sem,
+):
+    at = places()
+    x, y, z, c = at["x"], at["y"], at["z"], at["c"]
+
+    def layer_of(s):
+        return LAYERS - 1 - lax.rem(s, 3)
+
+    def rows_of(s):
+        return pl.ds(pl.multiple_of((s // 3) * ROWS_N, 8), ROWS_N)
+
+    def rows_e(s):
+        return pl.ds(pl.multiple_of(s * ROWS_E, 8), ROWS_E)
+
+    def own_loads(s):
+        slot = lax.rem(s, 3)
+        return (
+            pltpu.make_async_copy(
+                n_ref.at[:, layer_of(s) - 1, :, c, rows_of(s)], own_n.at[slot], own_sem.at[slot, 0]
+            ),
+            pltpu.make_async_copy(e_ref.at[:, c, rows_e(s)], own_e.at[slot], own_sem.at[slot, 1]),
+        )
+
+    def core_copies(s):
+        slot = lax.rem(s, CORE_SLOTS)
+        return (
+            remote(
+                n_ref.at[:, layer_of(s) - 1, :, 1 - c, rows_of(s)],
+                core_n.at[slot],
+                core_send.at[s, 0],
+                core_recv.at[slot, 0],
+                at["at_core"],
+            ),
+            remote(
+                e_ref.at[:, 1 - c, rows_e(s)],
+                core_e.at[slot],
+                core_send.at[s, 1],
+                core_recv.at[slot, 1],
+                at["at_core"],
+            ),
+        )
+
+    def first_copies(s):
+        slot = lax.rem(s, SEND_SLOTS)
+        return (
+            remote(xs_a.at[slot], xr_a.at[s], xs_a_sem.at[slot], xr_a_sem.at[s], at["at_x"]),
+            remote(ys_b.at[slot], yr_b.at[s], ys_b_sem.at[slot], yr_b_sem.at[s], at["at_y"]),
+            remote(ys_e.at[slot], yr_e.at[s], ys_e_sem.at[slot], yr_e_sem.at[s], at["at_y"]),
+        )
+
+    def second_copies(s):
+        slot = lax.rem(s, SEND_SLOTS)
+        return (
+            remote(ys_a.at[slot], yr_a.at[s], ys_a_sem.at[slot], yr_a_sem.at[s], at["at_y"]),
+            remote(xs_b.at[slot], xr_b.at[s], xs_b_sem.at[slot], xr_b_sem.at[s], at["at_x"]),
+        )
+
+    def up_copy(s):
+        slot = lax.rem(s, SUM_SLOTS)
+        return remote(sum_n.at[slot], up_n.at[s], z_n_sem.at[slot], up_n_sem.at[s], at["above"])
+
+    def down_copy(s):
+        slot = lax.rem(s, SUM_SLOTS)
+        return remote(sum_n.at[slot], down_n.at[s], z_n_sem.at[slot], down_n_sem.at[s], at["below"])
+
+    def down_copy_e(s):
+        slot = lax.rem(s, SUM_SLOTS)
+        return remote(sum_e.at[slot], down_e.at[s], z_e_sem.at[slot], down_e_sem.at[s], at["below"])
+
+    for s in range(2):
+        for copy in own_loads(s):
+            copy.start()
+    greet_neighbours(at)
+    for s in range(2):
+        for copy in core_copies(s):
+            copy.start()
+
+    def first(s):
+        @pl.when(s + 2 < PIECES)
+        def _():
+            for copy in own_loads(s + 2):
+                copy.start()
+
+            @pl.when(s + 2 >= CORE_SLOTS)
+            def _():
+                pl.semaphore_wait(credit, 1)
+
+            for copy in core_copies(s + 2):
+                copy.start()
+
+        for copy in own_loads(s):
+            copy.wait()
+        for copy in core_copies(s):
+            copy.wait_recv()
+
+        @pl.when(s >= SEND_SLOTS)
+        def _():
+            for copy in first_copies(s - SEND_SLOTS):
+                copy.wait_send()
+
+        own, core = lax.rem(s, 3), lax.rem(s, CORE_SLOTS)
+        send, keep = lax.rem(s, SEND_SLOTS), lax.rem(s, KEEP)
+        a, b = pl.ds(0, ROWS_A), pl.ds(ROWS_A, ROWS_B)
+        for other in range(2):
+            xs_a[send, other] = own_n[own, 1 - x, other, a] + core_n[core, 1 - x, other, a]
+        to_x, to_y, to_y_e = first_copies(s)
+        to_x.start()
+        for other in range(2):
+            ys_b[send, other] = own_n[own, other, 1 - y, b] + core_n[core, other, 1 - y, b]
+        to_y.start()
+        ys_e[send] = own_e[own, 1 - y] + core_e[core, 1 - y]
+        to_y_e.start()
+        keep_own[keep] = own_n[own, x, y] + core_n[core, x, y]
+        keep_a[keep] = own_n[own, x, 1 - y, a] + core_n[core, x, 1 - y, a]
+        keep_b[keep] = own_n[own, 1 - x, y, b] + core_n[core, 1 - x, y, b]
+        keep_e[keep] = own_e[own, y] + core_e[core, y]
+
+        @pl.when(s + CORE_SLOTS < PIECES)
+        def _():
+            pl.semaphore_signal(credit, inc=1, device_id=at["at_core"], device_id_type=MESH)
+
+    def second(s):
+        to_x, to_y, _ = first_copies(s)
+        to_x.wait_recv()
+        to_y.wait_recv()
+
+        @pl.when(s >= SEND_SLOTS)
+        def _():
+            for copy in second_copies(s - SEND_SLOTS):
+                copy.wait_send()
+
+        send, keep = lax.rem(s, SEND_SLOTS), lax.rem(s, KEEP)
+        a, b = pl.ds(0, ROWS_A), pl.ds(ROWS_A, ROWS_B)
+        ys_a[send] = keep_a[keep] + xr_a[s, 1 - y]
+        xs_b[send] = keep_b[keep] + yr_b[s, 1 - x]
+        for copy in second_copies(s):
+            copy.start()
+        keep_own[keep, a] = keep_own[keep, a] + xr_a[s, y]
+        keep_own[keep, b] = keep_own[keep, b] + yr_b[s, x]
+
+    def third(s):
+        first_copies(s)[2].wait_recv()
+        for copy in second_copies(s):
+            copy.wait_recv()
+
+        @pl.when((s >= SUM_SLOTS) & (z != layer_of(s)))
+        def _():
+            up_copy(s - SUM_SLOTS).wait_send()
+
+        @pl.when((s >= SUM_SLOTS) & (z > 0))
+        def _():
+            down_copy_e(s - SUM_SLOTS).wait_send()
+
+        slot, keep = lax.rem(s, SUM_SLOTS), lax.rem(s, KEEP)
+        a, b = pl.ds(0, ROWS_A), pl.ds(ROWS_A, ROWS_B)
+        sum_n[slot, a] = keep_own[keep, a] + yr_a[s]
+        sum_n[slot, b] = keep_own[keep, b] + xr_b[s]
+        sum_e[slot] = keep_e[keep] + yr_e[s]
+
+    def along(s, hop):
+        slot = lax.rem(s, SUM_SLOTS)
+        layer = layer_of(s)
+        last = LAYERS - 1
+        away = jnp.where(z < layer, z, jnp.where(z > layer, last - z, jnp.maximum(z, last - z)))
+
+        @pl.when(away == hop)
+        def _():
+            @pl.when((z > 0) & (z <= layer))
+            def _():
+                up_copy(s).wait_recv()
+                sum_n[slot] = sum_n[slot] + up_n[s]
+
+            @pl.when((z < last) & (z >= layer))
+            def _():
+                down_copy(s).wait_recv()
+                sum_n[slot] = sum_n[slot] + down_n[s]
+
+            @pl.when(z < layer)
+            def _():
+                up_copy(s).start()
+
+            @pl.when(z > layer)
+            def _():
+                down_copy(s).start()
+
+            @pl.when(z == layer)
+            def _():
+                out_ref[rows_of(s)] = sum_n[slot]
+
+        away_e = jnp.where(z == 0, last, last - z)
+
+        @pl.when(away_e == hop)
+        def _():
+            @pl.when(z < last)
+            def _():
+                down_copy_e(s).wait_recv()
+                sum_e[slot] = sum_e[slot] + down_e[s]
+
+            @pl.when(z > 0)
+            def _():
+                down_copy_e(s).start()
+
+            @pl.when(z == 0)
+            def _():
+                out_ref[rows_e(s)] = sum_e[slot]
+
+    def guarded(run, s):
+        @pl.when((s >= 0) & (s < PIECES))
+        def _():
+            run(s)
+
+    def step(t, carry):
+        guarded(first, t)
+        guarded(second, t - LAG)
+        guarded(third, t - 2 * LAG)
+        for hop in range(LAYERS):
+            guarded(functools.partial(along, hop=hop), t - 2 * LAG - hop * HOP_LAG)
+        return carry
+
+    lax.fori_loop(0, PIECES + 2 * LAG + (LAYERS - 1) * HOP_LAG, step, 0)
+
+    def drain_sends(i, carry):
+        s = PIECES - SEND_SLOTS + i
+        for copy in first_copies(s) + second_copies(s):
+            copy.wait_send()
+        return carry
+
+    lax.fori_loop(0, SEND_SLOTS, drain_sends, 0)
+
+    def drain_sums(i, carry):
+        s = PIECES - SUM_SLOTS + i
+
+        @pl.when(z != layer_of(s))
+        def _():
+            up_copy(s).wait_send()
+
+        @pl.when(z > 0)
+        def _():
+            down_copy_e(s).wait_send()
+
+        return carry
+
+    lax.fori_loop(0, SUM_SLOTS, drain_sums, 0)
+
+    def drain_core(s, carry):
+        for copy in core_copies(s):
+            copy.wait_send()
+        return carry
+
+    lax.fori_loop(0, PIECES, drain_core, 0)
+
+    @pl.when(z == 0)
+    def _():
+        out_ref[pl.ds(PIECES * ROWS_E, CHUNK - PIECES * ROWS_E)] = jnp.zeros(
+            (CHUNK - PIECES * ROWS_E, BS), jnp.float32
+        )
+
+
+def reduce_to_owners(rest, embed):
+    def room(*shape):
+        return pltpu.VMEM(shape + (BS,), jnp.float32)
+
+    def sems(*shape):
+        return pltpu.SemaphoreType.DMA(shape)
+
+    return pl.pallas_call(
+        reduce_kernel,
+        out_shape=jax.ShapeDtypeStruct((CHUNK, BS), jnp.float32),
+        in_specs=[pl.BlockSpec(memory_space=pl.ANY)] * 2,
+        out_specs=pl.BlockSpec(memory_space=pltpu.VMEM),
+        scratch_shapes=[
+            room(3, 2, 2, ROWS_N),
+            room(3, 2, ROWS_E),
+            room(CORE_SLOTS, 2, 2, ROWS_N),
+            room(CORE_SLOTS, 2, ROWS_E),
+            room(KEEP, ROWS_N),
+            room(KEEP, ROWS_A),
+            room(KEEP, ROWS_B),
+            room(KEEP, ROWS_E),
+            room(SEND_SLOTS, 2, ROWS_A),
+            room(SEND_SLOTS, ROWS_B),
+            room(SEND_SLOTS, 2, ROWS_B),
+            room(SEND_SLOTS, ROWS_A),
+            room(SEND_SLOTS, ROWS_E),
+            room(PIECES, 2, ROWS_A),
+            room(PIECES, ROWS_B),
+            room(PIECES, 2, ROWS_B),
+            room(PIECES, ROWS_A),
+            room(PIECES, ROWS_E),
+            room(SUM_SLOTS, ROWS_N),
+            room(SUM_SLOTS, ROWS_E),
+            room(PIECES, ROWS_N),
+            room(PIECES, ROWS_N),
+            room(PIECES, ROWS_E),
+            sems(3, 2),
+            sems(PIECES, 2),
+            sems(CORE_SLOTS, 2),
+            pltpu.SemaphoreType.REGULAR,
+            sems(SEND_SLOTS),
+            sems(SEND_SLOTS),
+            sems(SEND_SLOTS),
+            sems(SEND_SLOTS),
+            sems(SEND_SLOTS),
+            sems(PIECES),
+            sems(PIECES),
+            sems(PIECES),
+            sems(PIECES),
+            sems(PIECES),
+            sems(SUM_SLOTS),
+            sems(SUM_SLOTS),
+            sems(PIECES),
+            sems(PIECES),
+            sems(PIECES),
+        ],
+        compiler_params=pltpu.CompilerParams(
+            collective_id=1, has_side_effects=True, vmem_limit_bytes=58 * MIB
+        ),
+        cost_estimate=pl.CostEstimate(flops=0, bytes_accessed=100 * MIB, transcendentals=0),
+        name="reduce_to_owners",
+    )(rest, embed)
+
+
+def blocks_kernel(first_block, per_row, step_rows, transposed, has_buffer, *refs):
+    x_ref, g_ref = refs[:2]
+    out_ref, tiles, sems = refs[-3:]
+    m, i = pl.program_id(0), pl.program_id(1)
+    steps = pl.num_programs(1)
+    at = m * steps + i
+    slot = lax.rem(at, 2)
+    total = pl.num_programs(0) * steps
+
+    def drain(which):
+        pltpu.make_async_copy(tiles.at[which], tiles.at[which], sems.at[which]).wait()
+
+    @pl.when(at >= 2)
+    def _():
+        drain(slot)
+
+    tiles[slot] = dot(x_ref[...], g_ref[...], ((0,), (1,) if transposed else (0,)))
+    for r in range(step_rows):
+        for c in range(per_row):
+            block = first_block + (i * step_rows + r) * per_row + c
+            chunk, at_row = block // 24, lax.rem(block, 24) * BS
+            pltpu.make_async_copy(
+                tiles.at[slot, r * BS : (r + 1) * BS, c * BS : (c + 1) * BS],
+                out_ref.at[m, chunk, pl.ds(pl.multiple_of(at_row, BS), BS)],
+                sems.at[slot],
+            ).start()
+
+    @pl.when(at == total - 1)
+    def _():
+        drain(slot)
+
+        @pl.when(total > 1)
+        def _():
+            drain(1 - slot)
+
+
+def grad_blocks(x, g, parts, rows, per_row, step_rows, first_block, split_x, split_g, buffer, name, chunks=12, depth=CHUNK, transposed=False):
+    steps = rows // step_rows
+    tokens = x.shape[0]
+    width = per_row * BS
+    x_spec = pl.BlockSpec(
+        (tokens, step_rows * BS), (lambda m, i: (0, m * steps + i)) if split_x else (lambda m, i: (0, i))
+    )
+    if transposed:
+        g_spec = pl.BlockSpec((width, tokens), lambda m, i: (0, 0))
+    else:
+        g_spec = pl.BlockSpec((tokens, width), (lambda m, i: (0, m)) if split_g else (lambda m, i: (0, 0)))
+    anywhere = pl.BlockSpec(memory_space=pl.ANY)
+    operands = [x, g] + ([] if buffer is None else [buffer])
+    return pl.pallas_call(
+        functools.partial(
+            blocks_kernel, first_block, per_row, step_rows, transposed, buffer is not None
+        ),
+        grid=(parts, steps),
+        out_shape=jax.ShapeDtypeStruct((parts, chunks, depth, BS), jnp.float32),
+        in_specs=[x_spec, g_spec] + ([] if buffer is None else [anywhere]),
+        out_specs=anywhere,
+        input_output_aliases={} if buffer is None else {2: 0},
+        scratch_shapes=[
+            pltpu.VMEM((2, step_rows * BS, width), jnp.float32),
+            pltpu.SemaphoreType.DMA((2,)),
+        ],
+        compiler_params=pltpu.CompilerParams(vmem_limit_bytes=32 * MIB),
+        cost_estimate=pl.CostEstimate(
+            flops=2 * tokens * parts * rows * BS * width,
+            bytes_accessed=parts * rows * BS * width * 4,
+            transcendentals=0,
+        ),
+        name=name,
+    )(*operands)
+
+
+def fast_mesh():
+    return lax.axis_size("dp") == 4 * LAYERS and lax.axis_size("mp") == MP
+
+
 def gather_weights(blocks):
-    low = blocks.astype(jnp.bfloat16)[0]
-    gathered = lax.all_gather(low, ("dp", "mp"), axis=0, tiled=True)
-    return gathered.reshape(lax.axis_size("dp"), MP, -1, BS, BS)
-
-
-def sum_small(values):
+    low = blocks.astype(jnp.bfloat16)[0, 0]
+    if fast_mesh():
+        gathered = gather_all(low.reshape(-1, BS), 8 * BS, True, 2, "gather_weights")
+    else:
+        gathered = lax.all_gather(low, ("dp", "mp"), axis=0, tiled=False)
+        gathered = gathered.reshape((-1, MP) + low.shape).swapaxes(0, 1)
+    return gathered.reshape(MP, -1, BS, BS)
+
+
+def sum_sums(values):
+    if fast_mesh():
+        return jnp.sum(gather_all(values, 8, False, 3, "gather_sums", pltpu.VMEM), (0, 1))
     return lax.psum(values, ("dp", "mp"))
 
 
@@ -452,13 +1145,12 @@
     return lax.ppermute(values, "mp", [(0, 1), (1, 0)])
 
 
-def reduce_blocks(embed_grad, block_grads):
+def reduce_plain(rest, embed):
     part = lax.axis_index("mp")
     own = (jnp.arange(MP) == part).astype(jnp.float32)
-    first = embed_grad[None] * own[:, None, None, None]
-    every = jnp.concatenate([first, block_grads], 1)
+    first = embed.reshape(1, -1, BS, BS) * own[:, None, None, None]
     dp = lax.axis_size("dp")
-    every = every.reshape(MP, dp, -1, BS, BS).transpose(1, 0, 2, 3, 4)
+    every = jnp.concatenate([first, rest], 1).reshape(MP, dp, -1, BS, BS).transpose(1, 0, 2, 3, 4)
     return lax.psum_scatter(
         every.reshape(dp * MP, -1, BS, BS), ("dp", "mp"), scatter_dimension=0, tiled=True
     )[0]
@@ -531,17 +1223,15 @@
     gain, shift = pieces["norm_gain"], pieces["norm_bias"]
 
     gathered = gather_weights(blocks)
-    per_part = [gathered[:, m].reshape(-1, BS, BS) for m in range(MP)]
     starts = [0]
     for height, breadth in LOCAL_SHAPES:
         starts.append(starts[-1] + height * breadth // (BS * BS))
 
     def matrix_of(which, m):
-        piece = per_part[m][starts[which] : starts[which + 1]]
-        return from_blocks(piece, *LOCAL_SHAPES[which])
-
-    own_embed = lax.dynamic_index_in_dim(gathered, part, 1, False).reshape(-1, BS, BS)
-    w_embed = from_blocks(own_embed[:E_BLOCKS], *LOCAL_SHAPES[0])
+        return from_blocks(gathered[m, starts[which] : starts[which + 1]], *LOCAL_SHAPES[which])
+
+    own_embed = lax.dynamic_index_in_dim(gathered[:, :E_BLOCKS], part, 0, False)
+    w_embed = from_blocks(own_embed, *LOCAL_SHAPES[0])
     w_qkv = jnp.concatenate([matrix_of(1, m) for m in range(MP)], 1)
     w_proj = jnp.concatenate([matrix_of(2, m) for m in range(MP)], 0)
     w_up = jnp.concatenate([matrix_of(3, m) for m in range(MP)], 1)
@@ -593,7 +1283,7 @@
         grid_labels,
         batch,
     )
-    sums = sum_small(sums)
+    sums = sum_sums(sums)
     gu_t, conv_grad, head_grad, small, deconv_bias_grad = decoder_backward(
         all_crops,
         sums,
@@ -614,7 +1304,6 @@
     grad_conv_weight = conv_grad.reshape(27, CF, DEC).transpose(0, 2, 1)
     grad_head_weight = head_grad[:, :NCLS]
 
-    grad_deconv = dot_tn(stacked, gu_t.T)
     stacked_back = dot(gu_t, w_deconv, ((0,), (1,)))
     back_zero_s, back_one_s, back_two = [
         jnp.concatenate([stacked_back[:, (3 * m + s) * HALF : (3 * m + s + 1) * HALF] for m in range(MP)], 1)
@@ -623,9 +1312,7 @@
     grad_down_bias = jnp.sum(back_two, 0)
     two_low = back_two.astype(jnp.bfloat16)
     back_hidden = (hidden_slope * dot_nt(two_low, w_down)).astype(jnp.bfloat16)
-    grad_down = dot_tn(active, two_low)
     grad_up_bias = jnp.sum(back_hidden.astype(jnp.float32), 0)
-    grad_up = dot_tn(normed_two, back_hidden)
     back_normed_two = dot_nt(back_hidden, w_up)
     grad_gain_two = jnp.sum(back_normed_two * normal_two, 0)
     grad_shift_two = jnp.sum(back_normed_two, 0)
@@ -634,13 +1321,11 @@
     )
     grad_proj_bias = jnp.sum(back_one, 0)
     one_low = back_one.astype(jnp.bfloat16)
-    grad_proj = dot_tn(mixed, one_low)
     back_mixed = dot_nt(one_low, w_proj).astype(jnp.bfloat16)
     back_q, back_k, back_v = attention_backward(qkv, back_mixed, lse)
     back_qkv = jnp.concatenate(
         [halves(piece)[m] for m in range(MP) for piece in (back_q, back_k, back_v)], 1
     )
-    grad_qkv = dot_tn(normed_one, back_qkv)
     grad_query_bias = jnp.sum(back_q.astype(jnp.float32), 0)
     grad_value_bias = jnp.sum(back_v.astype(jnp.float32), 0)
     back_normed_one = dot_nt(back_qkv, w_qkv)
@@ -651,23 +1336,28 @@
     )
     zero_low = back_zero.astype(jnp.bfloat16)
     other_low = swap_mp(zero_low)
-    grad_embed = dot_tn(own_rows, zero_low) + dot_tn(other_rows, other_low)
-
-    block_grads = jnp.stack(
-        [
-            jnp.concatenate(
-                [
-                    to_blocks(grad_qkv[:, m * 3 * HALF : (m + 1) * 3 * HALF]),
-                    to_blocks(grad_proj[m * HALF : (m + 1) * HALF]),
-                    to_blocks(grad_up[:, m * FF // MP : (m + 1) * FF // MP]),
-                    to_blocks(grad_down[m * FF // MP : (m + 1) * FF // MP]),
-                    to_blocks(grad_deconv[m * 3 * HALF : (m + 1) * 3 * HALF]),
-                ]
-            )
-            for m in range(MP)
-        ]
-    )
-    owned = reduce_blocks(to_blocks(grad_embed), block_grads)
+    zero_pair = jnp.where(
+        part == 0,
+        jnp.concatenate([zero_low, other_low]),
+        jnp.concatenate([other_low, zero_low]),
+    )
+
+    fast = fast_mesh()
+    depth = CHUNK if fast else 24 * BS
+    rest_grads = None
+    for name, x, g, rows, per_row, start, split_x, split_g in (
+        ("grad_deconv", stacked, gu_t, 9, 8, 216, True, False),
+        ("grad_down", active, two_low, 12, 6, 144, True, False),
+        ("grad_up", normed_two, back_hidden, 6, 12, 72, False, True),
+        ("grad_proj", mixed, one_low, 3, 6, 54, True, False),
+        ("grad_qkv", normed_one, back_qkv, 6, 9, 0, False, True),
+    ):
+        rest_grads = grad_blocks(
+            x, g, MP, rows, per_row, 3, start, split_x, split_g, rest_grads, name, 12, depth, g is gu_t
+        )
+    embed_grads = grad_blocks(
+        patches, zero_pair, 1, 16, 6, 4, 0, False, False, None, "grad_embed", 4, 24 * BS
+    )
     late = jnp.stack(
         [
             grad_gain_one,
@@ -691,11 +1381,28 @@
             grad_head_bias,
         ]
     )
-    aux_sum = sum_small(jnp.concatenate([back_zero.reshape(-1), rest]))
+    aux_parts = jnp.concatenate([back_zero.reshape(-1), rest])
+    if fast:
+        room = 12 * MP * AUX_ROWS * BS
+        aux_rows = jnp.pad(aux_parts, (0, room - aux_parts.shape[0])).reshape(MP, 12, AUX_ROWS, BS)
+        rest_grads = lax.dynamic_update_slice(rest_grads, aux_rows, (0, 0, 24 * BS, 0))
+        reduced = reduce_to_owners(
+            rest_grads.reshape(MP, LAYERS - 1, 2, 2, CHUNK, BS), embed_grads.reshape(2, 2, 24 * BS, BS)
+        )
+        owned = reduced[: 24 * BS].reshape(24, BS, BS)
+        square = jnp.broadcast_to(jnp.sum(owned * owned).reshape(1, 1), (8, BS))
+        gathered_aux = gather_all(
+            jnp.concatenate([reduced[24 * BS :], square]), 64, False, 4, "gather_aux"
+        )
+        block_square = jnp.sum(gathered_aux[:, :, AUX_ROWS, 0])
+        aux_sum = gathered_aux[:, 4:, :AUX_ROWS].reshape(-1)
+    else:
+        owned = reduce_plain(rest_grads.reshape(MP, -1, BS, BS), embed_grads)
+        aux_sum = lax.psum(aux_parts, ("dp", "mp"))
+        block_square = lax.psum(jnp.sum(owned * owned), ("dp", "mp"))
     positions_sum = aux_sum[: NTOK * D]
     embed_bias_sum = jnp.sum(positions_sum.reshape(NTOK, D), 0)
-    aux_total = jnp.concatenate([positions_sum, embed_bias_sum, aux_sum[NTOK * D :]])
-    block_square = sum_small(jnp.sum(owned * owned))
+    aux_total = jnp.concatenate([positions_sum, embed_bias_sum, aux_sum[NTOK * D : NAUX - D]])
     grad_norm = jnp.sqrt(block_square + jnp.sum(aux_total * aux_total))
     clip_scale = clip_value / jnp.maximum(grad_norm, clip_value)
     block_new, stat_new, moment_new, veloc_new = shampoo_step(

time: 1190 us -> 667 us (0.56)
  waiting for transfers between devices: 576 us -> 0.01 us
  Pallas kernels: 28.4 us -> 422 us
  local copies, waits for them, and re-layouts: 322 us -> 149 us
  blocking collectives: 78.2 us -> 0 us
  other arithmetic: 66.6 us -> 27.2 us
  matrix products: 87.1 us -> 50.9 us
  between operations: 18.7 us -> 5.63 us
    reduce_scatter x1 -> x0, waiting for transfers between devices: 427 us -> none  [reduce_blocks(): lax.psum_scatter(every.reshape(dp * MP, -1, BS, BS), ('dp', 'mp'), scatte...]
    pallas_call x0 -> x10, Pallas kernels: none -> 394 us  [the longest x1 211 us: reduce_to_owners(): pl.pallas_call(reduce_kernel, out_shape=jax.ShapeDtypeStruct((CHUNK, BS),...]
    all_gather x1 -> x0, waiting for transfers between devices: 143 us -> none  [gather_weights(): gathered = lax.all_gather(low, ('dp', 'mp'), axis=0, tiled=True)]
    transpose x10 -> x0, local copies, waits for them, and re-layouts: 79 us -> none  [the longest x9 44.5 us: to_blocks(): return matrix.reshape(matrix.shape[0] // BS, BS, matrix.shape[1] // BS, B...]
    psum x2 -> x0, blocking collectives: 78.2 us -> none  [sum_small(): return lax.psum(values, ('dp', 'mp'))]
    reshape x12 -> x1, local copies, waits for them, and re-layouts: 46.2 us -> 2.44 us  [local(): aux_parts = jnp.concatenate([back_zero.reshape(-1), rest])]
    slice x14 -> x7, local copies, waits for them, and re-layouts: 61.2 us -> 26.2 us  [the longest x3 16.9 us: matrix_of(): gathered[m, starts[which]:starts[which + 1]]]
    dot_general x19 -> x12, matrix products: 75.1 us -> 40.9 us  [dot(): lax.dot_general(a, b, (dims, ((), ())), preferred_element_type=jnp.float32)]
  transfers between devices with their start and end apart: 5 -> 2, of which waited for: 3 -> 0; matrix products, arithmetic and copies ran while one was open for 24% -> 10% of each run, Pallas kernels for 0% -> 3%
where the time goes in v2:
time: 667 us; the launch traced here: 656 us
  Pallas kernels  422 us (63%)
  local copies, waits for them, and re-layouts  149 us (22%)
  matrix products  50.9 us (8%)
  other arithmetic  27.2 us (4%)
    pallas_call x1, Pallas kernels, reduce_to_owners(): pl.pallas_call(reduce_kernel, out_shape=jax.ShapeDtypeStruct((CHUNK, BS),...  211 us
    pallas_call x3, Pallas kernels, gather_all(): pl.pallas_call(functools.partial(gather_kernel, rows, rows_a, skip), out_...  150 us
    unnamed x237, local copies, waits for them, and re-layouts  45.2 us
    dot_general x12, matrix products, dot(): lax.dot_general(a, b, (dims, ((), ())), preferred_element_type=jnp.float32)  40.9 us
    pallas_call x6, Pallas kernels, grad_blocks(): pl.pallas_call(functools.partial(blocks_kernel, first_block, per_row, ste...  33.2 us
    transpose x11, local copies, waits for them, and re-layouts, from_blocks(): return piece.reshape(height // BS, breadth // BS, BS, BS).transpose(0, 2,...  27 us
    concatenate x1, local copies, waits for them, and re-layouts, local(): aux_parts = jnp.concatenate([back_zero.reshape(-1), rest])  18.7 us
    slice x3, local copies, waits for them, and re-layouts, matrix_of(): gathered[m, starts[which]:starts[which + 1]]  16.9 us
  transfers between devices with their start and end apart: 2, of which 0 were waited for; matrix products, arithmetic and copies ran while one was open for 10% of the time, Pallas kernels for 3%

profile of v2, /device:TPU:0, one launch (start us, length us, event | category | flops | bytes accessed | tf_op | source)
XLA Modules:
  0.0 656.4 jit_solution(13417456507709225791)
XLA Ops:
  2.2 112.0 %gather_weights.1 = bf16[2,16,3072,128]{3,2,1,0:T(8,128)(2,1)} custom-call(bf16[3072,128]{1,0:T(8,128)(2,1)S(1)} %bitcast.195), custom_call_target="tpu_custom_call" | custom-call | bytes 50331648 | tf_op jit(solution)/shard_map/gather_weights/pallas_call | solution.py:660
  114.2 8.1 %slice.296 = bf16[2,96,128,128]{3,2,1,0:T(8,128)(2,1)} slice(bf16[2,384,128,128]{3,2,1,0:T(8,128)(2,1)} %bitcast.200), slice={[0:2], [0:96], [0:128], [0:128]} | slice | bytes 12582912 | tf_op jit(solution)/shard_map/slice | solution.py:1233
  122.3 2.1 constant_dynamic-slice_fusion
  124.5 3.1 copy.45
  127.5 5.6 fusion.7
  134.7 2.4 fusion.60
  137.0 4.3 fusion.61
  141.3 10.2 %fusion.59 = (bf16[1,72,128,128]{3,2,1,0:T(8,128)(2,1)}, bf16[1,72,128,128]{3,2,1,0:T(8,128)(2,1)}, bf16[1,72,128,128]{3,2,1,0:T(8,128)(2,1)}, bf16[1,72,128,128...) fusion(bf16[2,384,128,128]{3,2,1,0:T(8,128)(2,1)} %bitcast.203), kind=kLoop, calls=%fused_computation.143 | loop fusion | bytes 28311552 | tf_op jit(solution)/shard_map/slice | solution.py:1231
  162.8 3.0 copy.46
  165.8 4.4 copy.47
  178.1 3.2 copy.44
  181.3 3.2 copy.43
  184.5 3.3 copy.51
  189.5 2.5 bitcast_dynamic-update-slice_fusion.3
  192.0 3.5 bitcast_dynamic-update-slice_fusion.6
  201.6 2.3 copy-done.57
  204.6 3.1 copy-done.1
  207.7 3.4 fusion.65
  213.6 2.0 fusion.6.qkv_q.qkv_k.qkv_v
  215.7 9.2 %attention_forward.1 = (bf16[512,768]{1,0:T(8,128)(2,1)S(1)}, f32[6,2,512]{2,1,0:T(2,128)S(1)}) custom-call(bf16[512,2304]{1,0:T(8,128)(2,1)S(1)} %fusion.6.qkv_q.qkv_k.qkv_v, bf16[512,2304]{1,0:T(8,128)(2,1)S(1)} %fusion.6.qkv_q.qkv_k.qkv_v, bf16[512,2304]{1,0:T(8,128)(2,1)S(1)} %fusion.6.qkv_q.qkv_k.qkv_v), custom_call_target="tpu_custom_call" | custom-call | flops 805306368 | bytes 3145728 | tf_op jit(solution)/shard_map/attention_forward/pallas_call | solution.py:163
  227.0 5.5 multiply_convert_fusion
  232.6 2.6 add_convert_fusion
  235.6 2.7 fusion.67.up_ref
  238.3 4.3 decoder_forward.1
  246.9 16.9 %gather_sums.1 = f32[2,16,16,128]{3,2,1,0:T(8,128)S(1)} custom-call(f32[16,128]{1,0:T(8,128)S(1)} %get-tuple-element.26.in_ref), custom_call_target="tpu_custom_call" | custom-call | bytes 262144 | tf_op jit(solution)/shard_map/gather_sums/pallas_call | solution.py:660
  272.0 2.2 decoder_backward.1
  275.1 5.1 fusion.68
  282.4 4.7 convert_reduce_fusion
  287.2 3.0 multiply_reduce_fusion.3
  293.9 12.7 %attention_backward.1 = (bf16[512,768]{1,0:T(8,128)(2,1)S(1)}, bf16[512,768]{1,0:T(8,128)(2,1)S(1)}, bf16[512,768]{1,0:T(8,128)(2,1)S(1)}) custom-call(bf16[512,2304]{1,0:T(8,128)(2,1)S(1)} %fusion.6.qkv_q.qkv_k.qkv_v, bf16[512,2304]{1,0:T(8,128)(2,1)S(1)} %fusion.6.qkv_q.qkv_k.qkv_v, bf16[512,2304]{1,0:T(8,128)(2,1)S(1)} %fusion.6.qkv_q.qkv_k.qkv_v, ...), custom_call_target="tpu_custom_call" | custom-call | flops 2013265920 | bytes 5505024 | tf_op jit(solution)/shard_map/attention_backward/pallas_call | solution.py:187
  307.6 6.4 grad_deconv.1.refs_2_
  322.0 4.5 multiply_reduce_fusion.4
  328.6 2.4 reshape.278
  331.1 18.7 %concatenate.59 = f32[458110]{0:T(1024)} concatenate(f32[393216]{0:T(1024)} %reshape.278, f32[5376]{0:T(1024)S(1)} %reshape.279, f32[3072]{0:T(1024)S(1)} %get-tuple-element.123, f32[768]{0:T(1024)S(1)} %get-tuple-element.108, f32[128]{0:T(128)S(1)} %slice_reduce_fusion.1, f32[55296]{0:T(1024)S(1)} %reshape.281, f32[16]{0:T(128)S(1)} %slice_reduce_fusion.4, f32[224]{0:T(256)S(1)} %reshape.282, ...), dimensions={0} | concatenate | bytes 3664880 | tf_op jit(solution)/shard_map/concatenate | solution.py:1384
  352.5 7.0 %grad_down.1.refs_2_ = f32[2,12,3264,128]{3,2,1,0:T(8,128)} custom-call(bf16[512,3072]{1,0:T(8,128)(2,1)S(1)} %copy-done.12, bf16[512,768]{1,0:T(8,128)(2,1)S(1)} %copy-done.8, f32[2,12,3264,128]{3,2,1,0:T(8,128)} %grad_deconv.1.refs_2_), custom_call_target="tpu_custom_call", output_to_operand_aliasing={{}: (2, {})} | custom-call | flops 2415919104 | bytes 9437184 | tf_op jit(solution)/shard_map/grad_down/pallas_call | solution.py:1101
  359.6 6.0 grad_up.1.refs_2_
  365.6 2.3 grad_proj.1.refs_2_
  368.0 5.1 grad_qkv.1
  376.2 6.2 grad_embed.1
  382.4 2.7 copy-done
  385.1 211.0 %reduce_to_owners.1 = f32[3264,128]{1,0:T(8,128)} custom-call(f32[2,3,2,2,3264,128]{5,4,3,2,1,0:T(8,128)} %bitcast.199, f32[2,2,3072,128]{3,2,1,0:T(8,128)} %bitcast.194), custom_call_target="tpu_custom_call" | custom-call | bytes 104857600 | tf_op jit(solution)/shard_map/reduce_to_owners/pallas_call | solution.py:995
  596.1 2.4 multiply_reduce_fusion.2
  600.1 20.8 %gather_aux.1 = f32[2,16,200,128]{3,2,1,0:T(8,128)S(1)} custom-call(f32[200,128]{1,0:T(8,128)S(1)} %concatenate.62.in_ref), custom_call_target="tpu_custom_call" | custom-call | bytes 3276800 | tf_op jit(solution)/shard_map/gather_aux/pallas_call | solution.py:660
  626.5 2.5 multiply_reduce_fusion
  632.3 3.4 fusion.26
  635.7 2.8 fusion.25
  644.3 2.2 fusion.22
  651.8 3.3 multiply_subtract_fusion
  (337 shorter events, 90.3 us)
Async XLA Ops:
  127.5 6.2 copy-start.39
  133.2 71.4 %collective-permute-start = (f32[512,768]{1,0:T(8,128)}, f32[512,768]{1,0:T(8,128)}, u32[]{:S(2)}, u32[]{:S(2)}) collective-permute-start(f32[512,768]{1,0:T(8,128)} %fusion.7), channel_id=1, source_target_pairs={{0,1},{1,0},{2,3},{3,2},{4,5},{5,4},{6,7},{7,6},{8,9},{9,8},{10,11... | collective-permute-start | bytes 4718600 | tf_op jit(solution)/shard_map/ppermute | solution.py:1145
  133.8 93.2 %copy-start.93 = (f32[3072]{0:T(1024)}, f32[3072]{0:T(1024)S(1)}, u32[]{:S(2)}) copy-start(f32[3072]{0:T(1024)S(1)} %slice.252) | copy-start | bytes 36868
  134.5 77.0 %copy-start.82 = (f32[768]{0:T(1024)}, f32[768]{0:T(1024)S(1)}, u32[]{:S(2)}) copy-start(f32[768]{0:T(1024)S(1)} %get-tuple-element.104) | copy-start | bytes 9220
  134.5 91.8 %copy-start.80 = (f32[768]{0:T(1024)}, f32[768]{0:T(1024)S(1)}, u32[]{:S(2)}) copy-start(f32[768]{0:T(1024)S(1)} %get-tuple-element.101) | copy-start | bytes 9220
  154.2 4.5 slice-start
  192.0 5.4 copy-start.74
  198.2 6.4 copy-start.72
  198.8 28.2 %copy-start.75 = (bf16[768,3072]{1,0:T(8,128)(2,1)}, bf16[768,3072]{1,0:T(8,128)(2,1)S(1)}, u32[]{:S(2)}) copy-start(bf16[768,3072]{1,0:T(8,128)(2,1)S(1)} %bitcast_dynamic-update-slice_fusion.2) | copy-start | bytes 14155780
  199.4 5.2 copy-start.64
  199.5 25.5 %copy-start.78 = (bf16[768,768]{1,0:T(8,128)(2,1)}, bf16[768,768]{1,0:T(8,128)(2,1)S(1)}, u32[]{:S(2)}) copy-start(bf16[768,768]{1,0:T(8,128)(2,1)S(1)} %bitcast_dynamic-update-slice_fusion.8) | copy-start | bytes 3538948
  204.6 31.0 %copy-start.73 = (bf16[2304,1024]{1,0:T(8,128)(2,1)}, bf16[2304,1024]{1,0:T(8,128)(2,1)S(1)}, u32[]{:S(2)}) copy-start(bf16[2304,1024]{1,0:T(8,128)(2,1)S(1)} %bitcast_dynamic-update-slice_fusion.4) | copy-start | bytes 14155780
  211.0 13.9 %copy-start.44 = (f32[512,768]{1,0:T(8,128)}, f32[512,768]{1,0:T(8,128)S(1)}, u32[]{:S(2)}) copy-start(f32[512,768]{1,0:T(8,128)S(1)} %get-tuple-element.116) | copy-start | bytes 4718596
  215.7 9.3 %copy-start.96 = (f32[768]{0:T(1024)S(1)}, f32[768]{0:T(1024)}, u32[]{:S(2)}) copy-start(f32[768]{0:T(1024)} %get-tuple-element.102) | copy-start | bytes 9220
  225.9 6.7 %copy-start.46 = (f32[512,768]{1,0:T(8,128)}, f32[512,768]{1,0:T(8,128)S(1)}, u32[]{:S(2)}) copy-start(f32[512,768]{1,0:T(8,128)S(1)} %get-tuple-element.118) | copy-start | bytes 4718596
  226.3 6.3 slice-start.1
  226.9 5.6 copy-start.5
  227.0 5.6 slice-start.2
  227.0 5.6 copy-start.95
  238.3 4.3 copy-start.37
  272.0 9.8 %slice-start.3 = ((s8[4718592]{0:T(1024)(128)(4,1)}), s8[524288]{0:T(1024)(128)(4,1)S(1)}, s32[]{:S(2)}) async-start(s8[4718592]{0:T(1024)(128)(4,1)} %bitcast.241), calls=%async_computation.3 | async-start | bytes 1048576
  272.0 9.8 %slice-start.7 = ((s8[6291456]{0:T(1024)(128)(4,1)}), s8[4194304]{0:T(1024)(128)(4,1)S(1)}, s32[]{:S(2)}) async-start(s8[6291456]{0:T(1024)(128)(4,1)} %bitcast.246), calls=%async_computation.7 | async-start | bytes 8388608
  275.1 6.7 %slice-start.4 = ((s8[4718592]{0:T(1024)(128)(4,1)}), s8[4194304]{0:T(1024)(128)(4,1)S(1)}, s32[]{:S(2)}) async-start(s8[4718592]{0:T(1024)(128)(4,1)} %bitcast.241), calls=%async_computation.4 | async-start | bytes 8388608
  275.1 6.7 %slice-start.8 = ((s8[6291456]{0:T(1024)(128)(4,1)}), s8[2097152]{0:T(1024)(128)(4,1)S(1)}, s32[]{:S(2)}) async-start(s8[6291456]{0:T(1024)(128)(4,1)} %bitcast.246), calls=%async_computation.8 | async-start | bytes 4194304
  281.7 5.4 slice-start.5
  281.8 5.3 copy-start.7
  282.4 4.7 copy-start.47
  282.4 4.7 slice-start.6
  282.4 4.8 copy-start.81
  282.4 4.8 copy-start.87
  282.4 4.8 copy-start.91
  293.9 13.7 %copy-start.4 = (bf16[512,2304]{1,0:T(8,128)(2,1)S(1)}, bf16[512,2304]{1,0:T(8,128)(2,1)}, u32[]{:S(2)}) copy-start(bf16[512,2304]{1,0:T(8,128)(2,1)} %copy-done.3) | copy-start | bytes 7077892
  306.6 7.4 %copy-start.15 = (bf16[512,768]{1,0:T(8,128)(2,1)}, bf16[512,768]{1,0:T(8,128)(2,1)S(1)}, u32[]{:S(2)}) copy-start(bf16[512,768]{1,0:T(8,128)(2,1)S(1)} %get-tuple-element.37) | copy-start | bytes 2359300
  306.7 7.4 %copy-start.25 = (bf16[512,768]{1,0:T(8,128)(2,1)}, bf16[512,768]{1,0:T(8,128)(2,1)S(1)}, u32[]{:S(2)}) copy-start(bf16[512,768]{1,0:T(8,128)(2,1)S(1)} %get-tuple-element.36) | copy-start | bytes 2359300
  317.4 4.6 copy-start.83
  317.4 4.6 copy-start.85
  317.4 4.6 copy-start.89
  322.0 4.6 copy-start.43
  322.0 4.6 copy-start.61
  322.0 4.6 copy-start.62
  351.6 7.9 %copy-start.6 = (bf16[512,768]{1,0:T(8,128)(2,1)S(1)}, bf16[512,768]{1,0:T(8,128)(2,1)}, u32[]{:S(2)}) copy-start(bf16[512,768]{1,0:T(8,128)(2,1)} %copy-done.5) | copy-start | bytes 2359300
  351.6 23.1 %collective-permute-start.1 = (bf16[512,768]{1,0:T(8,128)(2,1)}, bf16[512,768]{1,0:T(8,128)(2,1)S(1)}, u32[]{:S(2)}, u32[]{:S(2)}) collective-permute-start(bf16[512,768]{1,0:T(8,128)(2,1)} %get-tuple-element.79), channel_id=1, source_target_pairs={{0,1},{1,0},{2,3},{3,2},{4,5},{5,4},{6,7},{7,6},{8,9},{9,8},{10,11... | collective-permute-start | bytes 2359304 | tf_op jit(solution)/shard_map/ppermute | solution.py:1145
  352.5 7.0 %copy-start.14 = (bf16[512,3072]{1,0:T(8,128)(2,1)S(1)}, bf16[512,3072]{1,0:T(8,128)(2,1)}, u32[]{:S(2)}) copy-start(bf16[512,3072]{1,0:T(8,128)(2,1)} %copy-done.13) | copy-start | bytes 9437188
  359.6 6.1 copy-start.10
  359.6 6.1 copy-start.24
  368.0 6.8 %copy-start.66 = (bf16[512,768]{1,0:T(8,128)(2,1)S(1)}, bf16[512,768]{1,0:T(8,128)(2,1)}, u32[]{:S(2)}) copy-start(bf16[512,768]{1,0:T(8,128)(2,1)} %get-tuple-element.79) | copy-start | bytes 2359300
  624.9 5.5 copy-start.41
  646.5 4.1 copy-start.71
  (63 other events, 126.3 us)

commit v3 on v2

--- a/solution.py
+++ b/solution.py
@@ -94,32 +94,6 @@
         pieces[section_name] = vector[offset : offset + length].reshape(section_shape)
         offset += length
     return pieces
-
-
-LOCAL_SHAPES = [
-    (PV // MP, D),
-    (D, 3 * HALF),
-    (HALF, D),
-    (D, FF // MP),
-    (FF // MP, D),
-    (3 * HALF, 8 * DEC),
-]
-
-
-def from_blocks(piece, height, breadth):
-    return (
-        piece.reshape(height // BS, breadth // BS, BS, BS)
-        .transpose(0, 2, 1, 3)
-        .reshape(height, breadth)
-    )
-
-
-def to_blocks(matrix):
-    return (
-        matrix.reshape(matrix.shape[0] // BS, BS, matrix.shape[1] // BS, BS)
-        .transpose(0, 2, 1, 3)
-        .reshape(-1, BS, BS)
-    )
 
 
 def attention_forward_kernel(qkv_q, qkv_k, qkv_v, mixed_ref, lse_ref):
@@ -439,16 +413,17 @@
 
 
 LAYERS = 4
-PIECES = 24
-ROWS_A = 272
-ROWS_B = 136
-ROWS_N = ROWS_A + ROWS_B
-ROWS_E = 128
-CHUNK = 8 * ROWS_N
-AUX_ROWS = CHUNK - 24 * BS
+GATHER_LAG = 2
+PIECES = 32
+BLOCK_ROWS = 24 * BS
+AUX_ROWS = 256
+CHUNK = BLOCK_ROWS + AUX_ROWS
+ROWS_N = 2 * CHUNK // PIECES
+ROWS_F = BLOCK_ROWS // PIECES
 LAG = 2
-HOP_LAG = 1
-CORE_SLOTS = 6
+HOP_LAG = 2
+AHEAD = 3
+CORE_SLOTS = 8
 SEND_SLOTS = 4
 KEEP = 8
 SUM_SLOTS = 12
@@ -499,51 +474,47 @@
     pl.semaphore_wait(barrier, peers)
 
 
-def gather_kernel(rows, rows_a, skip, in_ref, out_ref, local_sem, up_sem, down_sem, z_recv, x_send, x_recv, y_send, y_recv, core_send, core_recv):
+def gather_kernel(rows, parts, skip, in_ref, out_ref, local_sem, up_sem, down_sem, z_recv, x_send, x_recv, y_send, y_recv, core_send, core_recv):
     at = places()
     x, y, z, c = at["x"], at["y"], at["z"], at["c"]
     last = LAYERS - 1
-    every, a, b = pl.ds(0, rows), pl.ds(0, rows_a), pl.ds(rows_a, rows - rows_a)
-
-    def spot(l, y_at, c_at, x_at, part):
-        return out_ref.at[x_at, l * 4 + y_at * 2 + c_at, part]
+    size = rows // parts
+    by_x = -(-parts // 3)
+
+    def spot(l, y_at, c_at, x_at, p):
+        return out_ref.at[x_at, l * 4 + y_at * 2 + c_at, pl.ds(p * size, size)]
 
     def send(ref, send_sem, recv_sem, device):
         return remote(ref, ref, send_sem, recv_sem, device)
 
-    def up(l):
-        return send(spot(l, y, c, x, every), up_sem.at[l], z_recv.at[l], at["above"])
-
-    def down(l):
-        return send(spot(l, y, c, x, every), down_sem.at[l], z_recv.at[l], at["below"])
-
-    def x_a(l, x_at):
-        return send(spot(l, y, c, x_at, a), x_send.at[l, 0], x_recv.at[l, 0], at["at_x"])
-
-    def x_b(l, x_at):
-        return send(spot(l, y, c, x_at, b), x_send.at[l, 1], x_recv.at[l, 1], at["at_x"])
-
-    def x_relay(l, x_at):
-        return send(spot(l, 1 - y, c, x_at, b), x_send.at[l, 2], x_recv.at[l, 2], at["at_x"])
-
-    def y_a(l, y_at):
-        return send(spot(l, y_at, c, x, a), y_send.at[l, 0], y_recv.at[l, 0], at["at_y"])
-
-    def y_b(l, y_at):
-        return send(spot(l, y_at, c, x, b), y_send.at[l, 1], y_recv.at[l, 1], at["at_y"])
-
-    def y_relay(l, y_at):
-        return send(spot(l, y_at, c, 1 - x, a), y_send.at[l, 2], y_recv.at[l, 2], at["at_y"])
-
-    def core(l, kind, c_at):
-        spots = (
-            spot(l, y, c_at, x, every),
-            spot(l, 1 - y, c_at, x, every),
-            spot(l, y, c_at, 1 - x, every),
-            spot(l, 1 - y, c_at, 1 - x, a),
-            spot(l, 1 - y, c_at, 1 - x, b),
+    def up(l, p):
+        return send(spot(l, y, c, x, p), up_sem.at[l, p], z_recv.at[l, p], at["above"])
+
+    def down(l, p):
+        return send(spot(l, y, c, x, p), down_sem.at[l, p], z_recv.at[l, p], at["below"])
+
+    def x_direct(l, p, x_at):
+        return send(spot(l, y, c, x_at, p), x_send.at[l, p, 0], x_recv.at[l, p, 0], at["at_x"])
+
+    def y_direct(l, p, y_at):
+        return send(spot(l, y_at, c, x, p), y_send.at[l, p, 0], y_recv.at[l, p, 0], at["at_y"])
+
+    def diagonal(l, p, y_at, x_at):
+        if p < by_x:
+            return send(spot(l, y_at, c, x_at, p), y_send.at[l, p, 1], y_recv.at[l, p, 1], at["at_y"])
+        return send(spot(l, y_at, c, x_at, p), x_send.at[l, p, 1], x_recv.at[l, p, 1], at["at_x"])
+
+    def relayed(l, p):
+        return diagonal(l, p, y, 1 - x) if p < by_x else diagonal(l, p, 1 - y, x)
+
+    def core(l, p, kind, c_at):
+        y_at, x_at = ((y, x), (1 - y, x), (y, 1 - x), (1 - y, 1 - x))[kind]
+        return send(
+            spot(l, y_at, c_at, x_at, p),
+            core_send.at[l, p, kind],
+            core_recv.at[l, p, kind],
+            at["at_core"],
         )
-        return send(spots[kind], core_send.at[l, kind], core_recv.at[l, kind], at["at_core"])
 
     def wide(l):
         return (l > 0) if skip else (l >= 0)
@@ -553,126 +524,119 @@
     greet_neighbours(at)
     own.wait()
 
-    def arrive(l, came_up, came_down):
+    def arrive(l, p, came_up, came_down):
         if not (came_up and came_down):
-            up(l).wait_recv()
+            up(l, p).wait_recv()
         if came_up:
 
             @pl.when(z < last)
             def _():
-                up(l).start()
+                up(l, p).start()
 
         if came_down:
 
             @pl.when(z > 0)
             def _():
-                down(l).start()
-
-        y_b(l, y).start()
+                down(l, p).start()
 
         @pl.when(wide(l))
         def _():
-            x_a(l, x).start()
-            x_b(l, x).start()
-
-        y_a(l, y).start()
-        core(l, 0, c).start()
-
-    def relay(l):
-        y_b(l, 1 - y).wait_recv()
+            x_direct(l, p, x).start()
+
+        y_direct(l, p, y).start()
+        core(l, p, 0, c).start()
+
+    def relay(l, p):
+        y_direct(l, p, 1 - y).wait_recv()
 
         @pl.when(wide(l))
         def _():
-            x_relay(l, x).start()
-            x_a(l, 1 - x).wait_recv()
-            y_relay(l, y).start()
-
-        y_a(l, 1 - y).wait_recv()
-        core(l, 1, c).start()
-
+            if p >= by_x:
+                relayed(l, p).start()
+            x_direct(l, p, 1 - x).wait_recv()
+            if p < by_x:
+                relayed(l, p).start()
+            core(l, p, 2, c).start()
+
+        core(l, p, 1, c).start()
+
+    def finish(l, p):
         @pl.when(wide(l))
         def _():
-            x_b(l, 1 - x).wait_recv()
-            core(l, 2, c).start()
-
-    def finish(l):
-        @pl.when(wide(l))
-        def _():
-            y_relay(l, 1 - y).wait_recv()
-            core(l, 3, c).start()
-            x_relay(l, 1 - x).wait_recv()
-            core(l, 4, c).start()
-
-    def both(r, run):
-        if r < 0 or r >= LAYERS:
+            diagonal(l, p, 1 - y, 1 - x).wait_recv()
+            core(l, p, 3, c).start()
+
+    def both(tick, run):
+        if tick < 0 or tick >= LAYERS * parts:
             return
+        r, p = tick // parts, tick % parts
         if r == 0:
-            run(z, True, True)
+            run(z, p, True, True)
             return
 
         @pl.when(z - r >= 0)
         def _():
-            run(z - r, True, False)
+            run(z - r, p, True, False)
 
         @pl.when(z + r <= last)
         def _():
-            run(z + r, False, True)
-
-    for r in range(LAYERS + 2):
-        both(r, arrive)
-        both(r - 1, lambda l, up_way, down_way: relay(l))
-        both(r - 2, lambda l, up_way, down_way: finish(l))
+            run(z + r, p, False, True)
+
+    for tick in range(LAYERS * parts + 2 * GATHER_LAG):
+        both(tick, arrive)
+        both(tick - GATHER_LAG, lambda l, p, up_way, down_way: relay(l, p))
+        both(tick - 2 * GATHER_LAG, lambda l, p, up_way, down_way: finish(l, p))
 
     def settle(l, carry):
-        for kind in (0, 1):
-            core(l, kind, 1 - c).wait_recv()
-            core(l, kind, c).wait_send()
-        y_a(l, y).wait_send()
-        y_b(l, y).wait_send()
-
-        @pl.when(wide(l))
-        def _():
-            for kind in (2, 3, 4):
-                core(l, kind, 1 - c).wait_recv()
-                core(l, kind, c).wait_send()
-            for copy in (x_a(l, x), x_b(l, x), x_relay(l, x), y_relay(l, y)):
-                copy.wait_send()
-
-        @pl.when((l <= z) & (z < last))
-        def _():
-            up(l).wait_send()
-
-        @pl.when((l >= z) & (z > 0))
-        def _():
-            down(l).wait_send()
+        for p in range(parts):
+            for kind in (0, 1):
+                core(l, p, kind, 1 - c).wait_recv()
+                core(l, p, kind, c).wait_send()
+            y_direct(l, p, y).wait_send()
+
+            @pl.when(wide(l))
+            def _(p=p):
+                for kind in (2, 3):
+                    core(l, p, kind, 1 - c).wait_recv()
+                    core(l, p, kind, c).wait_send()
+                x_direct(l, p, x).wait_send()
+                relayed(l, p).wait_send()
+
+            @pl.when((l <= z) & (z < last))
+            def _(p=p):
+                up(l, p).wait_send()
+
+            @pl.when((l >= z) & (z > 0))
+            def _(p=p):
+                down(l, p).wait_send()
 
         return carry
 
     lax.fori_loop(0, LAYERS, settle, 0)
 
 
-def gather_all(values, rows_a, skip, collective_id, name, memory=pl.ANY):
+def gather_all(values, parts, skip, collective_id, name):
     rows = values.shape[0]
 
     def sems(*shape):
         return pltpu.SemaphoreType.DMA(shape)
 
     return pl.pallas_call(
-        functools.partial(gather_kernel, rows, rows_a, skip),
+        functools.partial(gather_kernel, rows, parts, skip),
         out_shape=jax.ShapeDtypeStruct((MP, 4 * LAYERS, rows, BS), values.dtype),
-        in_specs=[pl.BlockSpec(memory_space=memory)],
-        out_specs=pl.BlockSpec(memory_space=memory),
+        in_specs=[pl.BlockSpec(memory_space=pl.ANY)],
+        out_specs=pl.BlockSpec(memory_space=pl.ANY),
         scratch_shapes=[
             pltpu.SemaphoreType.DMA,
-            sems(LAYERS),
-            sems(LAYERS),
-            sems(LAYERS),
-            sems(LAYERS, 3),
-            sems(LAYERS, 3),
-            sems(LAYERS, 3),
-            sems(LAYERS, 3),
-            sems(LAYERS, 5),
-            sems(LAYERS, 5),
+            sems(LAYERS, parts),
+            sems(LAYERS, parts),
+            sems(LAYERS, parts),
+            sems(LAYERS, parts, 2),
+            sems(LAYERS, parts, 2),
+            sems(LAYERS, parts, 2),
+            sems(LAYERS, parts, 2),
+            sems(LAYERS, parts, 4),
+            sems(LAYERS, parts, 4),
         ],
         compiler_params=pltpu.CompilerParams(
             collective_id=collective_id, has_side_effects=True, vmem_limit_bytes=32 * MIB
@@ -685,104 +649,90 @@
 def reduce_kernel(
     n_ref,
     e_ref,
+    f_ref,
     out_ref,
+    square_ref,
     own_n,
-    own_e,
+    own_f,
     core_n,
-    core_e,
-    keep_own,
-    keep_a,
-    keep_b,
-    keep_e,
-    xs_a,
-    xs_b,
-    ys_b,
-    ys_a,
-    ys_e,
-    xr_a,
-    xr_b,
-    yr_b,
-    yr_a,
-    yr_e,
+    core_f,
+    keep_n,
+    keep_f,
+    xs_n,
+    ys_n,
+    ys_f,
+    xr_n,
+    yr_n,
+    yr_f,
     sum_n,
-    sum_e,
+    sum_f,
     up_n,
     down_n,
+    up_f,
     down_e,
     own_sem,
     core_send,
     core_recv,
     credit,
-    xs_a_sem,
-    xs_b_sem,
-    ys_b_sem,
-    ys_a_sem,
-    ys_e_sem,
-    xr_a_sem,
-    xr_b_sem,
-    yr_b_sem,
-    yr_a_sem,
-    yr_e_sem,
+    xs_sem,
+    ys_n_sem,
+    ys_f_sem,
+    xr_sem,
+    yr_n_sem,
+    yr_f_sem,
     z_n_sem,
-    z_e_sem,
+    z_f_sem,
     up_n_sem,
     down_n_sem,
+    up_f_sem,
     down_e_sem,
 ):
     at = places()
     x, y, z, c = at["x"], at["y"], at["z"], at["c"]
+    last = LAYERS - 1
 
     def layer_of(s):
-        return LAYERS - 1 - lax.rem(s, 3)
+        return 1 + lax.rem(s, 2)
 
     def rows_of(s):
-        return pl.ds(pl.multiple_of((s // 3) * ROWS_N, 8), ROWS_N)
-
-    def rows_e(s):
-        return pl.ds(pl.multiple_of(s * ROWS_E, 8), ROWS_E)
+        return pl.ds(pl.multiple_of((s // 2) * ROWS_N, 8), ROWS_N)
+
+    def rows_f(s):
+        return pl.ds(pl.multiple_of(s * ROWS_F, 8), ROWS_F)
 
     def own_loads(s):
         slot = lax.rem(s, 3)
+        mine = n_ref.at[:, layer_of(s) - 1, :, c, rows_of(s)]
         return (
-            pltpu.make_async_copy(
-                n_ref.at[:, layer_of(s) - 1, :, c, rows_of(s)], own_n.at[slot], own_sem.at[slot, 0]
-            ),
-            pltpu.make_async_copy(e_ref.at[:, c, rows_e(s)], own_e.at[slot], own_sem.at[slot, 1]),
+            pltpu.make_async_copy(mine, own_n.at[slot], own_sem.at[slot, 0]),
+            pltpu.make_async_copy(e_ref.at[:, c, rows_f(s)], own_f.at[slot, 0], own_sem.at[slot, 1]),
+            pltpu.make_async_copy(f_ref.at[:, c, rows_f(s)], own_f.at[slot, 1], own_sem.at[slot, 2]),
         )
 
     def core_copies(s):
         slot = lax.rem(s, CORE_SLOTS)
-        return (
-            remote(
-                n_ref.at[:, layer_of(s) - 1, :, 1 - c, rows_of(s)],
-                core_n.at[slot],
-                core_send.at[s, 0],
-                core_recv.at[slot, 0],
-                at["at_core"],
-            ),
-            remote(
-                e_ref.at[:, 1 - c, rows_e(s)],
-                core_e.at[slot],
-                core_send.at[s, 1],
-                core_recv.at[slot, 1],
-                at["at_core"],
-            ),
+        sources = (
+            n_ref.at[:, layer_of(s) - 1, :, 1 - c, rows_of(s)],
+            e_ref.at[:, 1 - c, rows_f(s)],
+            f_ref.at[:, 1 - c, rows_f(s)],
         )
-
-    def first_copies(s):
+        targets = (core_n.at[slot], core_f.at[slot, 0], core_f.at[slot, 1])
+        return [
+            remote(source, target, core_send.at[s, i], core_recv.at[slot, i], at["at_core"])
+            for i, (source, target) in enumerate(zip(sources, targets))
+        ]
+
+    def x_copy(s):
         slot = lax.rem(s, SEND_SLOTS)
-        return (
-            remote(xs_a.at[slot], xr_a.at[s], xs_a_sem.at[slot], xr_a_sem.at[s], at["at_x"]),
-            remote(ys_b.at[slot], yr_b.at[s], ys_b_sem.at[slot], yr_b_sem.at[s], at["at_y"]),
-            remote(ys_e.at[slot], yr_e.at[s], ys_e_sem.at[slot], yr_e_sem.at[s], at["at_y"]),
-        )
-
-    def second_copies(s):
+        return remote(xs_n.at[slot], xr_n.at[s], xs_sem.at[slot], xr_sem.at[s], at["at_x"])
+
+    def y_copy_f(s):
         slot = lax.rem(s, SEND_SLOTS)
-        return (
-            remote(ys_a.at[slot], yr_a.at[s], ys_a_sem.at[slot], yr_a_sem.at[s], at["at_y"]),
-            remote(xs_b.at[slot], xr_b.at[s], xs_b_sem.at[slot], xr_b_sem.at[s], at["at_x"]),
-        )
+        return remote(ys_f.at[slot], yr_f.at[s], ys_f_sem.at[slot], yr_f_sem.at[s], at["at_y"])
+
+    def y_copy(s):
+        slot = lax.rem(s, SEND_SLOTS)
+        return remote(ys_n.at[slot], yr_n.at[s], ys_n_sem.at[slot], yr_n_sem.at[s], at["at_y"])
 
     def up_copy(s):
         slot = lax.rem(s, SUM_SLOTS)
@@ -794,13 +744,23 @@
 
     def down_copy_e(s):
         slot = lax.rem(s, SUM_SLOTS)
-        return remote(sum_e.at[slot], down_e.at[s], z_e_sem.at[slot], down_e_sem.at[s], at["below"])
-
+        source, sem = sum_f.at[slot, 0], z_f_sem.at[slot, 0]
+        return remote(source, down_e.at[s], sem, down_e_sem.at[s], at["below"])
+
+    def up_copy_f(s):
+        slot = lax.rem(s, SUM_SLOTS)
+        source, sem = sum_f.at[slot, 1], z_f_sem.at[slot, 1]
+        return remote(source, up_f.at[s], sem, up_f_sem.at[s], at["above"])
+
+    def add_squares(values):
+        square_ref[...] += jnp.sum((values * values).reshape(-1, 8, BS), 0)
+
+    square_ref[...] = jnp.zeros((8, BS), jnp.float32)
     for s in range(2):
         for copy in own_loads(s):
             copy.start()
     greet_neighbours(at)
-    for s in range(2):
+    for s in range(AHEAD):
         for copy in core_copies(s):
             copy.start()
 
@@ -810,11 +770,13 @@
             for copy in own_loads(s + 2):
                 copy.start()
 
-            @pl.when(s + 2 >= CORE_SLOTS)
+        @pl.when(s + AHEAD < PIECES)
+        def _():
+            @pl.when(s + AHEAD >= CORE_SLOTS)
             def _():
                 pl.semaphore_wait(credit, 1)
 
-            for copy in core_copies(s + 2):
+            for copy in core_copies(s + AHEAD):
                 copy.start()
 
         for copy in own_loads(s):
@@ -824,53 +786,39 @@
 
         @pl.when(s >= SEND_SLOTS)
         def _():
-            for copy in first_copies(s - SEND_SLOTS):
-                copy.wait_send()
+            x_copy(s - SEND_SLOTS).wait_send()
+            y_copy_f(s - SEND_SLOTS).wait_send()
 
         own, core = lax.rem(s, 3), lax.rem(s, CORE_SLOTS)
         send, keep = lax.rem(s, SEND_SLOTS), lax.rem(s, KEEP)
-        a, b = pl.ds(0, ROWS_A), pl.ds(ROWS_A, ROWS_B)
-        for other in range(2):
-            xs_a[send, other] = own_n[own, 1 - x, other, a] + core_n[core, 1 - x, other, a]
-        to_x, to_y, to_y_e = first_copies(s)
-        to_x.start()
-        for other in range(2):
-            ys_b[send, other] = own_n[own, other, 1 - y, b] + core_n[core, other, 1 - y, b]
-        to_y.start()
-        ys_e[send] = own_e[own, 1 - y] + core_e[core, 1 - y]
-        to_y_e.start()
-        keep_own[keep] = own_n[own, x, y] + core_n[core, x, y]
-        keep_a[keep] = own_n[own, x, 1 - y, a] + core_n[core, x, 1 - y, a]
-        keep_b[keep] = own_n[own, 1 - x, y, b] + core_n[core, 1 - x, y, b]
-        keep_e[keep] = own_e[own, y] + core_e[core, y]
+        xs_n[send] = own_n[own, 1 - x] + core_n[core, 1 - x]
+        x_copy(s).start()
+        for kind in range(2):
+            ys_f[send, kind] = own_f[own, kind, 1 - y] + core_f[core, kind, 1 - y]
+        y_copy_f(s).start()
+        keep_n[keep] = own_n[own, x] + core_n[core, x]
+        for kind in range(2):
+            keep_f[keep, kind] = own_f[own, kind, y] + core_f[core, kind, y]
 
         @pl.when(s + CORE_SLOTS < PIECES)
         def _():
             pl.semaphore_signal(credit, inc=1, device_id=at["at_core"], device_id_type=MESH)
 
     def second(s):
-        to_x, to_y, _ = first_copies(s)
-        to_x.wait_recv()
-        to_y.wait_recv()
+        x_copy(s).wait_recv()
 
         @pl.when(s >= SEND_SLOTS)
         def _():
-            for copy in second_copies(s - SEND_SLOTS):
-                copy.wait_send()
+            y_copy(s - SEND_SLOTS).wait_send()
 
         send, keep = lax.rem(s, SEND_SLOTS), lax.rem(s, KEEP)
-        a, b = pl.ds(0, ROWS_A), pl.ds(ROWS_A, ROWS_B)
-        ys_a[send] = keep_a[keep] + xr_a[s, 1 - y]
-        xs_b[send] = keep_b[keep] + yr_b[s, 1 - x]
-        for copy in second_copies(s):
-            copy.start()
-        keep_own[keep, a] = keep_own[keep, a] + xr_a[s, y]
-        keep_own[keep, b] = keep_own[keep, b] + yr_b[s, x]
+        ys_n[send] = keep_n[keep, 1 - y] + xr_n[s, 1 - y]
+        y_copy(s).start()
+        keep_n[keep, y] = keep_n[keep, y] + xr_n[s, y]
 
     def third(s):
-        first_copies(s)[2].wait_recv()
-        for copy in second_copies(s):
-            copy.wait_recv()
+        y_copy_f(s).wait_recv()
+        y_copy(s).wait_recv()
 
         @pl.when((s >= SUM_SLOTS) & (z != layer_of(s)))
         def _():
@@ -880,16 +828,17 @@
         def _():
             down_copy_e(s - SUM_SLOTS).wait_send()
 
+        @pl.when((s >= SUM_SLOTS) & (z < last))
+        def _():
+            up_copy_f(s - SUM_SLOTS).wait_send()
+
         slot, keep = lax.rem(s, SUM_SLOTS), lax.rem(s, KEEP)
-        a, b = pl.ds(0, ROWS_A), pl.ds(ROWS_A, ROWS_B)
-        sum_n[slot, a] = keep_own[keep, a] + yr_a[s]
-        sum_n[slot, b] = keep_own[keep, b] + xr_b[s]
-        sum_e[slot] = keep_e[keep] + yr_e[s]
+        sum_n[slot] = keep_n[keep, y] + yr_n[s]
+        sum_f[slot] = keep_f[keep] + yr_f[s]
 
     def along(s, hop):
         slot = lax.rem(s, SUM_SLOTS)
         layer = layer_of(s)
-        last = LAYERS - 1
         away = jnp.where(z < layer, z, jnp.where(z > layer, last - z, jnp.maximum(z, last - z)))
 
         @pl.when(away == hop)
@@ -915,15 +864,23 @@
             @pl.when(z == layer)
             def _():
                 out_ref[rows_of(s)] = sum_n[slot]
-
-        away_e = jnp.where(z == 0, last, last - z)
-
-        @pl.when(away_e == hop)
+                piece = s // 2
+                whole, cut = BLOCK_ROWS // ROWS_N, BLOCK_ROWS % ROWS_N
+
+                @pl.when(piece <= whole)
+                def _():
+                    add_squares(sum_n[slot, pl.ds(0, cut)])
+
+                @pl.when(piece < whole)
+                def _():
+                    add_squares(sum_n[slot, pl.ds(cut, ROWS_N - cut)])
+
+        @pl.when(jnp.where(z == 0, last, last - z) == hop)
         def _():
             @pl.when(z < last)
             def _():
                 down_copy_e(s).wait_recv()
-                sum_e[slot] = sum_e[slot] + down_e[s]
+                sum_f[slot, 0] = sum_f[slot, 0] + down_e[s]
 
             @pl.when(z > 0)
             def _():
@@ -931,7 +888,24 @@
 
             @pl.when(z == 0)
             def _():
-                out_ref[rows_e(s)] = sum_e[slot]
+                out_ref[rows_f(s)] = sum_f[slot, 0]
+                add_squares(sum_f[slot, 0])
+
+        @pl.when(z == hop)
+        def _():
+            @pl.when(z > 0)
+            def _():
+                up_copy_f(s).wait_recv()
+                sum_f[slot, 1] = sum_f[slot, 1] + up_f[s]
+
+            @pl.when(z < last)
+            def _():
+                up_copy_f(s).start()
+
+            @pl.when(z == last)
+            def _():
+                out_ref[rows_f(s)] = sum_f[slot, 1]
+                add_squares(sum_f[slot, 1])
 
     def guarded(run, s):
         @pl.when((s >= 0) & (s < PIECES))
@@ -950,7 +924,7 @@
 
     def drain_sends(i, carry):
         s = PIECES - SEND_SLOTS + i
-        for copy in first_copies(s) + second_copies(s):
+        for copy in (x_copy(s), y_copy_f(s), y_copy(s)):
             copy.wait_send()
         return carry
 
@@ -966,6 +940,10 @@
         @pl.when(z > 0)
         def _():
             down_copy_e(s).wait_send()
+
+        @pl.when(z < last)
+        def _():
+            up_copy_f(s).wait_send()
 
         return carry
 
@@ -978,14 +956,12 @@
 
     lax.fori_loop(0, PIECES, drain_core, 0)
 
-    @pl.when(z == 0)
+    @pl.when((z == 0) | (z == last))
     def _():
-        out_ref[pl.ds(PIECES * ROWS_E, CHUNK - PIECES * ROWS_E)] = jnp.zeros(
-            (CHUNK - PIECES * ROWS_E, BS), jnp.float32
-        )
-
-
-def reduce_to_owners(rest, embed):
+        out_ref[pl.ds(BLOCK_ROWS, AUX_ROWS)] = jnp.zeros((AUX_ROWS, BS), jnp.float32)
+
+
+def reduce_to_owners(rest, first, final):
     def room(*shape):
         return pltpu.VMEM(shape + (BS,), jnp.float32)
 
@@ -994,49 +970,44 @@
 
     return pl.pallas_call(
         reduce_kernel,
-        out_shape=jax.ShapeDtypeStruct((CHUNK, BS), jnp.float32),
-        in_specs=[pl.BlockSpec(memory_space=pl.ANY)] * 2,
-        out_specs=pl.BlockSpec(memory_space=pltpu.VMEM),
+        out_shape=(
+            jax.ShapeDtypeStruct((CHUNK, BS), jnp.float32),
+            jax.ShapeDtypeStruct((8, BS), jnp.float32),
+        ),
+        in_specs=[pl.BlockSpec(memory_space=pl.ANY)] * 3,
+        out_specs=(pl.BlockSpec(memory_space=pltpu.VMEM),) * 2,
         scratch_shapes=[
             room(3, 2, 2, ROWS_N),
-            room(3, 2, ROWS_E),
+            room(3, 2, 2, ROWS_F),
             room(CORE_SLOTS, 2, 2, ROWS_N),
-            room(CORE_SLOTS, 2, ROWS_E),
-            room(KEEP, ROWS_N),
-            room(KEEP, ROWS_A),
-            room(KEEP, ROWS_B),
-            room(KEEP, ROWS_E),
-            room(SEND_SLOTS, 2, ROWS_A),
-            room(SEND_SLOTS, ROWS_B),
-            room(SEND_SLOTS, 2, ROWS_B),
-            room(SEND_SLOTS, ROWS_A),
-            room(SEND_SLOTS, ROWS_E),
-            room(PIECES, 2, ROWS_A),
-            room(PIECES, ROWS_B),
-            room(PIECES, 2, ROWS_B),
-            room(PIECES, ROWS_A),
-            room(PIECES, ROWS_E),
+            room(CORE_SLOTS, 2, 2, ROWS_F),
+            room(KEEP, 2, ROWS_N),
+            room(KEEP, 2, ROWS_F),
+            room(SEND_SLOTS, 2, ROWS_N),
+            room(SEND_SLOTS, ROWS_N),
+            room(SEND_SLOTS, 2, ROWS_F),
+            room(PIECES, 2, ROWS_N),
+            room(PIECES, ROWS_N),
+            room(PIECES, 2, ROWS_F),
             room(SUM_SLOTS, ROWS_N),
-            room(SUM_SLOTS, ROWS_E),
+            room(SUM_SLOTS, 2, ROWS_F),
             room(PIECES, ROWS_N),
             room(PIECES, ROWS_N),
-            room(PIECES, ROWS_E),
-            sems(3, 2),
-            sems(PIECES, 2),
-            sems(CORE_SLOTS, 2),
+            room(PIECES, ROWS_F),
+            room(PIECES, ROWS_F),
+            sems(3, 3),
+            sems(PIECES, 3),
+            sems(CORE_SLOTS, 3),
             pltpu.SemaphoreType.REGULAR,
-            sems(SEND_SLOTS),
-            sems(SEND_SLOTS),
             sems(SEND_SLOTS),
             sems(SEND_SLOTS),
             sems(SEND_SLOTS),
             sems(PIECES),
             sems(PIECES),
             sems(PIECES),
+            sems(SUM_SLOTS),
+            sems(SUM_SLOTS, 2),
             sems(PIECES),
-            sems(PIECES),
-            sems(SUM_SLOTS),
-            sems(SUM_SLOTS),
             sems(PIECES),
             sems(PIECES),
             sems(PIECES),
@@ -1046,7 +1017,98 @@
         ),
         cost_estimate=pl.CostEstimate(flops=0, bytes_accessed=100 * MIB, transcendentals=0),
         name="reduce_to_owners",
-    )(rest, embed)
+    )(rest, first, final)
+
+
+MATRICES = [
+    (96, 6, 9, 3, True),
+    (150, 3, 6, 3, False),
+    (168, 6, 12, 3, True),
+    (240, 12, 6, 4, False),
+    (312, 9, 8, 3, False),
+]
+LOADS = 4
+
+
+def unblock_kernel(plan, kinds, blocks_ref, *refs):
+    outs, tiles = refs[:kinds], refs[kinds : 2 * kinds]
+    loaded, load_sem, store_sem = refs[2 * kinds :]
+    part = lax.axis_index("mp")
+
+    def load(i):
+        kind, m, first, rows, per_row, row, col = plan[i]
+        number = rows * per_row
+        return pltpu.make_async_copy(
+            blocks_ref.at[part if m is None else m, pl.ds(first, number)],
+            loaded.at[i % LOADS, pl.ds(0, number)],
+            load_sem.at[i % LOADS],
+        )
+
+    def store(i, slot):
+        kind, m, first, rows, per_row, row, col = plan[i]
+        return pltpu.make_async_copy(
+            tiles[kind].at[slot],
+            outs[kind].at[pl.ds(row, rows * BS), pl.ds(col, per_row * BS)],
+            store_sem.at[kind, slot],
+        )
+
+    history = [[] for _ in range(kinds)]
+    for i in range(min(LOADS - 1, len(plan))):
+        load(i).start()
+    for i, (kind, m, first, rows, per_row, row, col) in enumerate(plan):
+        if i + LOADS - 1 < len(plan):
+            load(i + LOADS - 1).start()
+        load(i).wait()
+        slot = len(history[kind]) % 2
+        if len(history[kind]) >= 2:
+            store(*history[kind][-2]).wait()
+        for r in range(rows):
+            for c in range(per_row):
+                tiles[kind][slot, r * BS : (r + 1) * BS, c * BS : (c + 1) * BS] = loaded[
+                    i % LOADS, r * per_row + c
+                ]
+        history[kind].append((i, slot))
+        store(i, slot).start()
+    for done in history:
+        for entry in done[-2:]:
+            store(*entry).wait()
+
+
+def unblock(gathered, embedding):
+    plan, shapes, tiles = [], [], []
+    if embedding:
+        plan = [(0, None, 24 * i, 4, 6, 4 * BS * i, 0) for i in range(4)]
+        shapes, tiles = [(PV // MP, D)], [(4 * BS, D)]
+    else:
+        for kind, (first, rows, per_row, step, beside) in enumerate(MATRICES):
+            tall, wide = rows * BS, per_row * BS
+            shapes.append((tall, MP * wide) if beside else (MP * tall, wide))
+            tiles.append((step * BS, wide))
+            for m in range(MP):
+                for at in range(0, rows, step):
+                    row = at * BS + (0 if beside else m * tall)
+                    plan.append(
+                        (kind, m, first + at * per_row, step, per_row, row, m * wide if beside else 0)
+                    )
+    anywhere = pl.BlockSpec(memory_space=pl.ANY)
+    largest = max(entry[3] * entry[4] for entry in plan)
+    return pl.pallas_call(
+        functools.partial(unblock_kernel, plan, len(shapes)),
+        out_shape=tuple(jax.ShapeDtypeStruct(shape, jnp.bfloat16) for shape in shapes),
+        in_specs=[anywhere],
+        out_specs=tuple([anywhere] * len(shapes)),
+        scratch_shapes=[pltpu.VMEM((2,) + tile, jnp.bfloat16) for tile in tiles]
+        + [
+            pltpu.VMEM((LOADS, largest, BS, BS), jnp.bfloat16),
+            pltpu.SemaphoreType.DMA((LOADS,)),
+            pltpu.SemaphoreType.DMA((len(shapes), 2)),
+        ],
+        compiler_params=pltpu.CompilerParams(vmem_limit_bytes=32 * MIB),
+        cost_estimate=pl.CostEstimate(
+            flops=0, bytes_accessed=(6 if embedding else 38) * MIB, transcendentals=0
+        ),
+        name="unblock_embedding" if embedding else "unblock",
+    )(gathered)
 
 
 def blocks_kernel(first_block, per_row, step_rows, transposed, has_buffer, *refs):
@@ -1085,12 +1147,13 @@
             drain(1 - slot)
 
 
-def grad_blocks(x, g, parts, rows, per_row, step_rows, first_block, split_x, split_g, buffer, name, chunks=12, depth=CHUNK, transposed=False):
+def grad_blocks(x, g, parts, rows, per_row, step_rows, first_block, split_x, split_g, buffer, name, chunks, depth, transposed=False, x_stride=None):
     steps = rows // step_rows
+    x_stride = x_stride or steps
     tokens = x.shape[0]
     width = per_row * BS
     x_spec = pl.BlockSpec(
-        (tokens, step_rows * BS), (lambda m, i: (0, m * steps + i)) if split_x else (lambda m, i: (0, i))
+        (tokens, step_rows * BS), (lambda m, i: (0, m * x_stride + i)) if split_x else (lambda m, i: (0, i))
     )
     if transposed:
         g_spec = pl.BlockSpec((width, tokens), lambda m, i: (0, 0))
@@ -1125,10 +1188,50 @@
     return lax.axis_size("dp") == 4 * LAYERS and lax.axis_size("mp") == MP
 
 
+def sum_kernel(devices, in_ref, out_ref, slots, send_sem, recv_sem):
+    me = lax.axis_index("dp") * MP + lax.axis_index("mp")
+    barrier = pltpu.get_barrier_semaphore()
+
+    def place(k):
+        peer = lax.rem(me + k, devices)
+        return (peer // MP, lax.rem(peer, MP))
+
+    def greet(k, carry):
+        pl.semaphore_signal(barrier, inc=1, device_id=place(k), device_id_type=MESH)
+        return carry
+
+    def copy(k, slot):
+        return remote(in_ref, slots.at[slot], send_sem.at[k], recv_sem.at[slot], place(k))
+
+    lax.fori_loop(1, devices, greet, 0)
+    slots[me] = in_ref[...]
+    pl.semaphore_wait(barrier, devices - 1)
+
+    def push(k, carry):
+        copy(k, me).start()
+        return carry
+
+    def pull(k, carry):
+        copy(k, lax.rem(me + devices - k, devices)).wait_recv()
+        return carry
+
+    def settle(k, carry):
+        copy(k, me).wait_send()
+        return carry
+
+    lax.fori_loop(1, devices, push, 0)
+    lax.fori_loop(1, devices, pull, 0)
+    total = slots[0]
+    for i in range(1, devices):
+        total = total + slots[i]
+    out_ref[...] = total
+    lax.fori_loop(1, devices, settle, 0)
+
+
 def gather_weights(blocks):
     low = blocks.astype(jnp.bfloat16)[0, 0]
     if fast_mesh():
-        gathered = gather_all(low.reshape(-1, BS), 8 * BS, True, 2, "gather_weights")
+        gathered = gather_all(low.reshape(-1, BS), 3, True, 2, "gather_weights")
     else:
         gathered = lax.all_gather(low, ("dp", "mp"), axis=0, tiled=False)
         gathered = gathered.reshape((-1, MP) + low.shape).swapaxes(0, 1)
@@ -1136,21 +1239,36 @@
 
 
 def sum_sums(values):
-    if fast_mesh():
-        return jnp.sum(gather_all(values, 8, False, 3, "gather_sums", pltpu.VMEM), (0, 1))
-    return lax.psum(values, ("dp", "mp"))
+    if not fast_mesh():
+        return lax.psum(values, ("dp", "mp"))
+    devices = 4 * LAYERS * MP
+    whole = pl.BlockSpec(memory_space=pltpu.VMEM)
+    return pl.pallas_call(
+        functools.partial(sum_kernel, devices),
+        out_shape=jax.ShapeDtypeStruct(values.shape, jnp.float32),
+        in_specs=[whole],
+        out_specs=whole,
+        scratch_shapes=[
+            pltpu.VMEM((devices,) + values.shape, jnp.float32),
+            pltpu.SemaphoreType.DMA((devices,)),
+            pltpu.SemaphoreType.DMA((devices,)),
+        ],
+        compiler_params=pltpu.CompilerParams(collective_id=3, has_side_effects=True),
+        name="sum_sums",
+    )(values)
 
 
 def swap_mp(values):
     return lax.ppermute(values, "mp", [(0, 1), (1, 0)])
 
 
-def reduce_plain(rest, embed):
+def reduce_plain(rest, first, final):
     part = lax.axis_index("mp")
     own = (jnp.arange(MP) == part).astype(jnp.float32)
-    first = embed.reshape(1, -1, BS, BS) * own[:, None, None, None]
+    ends = [piece.reshape(1, -1, BS, BS) * own[:, None, None, None] for piece in (first, final)]
     dp = lax.axis_size("dp")
-    every = jnp.concatenate([first, rest], 1).reshape(MP, dp, -1, BS, BS).transpose(1, 0, 2, 3, 4)
+    every = jnp.concatenate([ends[0], rest, ends[1]], 1)
+    every = every.reshape(MP, dp, -1, BS, BS).transpose(1, 0, 2, 3, 4)
     return lax.psum_scatter(
         every.reshape(dp * MP, -1, BS, BS), ("dp", "mp"), scatter_dimension=0, tiled=True
     )[0]
@@ -1223,20 +1341,8 @@
     gain, shift = pieces["norm_gain"], pieces["norm_bias"]
 
     gathered = gather_weights(blocks)
-    starts = [0]
-    for height, breadth in LOCAL_SHAPES:
-        starts.append(starts[-1] + height * breadth // (BS * BS))
-
-    def matrix_of(which, m):
-        return from_blocks(gathered[m, starts[which] : starts[which + 1]], *LOCAL_SHAPES[which])
-
-    own_embed = lax.dynamic_index_in_dim(gathered[:, :E_BLOCKS], part, 0, False)
-    w_embed = from_blocks(own_embed, *LOCAL_SHAPES[0])
-    w_qkv = jnp.concatenate([matrix_of(1, m) for m in range(MP)], 1)
-    w_proj = jnp.concatenate([matrix_of(2, m) for m in range(MP)], 0)
-    w_up = jnp.concatenate([matrix_of(3, m) for m in range(MP)], 1)
-    w_down = jnp.concatenate([matrix_of(4, m) for m in range(MP)], 0)
-    w_deconv = jnp.concatenate([matrix_of(5, m) for m in range(MP)], 0)
+    (w_embed,) = unblock(gathered, True)
+    w_qkv, w_proj, w_up, w_down, w_deconv = unblock(gathered, False)
 
     other_rows = lax.dynamic_slice_in_dim(patches, (1 - part) * NTOK, NTOK, 0)
     own_rows = lax.dynamic_slice_in_dim(patches, part * NTOK, NTOK, 0)
@@ -1263,6 +1369,20 @@
     streams = [s.astype(jnp.bfloat16) for s in (stream_zero, stream_one, stream_two)]
     stacked = jnp.concatenate([halves(s)[m] for m in range(MP) for s in streams], 1)
     up_t = dot(w_deconv, stacked, ((0,), (1,)))
+
+    def columns(array, which, width, start):
+        return lax.dynamic_slice_in_dim(array, which * width + start, width - start, 1)
+
+    down_start = 2 * FF // MP // 3
+    stacked_pair = jnp.concatenate(
+        [columns(stacked, part, 3 * HALF, 0), swap_mp(columns(stacked, 1 - part, 3 * HALF, 0))]
+    )
+    active_pair = jnp.concatenate(
+        [
+            columns(active, part, FF // MP, down_start),
+            swap_mp(columns(active, 1 - part, FF // MP, down_start)),
+        ]
+    )
 
     conv_weight = pieces["conv_weight"].astype(jnp.bfloat16).reshape(27, DEC, CF)
     conv_low = conv_weight.transpose(0, 2, 1).reshape(27 * CF, DEC)
@@ -1298,12 +1418,8 @@
         head_weight,
     )
     loss_value = small[0, 2]
-    grad_head_bias = small[:NCLS, 0]
-    grad_conv_bias = small[:, 1]
-    grad_deconv_bias = deconv_bias_grad[:, 0]
-    grad_conv_weight = conv_grad.reshape(27, CF, DEC).transpose(0, 2, 1)
-    grad_head_weight = head_grad[:, :NCLS]
-
+
+    gu_pair = jnp.concatenate([gu_t, swap_mp(gu_t)], 1)
     stacked_back = dot(gu_t, w_deconv, ((0,), (1,)))
     back_zero_s, back_one_s, back_two = [
         jnp.concatenate([stacked_back[:, (3 * m + s) * HALF : (3 * m + s + 1) * HALF] for m in range(MP)], 1)
@@ -1311,6 +1427,7 @@
     ]
     grad_down_bias = jnp.sum(back_two, 0)
     two_low = back_two.astype(jnp.bfloat16)
+    two_pair = jnp.concatenate([two_low, swap_mp(two_low)])
     back_hidden = (hidden_slope * dot_nt(two_low, w_down)).astype(jnp.bfloat16)
     grad_up_bias = jnp.sum(back_hidden.astype(jnp.float32), 0)
     back_normed_two = dot_nt(back_hidden, w_up)
@@ -1343,66 +1460,91 @@
     )
 
     fast = fast_mesh()
-    depth = CHUNK if fast else 24 * BS
+    depth = CHUNK if fast else BLOCK_ROWS
+    final_grads = grad_blocks(
+        stacked_pair, gu_pair, 1, 9, 8, 3, 24, True, False, None, "grad_deconv", 4, BLOCK_ROWS, True
+    )
+    final_grads = grad_blocks(
+        active_pair, two_pair, 1, 4, 6, 4, 0, True, False, final_grads, "grad_down_last", 4, BLOCK_ROWS
+    )
     rest_grads = None
-    for name, x, g, rows, per_row, start, split_x, split_g in (
-        ("grad_deconv", stacked, gu_t, 9, 8, 216, True, False),
-        ("grad_down", active, two_low, 12, 6, 144, True, False),
-        ("grad_up", normed_two, back_hidden, 6, 12, 72, False, True),
-        ("grad_proj", mixed, one_low, 3, 6, 54, True, False),
-        ("grad_qkv", normed_one, back_qkv, 6, 9, 0, False, True),
+    for name, x, g, rows, per_row, step_rows, start, split_x, split_g, stride in (
+        ("grad_down", active, two_low, 8, 6, 4, 144, True, False, 3),
+        ("grad_up", normed_two, back_hidden, 6, 12, 3, 72, False, True, None),
+        ("grad_proj", mixed, one_low, 3, 6, 3, 54, True, False, None),
+        ("grad_qkv", normed_one, back_qkv, 6, 9, 3, 0, False, True, None),
     ):
         rest_grads = grad_blocks(
-            x, g, MP, rows, per_row, 3, start, split_x, split_g, rest_grads, name, 12, depth, g is gu_t
+            x, g, MP, rows, per_row, step_rows, start, split_x, split_g, rest_grads, name, 8, depth,
+            x_stride=stride,
         )
-    embed_grads = grad_blocks(
-        patches, zero_pair, 1, 16, 6, 4, 0, False, False, None, "grad_embed", 4, 24 * BS
-    )
-    late = jnp.stack(
+    first_grads = grad_blocks(
+        patches, zero_pair, 1, 16, 6, 4, 0, False, False, None, "grad_embed", 4, BLOCK_ROWS
+    )
+    vectors = jnp.concatenate(
         [
-            grad_gain_one,
-            grad_gain_two,
-            grad_shift_one,
-            grad_shift_two,
-            grad_query_bias,
-            grad_value_bias,
-            grad_proj_bias,
+            jnp.stack(
+                [
+                    grad_gain_one,
+                    grad_gain_two,
+                    grad_shift_one,
+                    grad_shift_two,
+                    grad_query_bias,
+                    grad_value_bias,
+                    grad_proj_bias,
+                    grad_down_bias,
+                ]
+            ),
+            jnp.pad(grad_up_bias.reshape(FF // D, D), ((0, 8 - FF // D), (0, 0))),
         ]
     )
-    rest = jnp.concatenate(
+    wide = jnp.concatenate([back_zero, vectors])
+    tall = wide.shape[0]
+    aux_rows = jnp.concatenate(
+        [wide[:, j * BS : (j + 1) * BS] for j in range(D // BS)]
+        + [conv_grad, jnp.pad(head_grad, ((0, 0), (0, BS - CF))), small, deconv_bias_grad]
+    )
+    if fast:
+        room = 8 * MP * AUX_ROWS
+        placed = jnp.pad(aux_rows, ((0, room - aux_rows.shape[0]), (0, 0)))
+        placed = placed.reshape(MP, 8, AUX_ROWS, BS)
+        rest_grads = lax.dynamic_update_slice(rest_grads, placed, (0, 0, BLOCK_ROWS, 0))
+        reduced, squares = reduce_to_owners(
+            rest_grads.reshape(MP, 2, 2, 2, CHUNK, BS),
+            first_grads.reshape(2, 2, BLOCK_ROWS, BS),
+            final_grads.reshape(2, 2, BLOCK_ROWS, BS),
+        )
+        owned = reduced[:BLOCK_ROWS].reshape(24, BS, BS)
+        gathered_aux = gather_all(
+            jnp.concatenate([reduced[BLOCK_ROWS:], squares]), 1, False, 4, "gather_aux"
+        )
+        block_square = jnp.sum(gathered_aux[:, :, AUX_ROWS:])
+        aux_sum = gathered_aux[:, 4:12, :AUX_ROWS].reshape(-1, BS)
+    else:
+        owned = reduce_plain(rest_grads.reshape(MP, -1, BS, BS), first_grads, final_grads)
+        aux_sum = lax.psum(aux_rows, ("dp", "mp"))
+        block_square = lax.psum(jnp.sum(owned * owned), ("dp", "mp"))
+    wide_sum = jnp.concatenate([aux_sum[j * tall : (j + 1) * tall] for j in range(D // BS)], 1)
+    after = D // BS * tall
+    conv_sum = aux_sum[after : after + 27 * CF]
+    head_sum = aux_sum[after + 27 * CF : after + 28 * CF]
+    small_sum = aux_sum[after + 28 * CF : after + 29 * CF]
+    deconv_sum = aux_sum[after + 29 * CF : after + 29 * CF + DEC, 0]
+    positions_sum = wide_sum[:NTOK]
+    aux_total = jnp.concatenate(
         [
-            late.reshape(-1),
-            grad_up_bias,
-            grad_down_bias,
-            grad_deconv_bias,
-            grad_conv_weight.reshape(-1),
-            grad_conv_bias,
-            grad_head_weight.reshape(-1),
-            grad_head_bias,
+            positions_sum.reshape(-1),
+            jnp.sum(positions_sum, 0),
+            wide_sum[NTOK : NTOK + 7].reshape(-1),
+            wide_sum[NTOK + 8 : NTOK + 8 + FF // D].reshape(-1),
+            wide_sum[NTOK + 7],
+            deconv_sum,
+            conv_sum.reshape(27, CF, DEC).transpose(0, 2, 1).reshape(-1),
+            small_sum[:, 1],
+            head_sum[:, :NCLS].reshape(-1),
+            small_sum[:NCLS, 0],
         ]
     )
-    aux_parts = jnp.concatenate([back_zero.reshape(-1), rest])
-    if fast:
-        room = 12 * MP * AUX_ROWS * BS
-        aux_rows = jnp.pad(aux_parts, (0, room - aux_parts.shape[0])).reshape(MP, 12, AUX_ROWS, BS)
-        rest_grads = lax.dynamic_update_slice(rest_grads, aux_rows, (0, 0, 24 * BS, 0))
-        reduced = reduce_to_owners(
-            rest_grads.reshape(MP, LAYERS - 1, 2, 2, CHUNK, BS), embed_grads.reshape(2, 2, 24 * BS, BS)
-        )
-        owned = reduced[: 24 * BS].reshape(24, BS, BS)
-        square = jnp.broadcast_to(jnp.sum(owned * owned).reshape(1, 1), (8, BS))
-        gathered_aux = gather_all(
-            jnp.concatenate([reduced[24 * BS :], square]), 64, False, 4, "gather_aux"
-        )
-        block_square = jnp.sum(gathered_aux[:, :, AUX_ROWS, 0])
-        aux_sum = gathered_aux[:, 4:, :AUX_ROWS].reshape(-1)
-    else:
-        owned = reduce_plain(rest_grads.reshape(MP, -1, BS, BS), embed_grads)
-        aux_sum = lax.psum(aux_parts, ("dp", "mp"))
-        block_square = lax.psum(jnp.sum(owned * owned), ("dp", "mp"))
-    positions_sum = aux_sum[: NTOK * D]
-    embed_bias_sum = jnp.sum(positions_sum.reshape(NTOK, D), 0)
-    aux_total = jnp.concatenate([positions_sum, embed_bias_sum, aux_sum[NTOK * D : NAUX - D]])
     grad_norm = jnp.sqrt(block_square + jnp.sum(aux_total * aux_total))
     clip_scale = clip_value / jnp.maximum(grad_norm, clip_value)
     block_new, stat_new, moment_new, veloc_new = shampoo_step(

time: 667 us -> 605 us (0.907)
  local copies, waits for them, and re-layouts: 149 us -> 98.4 us
  Pallas kernels: 422 us -> 388 us
  waiting for transfers between devices: 0.01 us -> 13.7 us
    pallas_call x4 -> x6, Pallas kernels: 361 us -> 329 us  [the longest x1 177 us: reduce_to_owners(): pl.pallas_call(reduce_kernel, out_shape=(jax.ShapeDtypeStruct((CHUNK, BS)...]
    slice x12 -> x10, local copies, waits for them, and re-layouts: 29.6 us -> 2.27 us  [the longest x1 0.91 us: local(): reduced[BLOCK_ROWS:]]
    transpose x11 -> x1, local copies, waits for them, and re-layouts: 27 us -> 1.47 us  [local(): conv_sum.reshape(27, CF, DEC).transpose(0, 2, 1).reshape(-1)]
    ppermute x2 -> x6, waiting for transfers between devices: 0.01 us -> 13.7 us  [swap_mp(): return lax.ppermute(values, 'mp', [(0, 1), (1, 0)])]
    concatenate x7 -> x4, local copies, waits for them, and re-layouts: 26 us -> 18.5 us  [the longest x1 12.7 us: local(): jnp.concatenate([positions_sum.reshape(-1), jnp.sum(positions_sum, 0), wi...]
    pallas_call x6 -> x7, Pallas kernels: 33.2 us -> 30 us  [grad_blocks(): pl.pallas_call(functools.partial(blocks_kernel, first_block, per_row, ste...]
    unnamed x237 -> x202, local copies, waits for them, and re-layouts: 45.2 us -> 44.6 us
  transfers between devices with their start and end apart: 2 -> 6, of which waited for: 0 -> 1; matrix products, arithmetic and copies ran while one was open for 10% -> 12% of each run, Pallas kernels for 3% -> 8%
where the time goes in v3:
time: 605 us; the launch traced here: 594 us
  Pallas kernels  388 us (64%)
  local copies, waits for them, and re-layouts  98.4 us (16%)
  matrix products  51 us (8%)
  other arithmetic  31.2 us (5%)
  waiting for transfers between devices  13.7 us (2%)
  starting transfers between devices  6.27 us (1%)
    pallas_call x1, Pallas kernels, reduce_to_owners(): pl.pallas_call(reduce_kernel, out_shape=(jax.ShapeDtypeStruct((CHUNK, BS)...  177 us
    pallas_call x2, Pallas kernels, gather_all(): pl.pallas_call(functools.partial(gather_kernel, rows, parts, skip), out_s...  130 us
    unnamed x202, local copies, waits for them, and re-layouts  44.6 us
    dot_general x12, matrix products, dot(): lax.dot_general(a, b, (dims, ((), ())), preferred_element_type=jnp.float32)  41 us
    pallas_call x7, Pallas kernels, grad_blocks(): pl.pallas_call(functools.partial(blocks_kernel, first_block, per_row, ste...  30 us
    ppermute x6, waiting for transfers between devices, swap_mp(): return lax.ppermute(values, 'mp', [(0, 1), (1, 0)])  13.7 us
    concatenate x1, local copies, waits for them, and re-layouts, local(): jnp.concatenate([positions_sum.reshape(-1), jnp.sum(positions_sum, 0), wi...  12.7 us
    pallas_call x1, Pallas kernels, attention_backward(): pl.pallas_call(attention_backward_kernel, grid=(6,), out_shape=(jax.Shape...  12.7 us
  transfers between devices with their start and end apart: 6, of which 1 were waited for; matrix products, arithmetic and copies ran while one was open for 12% of the time, Pallas kernels for 8%

profile of v3, /device:TPU:0, one launch (start us, length us, event | category | flops | bytes accessed | tf_op | source)
XLA Modules:
  0.0 593.9 jit_solution(3579406470443914451)
XLA Ops:
  2.2 100.6 %gather_weights.1 = bf16[2,16,3072,128]{3,2,1,0:T(8,128)(2,1)} custom-call(bf16[3072,128]{1,0:T(8,128)(2,1)S(1)} %bitcast.109), custom_call_target="tpu_custom_call" | custom-call | bytes 50331648 | tf_op jit(solution)/shard_map/gather_weights/pallas_call | solution.py:624
  102.8 2.1 unblock_embedding.1
  104.9 4.5 fusion.7
  116.0 9.5 %unblock.1 = (bf16[768,2304]{1,0:T(8,128)(2,1)S(1)}, bf16[768,768]{1,0:T(8,128)(2,1)S(1)}, bf16[768,3072]{1,0:T(8,128)(2,1)S(1)}, bf16[3072,768]{1,0:T(8,128)(2,1)S(1)}, bf16[2304,1024]{1,0:T(8,128)(2,1)S(1)}) custom-call(bf16[2,384,128,128]{3,2,1,0:T(8,128)(2,1)} %bitcast.123), custom_call_target="tpu_custom_call" | custom-call | bytes 39845888 | tf_op jit(solution)/shard_map/unblock/pallas_call | solution.py:1095
  125.5 2.1 copy-done.31
  127.6 2.1 copy-done.32
  129.7 2.1 copy-done.33
  139.4 2.1 copy.71
  143.8 2.0 reshape.230
  145.7 3.6 copy.66
  150.5 2.8 reshape.224
  156.8 4.4 fusion.56
  163.9 2.0 fusion.6.qkv_q.qkv_k.qkv_v
  166.8 9.2 %attention_forward.1 = (bf16[512,768]{1,0:T(8,128)(2,1)S(1)}, f32[6,2,512]{2,1,0:T(2,128)S(1)}) custom-call(bf16[512,2304]{1,0:T(8,128)(2,1)S(1)} %fusion.6.qkv_q.qkv_k.qkv_v, bf16[512,2304]{1,0:T(8,128)(2,1)S(1)} %fusion.6.qkv_q.qkv_k.qkv_v, bf16[512,2304]{1,0:T(8,128)(2,1)S(1)} %fusion.6.qkv_q.qkv_k.qkv_v), custom_call_target="tpu_custom_call" | custom-call | flops 805306368 | bytes 3145728 | tf_op jit(solution)/shard_map/attention_forward/pallas_call | solution.py:137
  178.1 5.5 multiply_convert_fusion
  183.7 2.6 add_convert_fusion
  186.9 2.6 convolution_bitcast_fusion.up_ref
  189.6 4.3 decoder_forward.1
  196.8 10.0 %sum_sums.1.sums_ref = f32[16,128]{1,0:T(8,128)} custom-call(f32[16,128]{1,0:T(8,128)} %copy-done.30), custom_call_target="tpu_custom_call" | custom-call | tf_op jit(solution)/shard_map/sum_sums/pallas_call | solution.py:1246
  210.3 3.1 decoder_backward.1
  213.4 5.5 fusion.58
  222.6 4.6 convert_reduce_fusion
  227.3 3.0 multiply_reduce_fusion.2
  234.0 12.7 %attention_backward.1 = (bf16[512,768]{1,0:T(8,128)(2,1)S(1)}, bf16[512,768]{1,0:T(8,128)(2,1)S(1)}, bf16[512,768]{1,0:T(8,128)(2,1)S(1)}) custom-call(bf16[512,2304]{1,0:T(8,128)(2,1)S(1)} %fusion.6.qkv_q.qkv_k.qkv_v, bf16[512,2304]{1,0:T(8,128)(2,1)S(1)} %fusion.6.qkv_q.qkv_k.qkv_v, bf16[512,2304]{1,0:T(8,128)(2,1)S(1)} %fusion.6.qkv_q.qkv_k.qkv_v, ...), custom_call_target="tpu_custom_call" | custom-call | flops 2013265920 | bytes 5505024 | tf_op jit(solution)/shard_map/attention_backward/pallas_call | solution.py:161
  247.0 4.3 grad_down.1.refs_2_
  260.7 4.6 multiply_reduce_fusion.3
  265.4 2.0 fusion.49
  269.1 5.8 concatenate.57
  280.8 1.9 copy-done.10
  282.7 5.8 grad_up.1.refs_2_
  290.0 2.3 grad_proj.1.refs_2_
  292.3 5.1 grad_qkv.1
  301.5 13.7 %collective-permute-done.1 = bf16[512,768]{1,0:T(8,128)(2,1)} collective-permute-done((bf16[512,768]{1,0:T(8,128)(2,1)}, bf16[512,768]{1,0:T(8,128)(2,1)}, u32[]{:S(2)}, u32[]{:S(2)}) %collective-permute-start.1) | collective-permute-done | bytes 786464 | tf_op jit(solution)/shard_map/ppermute | solution.py:1262
  315.2 2.3 maximum_select_fusion.refs_1_
  317.5 6.2 %grad_embed.1 = f32[1,4,3072,128]{3,2,1,0:T(8,128)S(1)} custom-call(bf16[1024,2048]{1,0:T(8,128)(2,1)S(1)} %copy-done.4, bf16[1024,768]{1,0:T(8,128)(2,1)S(1)} %maximum_select_fusion.refs_1_), custom_call_target="tpu_custom_call" | custom-call | flops 3221225472 | bytes 6291456 | tf_op jit(solution)/shard_map/grad_embed/pallas_call | solution.py:1164
  323.8 2.6 copy-done.1
  326.4 1.9 pad_maximum_fusion.1.refs_1_
  329.8 4.9 grad_deconv.1.refs_2_
  336.0 2.7 copy-done
  338.6 177.0 %reduce_to_owners.1 = (f32[3328,128]{1,0:T(8,128)}, f32[8,128]{1,0:T(8,128)}) custom-call(f32[2,2,2,2,3328,128]{5,4,3,2,1,0:T(8,128)} %bitcast.121, f32[2,2,3072,128]{3,2,1,0:T(8,128)} %bitcast.108, f32[2,2,3072,128]{3,2,1,0:T(8,128)} %bitcast.107), custom_call_target="tpu_custom_call" | custom-call | bytes 104857600 | tf_op jit(solution)/shard_map/reduce_to_owners/pallas_call | solution.py:971
  517.3 29.5 %gather_aux.1 = f32[2,16,264,128]{3,2,1,0:T(8,128)S(1)} custom-call(f32[264,128]{1,0:T(8,128)S(1)} %pad_maximum_fusion.5.in_ref), custom_call_target="tpu_custom_call" | custom-call | bytes 4325376 | tf_op jit(solution)/shard_map/gather_aux/pallas_call | solution.py:624
  553.1 12.7 %concatenate.67 = f32[458878]{0:T(1024)S(1)} concatenate(f32[393216]{0:T(1024)} %reshape.239, f32[768]{0:T(1024)S(1)} %get-tuple-element.123, f32[5376]{0:T(1024)S(1)} %reshape.240, f32[3072]{0:T(1024)S(1)} %reshape.241, f32[768]{0:T(1024)S(1)} %slice_reduce_fusion.4, f32[128]{0:T(128)S(1)} %slice_reduce_fusion.1, f32[55296]{0:T(1024)} %reshape.243, f32[16]{0:T(128)S(1)} %slice_reduce_fusion.3, ...), dimensions={0} | concatenate | bytes 3671024 | tf_op jit(solution)/shard_map/concatenate | solution.py:1534
  570.2 3.4 fusion.22
  573.6 2.8 fusion.21
  580.3 1.9 multiply_reduce_fusion.1
  582.2 2.2 fusion.18
  584.4 2.0 maximum_bitcast_fusion
  589.3 3.3 multiply_subtract_fusion
  (305 shorter events, 84.4 us)
Async XLA Ops:
  109.4 47.4 %collective-permute-start = (f32[512,768]{1,0:T(8,128)}, f32[512,768]{1,0:T(8,128)}, u32[]{:S(2)}, u32[]{:S(2)}) collective-permute-start(f32[512,768]{1,0:T(8,128)} %fusion.7), channel_id=1, source_target_pairs={{0,1},{1,0},{2,3},{3,2},{4,5},{5,4},{6,7},{7,6},{8,9},{9,8},{10,11... | collective-permute-start | bytes 4718600 | tf_op jit(solution)/shard_map/ppermute | solution.py:1262
  136.4 6.7 %copy-start.71 = (s32[1,4096]{1,0:T(1,128)S(1)}, s32[1,4096]{1,0:T(1,128)}, u32[]{:S(2)}) copy-start(s32[1,4096]{1,0:T(1,128)} %param.12) | copy-start | bytes 49156
  156.8 4.8 copy-start.61
  161.3 14.7 %copy-start.43 = (f32[512,768]{1,0:T(8,128)}, f32[512,768]{1,0:T(8,128)S(1)}, u32[]{:S(2)}) copy-start(f32[512,768]{1,0:T(8,128)S(1)} %get-tuple-element.135) | copy-start | bytes 4718596
  161.6 4.3 copy-start.67
  166.8 9.2 %copy-start.37 = (bf16[768,768]{1,0:T(8,128)(2,1)S(1)}, bf16[768,768]{1,0:T(8,128)(2,1)}, u32[]{:S(2)}) copy-start(bf16[768,768]{1,0:T(8,128)(2,1)} %copy-done.36) | copy-start | bytes 3538948
  166.8 11.3 %slice-start = ((s8[4718592]{0:T(1024)(128)(4,1)}), s8[4194304]{0:T(1024)(128)(4,1)S(1)}, s32[]{:S(2)}) async-start(s8[4718592]{0:T(1024)(128)(4,1)} %bitcast.111), calls=%async_computation | async-start | bytes 8388608
  176.9 6.7 %copy-start.45 = (f32[512,768]{1,0:T(8,128)}, f32[512,768]{1,0:T(8,128)S(1)}, u32[]{:S(2)}) copy-start(f32[512,768]{1,0:T(8,128)S(1)} %get-tuple-element.137) | copy-start | bytes 4718596
  177.3 6.3 %slice-start.4 = ((s8[4718592]{0:T(1024)(128)(4,1)}), s8[4194304]{0:T(1024)(128)(4,1)S(1)}, s32[]{:S(2)}) async-start(s8[4718592]{0:T(1024)(128)(4,1)} %bitcast.115), calls=%async_computation.4 | async-start | bytes 8388608
  178.0 5.6 copy-start.7
  178.1 5.5 slice-start.5
  178.1 8.5 %slice-start.8 = ((s8[4718592]{0:T(1024)(128)(4,1)}), s8[524288]{0:T(1024)(128)(4,1)S(1)}, s32[]{:S(2)}) async-start(s8[4718592]{0:T(1024)(128)(4,1)} %bitcast.119), calls=%async_computation.8 | async-start | bytes 1048576
  183.7 3.3 slice-start.9
  186.6 3.0 copy-start.51
  210.3 12.3 %slice-start.6 = ((s8[4718592]{0:T(1024)(128)(4,1)}), s8[524288]{0:T(1024)(128)(4,1)S(1)}, s32[]{:S(2)}) async-start(s8[4718592]{0:T(1024)(128)(4,1)} %bitcast.117), calls=%async_computation.6 | async-start | bytes 1048576
  210.3 12.3 %slice-start.10 = ((s8[6291456]{0:T(1024)(128)(4,1)}), s8[4194304]{0:T(1024)(128)(4,1)S(1)}, s32[]{:S(2)}) async-start(s8[6291456]{0:T(1024)(128)(4,1)} %bitcast.146), calls=%async_computation.10 | async-start | bytes 8388608
  213.4 5.5 copy-start.25
  213.4 5.5 copy-start.28
  213.4 9.2 %slice-start.7 = ((s8[4718592]{0:T(1024)(128)(4,1)}), s8[4194304]{0:T(1024)(128)(4,1)S(1)}, s32[]{:S(2)}) async-start(s8[4718592]{0:T(1024)(128)(4,1)} %bitcast.117), calls=%async_computation.7 | async-start | bytes 8388608
  213.4 9.2 %slice-start.11 = ((s8[6291456]{0:T(1024)(128)(4,1)}), s8[2097152]{0:T(1024)(128)(4,1)S(1)}, s32[]{:S(2)}) async-start(s8[6291456]{0:T(1024)(128)(4,1)} %bitcast.146), calls=%async_computation.11 | async-start | bytes 4194304
  218.9 107.6 %collective-permute-start.5 = (bf16[1024,512]{1,0:T(8,128)(2,1)}, bf16[1024,512]{1,0:T(8,128)(2,1)}, u32[]{:S(2)}, u32[]{:S(2)}) collective-permute-start(bf16[1024,512]{1,0:T(8,128)(2,1)} %get-tuple-element.45), channel_id=1, source_target_pairs={{0,1},{1,0},{2,3},{3,2},{4,5},{5,4},{6,7},{7,6},{8,9},{9,8},{10,11... | collective-permute-start | bytes 3145736 | tf_op jit(solution)/shard_map/ppermute | solution.py:1262
  221.9 5.3 slice-start.2
  222.0 78.1 %collective-permute-start.3 = (bf16[512,768]{1,0:T(8,128)(2,1)S(1)}, bf16[512,768]{1,0:T(8,128)(2,1)}, u32[]{:S(2)}, u32[]{:S(2)}) collective-permute-start(bf16[512,768]{1,0:T(8,128)(2,1)S(1)} %fusion.38.refs_1_), channel_id=1, source_target_pairs={{0,1},{1,0},{2,3},{3,2},{4,5},{5,4},{6,7},{7,6},{8,9},{9,8},{10,11... | collective-permute-start | bytes 2359304 | tf_op jit(solution)/shard_map/ppermute | solution.py:1262
  222.6 4.6 slice-start.3
  222.6 4.6 copy-start.46
  222.6 4.7 copy-start.66
  222.6 4.7 copy-start.70
  227.2 3.1 copy-start.9
  234.0 12.9 %copy-start.3 = (bf16[512,3072]{1,0:T(8,128)(2,1)S(1)}, bf16[512,3072]{1,0:T(8,128)(2,1)}, u32[]{:S(2)}) copy-start(bf16[512,3072]{1,0:T(8,128)(2,1)} %copy-done.2) | copy-start | bytes 9437188
  246.7 4.6 copy-start.11
  246.7 4.6 copy-start.13
  246.7 4.6 copy-start.21
  247.0 7.0 %copy-start.52 = (bf16[512,2304]{1,0:T(8,128)(2,1)S(1)}, bf16[512,2304]{1,0:T(8,128)(2,1)}, u32[]{:S(2)}) copy-start(bf16[512,2304]{1,0:T(8,128)(2,1)} %copy-done.51) | copy-start | bytes 7077892
  252.5 46.5 %collective-permute-start.2 = (bf16[512,512]{1,0:T(8,128)(2,1)}, bf16[512,512]{1,0:T(8,128)(2,1)}, u32[]{:S(2)}, u32[]{:S(2)}) collective-permute-start(bf16[512,512]{1,0:T(8,128)(2,1)} %get-tuple-element.113), channel_id=1, source_target_pairs={{0,1},{1,0},{2,3},{3,2},{4,5},{5,4},{6,7},{7,6},{8,9},{9,8},{10,11... | collective-permute-start | bytes 1572872 | tf_op jit(solution)/shard_map/ppermute | solution.py:1262
  255.7 72.6 %collective-permute-start.4 = (bf16[512,1152]{1,0:T(8,128)(2,1)}, bf16[512,1152]{1,0:T(8,128)(2,1)}, u32[]{:S(2)}, u32[]{:S(2)}) collective-permute-start(bf16[512,1152]{1,0:T(8,128)(2,1)} %get-tuple-element.115), channel_id=1, source_target_pairs={{0,1},{1,0},{2,3},{3,2},{4,5},{5,4},{6,7},{7,6},{8,9},{9,8},{10,11... | collective-permute-start | bytes 3538952 | tf_op jit(solution)/shard_map/ppermute | solution.py:1262
  256.7 2.8 copy-start.22
  260.7 4.7 copy-start.42
  260.7 4.7 copy-start.53
  260.7 4.7 copy-start.54
  267.4 47.8 %collective-permute-start.1 = (bf16[512,768]{1,0:T(8,128)(2,1)}, bf16[512,768]{1,0:T(8,128)(2,1)}, u32[]{:S(2)}, u32[]{:S(2)}) collective-permute-start(bf16[512,768]{1,0:T(8,128)(2,1)} %get-tuple-element.102), channel_id=1, source_target_pairs={{0,1},{1,0},{2,3},{3,2},{4,5},{5,4},{6,7},{7,6},{8,9},{9,8},{10,11... | collective-permute-start | bytes 2359304 | tf_op jit(solution)/shard_map/ppermute | solution.py:1262
  274.8 5.9 %copy-start.8 = (bf16[512,768]{1,0:T(8,128)(2,1)S(1)}, bf16[512,768]{1,0:T(8,128)(2,1)}, u32[]{:S(2)}) copy-start(bf16[512,768]{1,0:T(8,128)(2,1)} %copy-done.7) | copy-start | bytes 2359300
  282.7 5.9 copy-start.29
  282.7 5.9 copy-start.26
  300.1 17.4 %copy-start.4 = (bf16[1024,2048]{1,0:T(8,128)(2,1)S(1)}, bf16[1024,2048]{1,0:T(8,128)(2,1)}, u32[]{:S(2)}) copy-start(bf16[1024,2048]{1,0:T(8,128)(2,1)} %refs_0_.1) | copy-start | bytes 12582916
  573.6 2.8 copy-start.47
  573.6 2.8 copy-start.49
  584.4 3.6 copy-start.59
  586.4 2.8 copy-start.58
  (44 other events, 73.6 us)

commit v4 on v3

--- a/solution.py
+++ b/solution.py
@@ -414,6 +414,7 @@
 
 LAYERS = 4
 GATHER_LAG = 2
+THIRDS = tuple((8 * BS * i, 8 * BS) for i in range(3))
 PIECES = 32
 BLOCK_ROWS = 24 * BS
 AUX_ROWS = 256
@@ -474,15 +475,13 @@
     pl.semaphore_wait(barrier, peers)
 
 
-def gather_kernel(rows, parts, skip, in_ref, out_ref, local_sem, up_sem, down_sem, z_recv, x_send, x_recv, y_send, y_recv, core_send, core_recv):
+def gather_kernel(parts, by_x, skip, middle, in_ref, out_ref, local_sem, up_sem, down_sem, z_recv, x_send, x_recv, y_send, y_recv, core_send, core_recv):
     at = places()
     x, y, z, c = at["x"], at["y"], at["z"], at["c"]
     last = LAYERS - 1
-    size = rows // parts
-    by_x = -(-parts // 3)
 
     def spot(l, y_at, c_at, x_at, p):
-        return out_ref.at[x_at, l * 4 + y_at * 2 + c_at, pl.ds(p * size, size)]
+        return out_ref.at[x_at, l * 4 + y_at * 2 + c_at, pl.ds(*parts[p])]
 
     def send(ref, send_sem, recv_sem, device):
         return remote(ref, ref, send_sem, recv_sem, device)
@@ -566,77 +565,89 @@
             diagonal(l, p, 1 - y, 1 - x).wait_recv()
             core(l, p, 3, c).start()
 
+    def held(l, p):
+        return ((l > 0) & (l < last)) if p in middle else ((l >= 0) & (l <= last))
+
+    number = len(parts)
+
     def both(tick, run):
-        if tick < 0 or tick >= LAYERS * parts:
+        if tick < 0 or tick >= LAYERS * number:
             return
-        r, p = tick // parts, tick % parts
+        r, p = tick // number, tick % number
         if r == 0:
-            run(z, p, True, True)
+
+            @pl.when(held(z, p))
+            def _():
+                run(z, p, True, True)
+
             return
 
-        @pl.when(z - r >= 0)
+        @pl.when(held(z - r, p))
         def _():
             run(z - r, p, True, False)
 
-        @pl.when(z + r <= last)
+        @pl.when(held(z + r, p))
         def _():
             run(z + r, p, False, True)
 
-    for tick in range(LAYERS * parts + 2 * GATHER_LAG):
+    for tick in range(LAYERS * number + 2 * GATHER_LAG):
         both(tick, arrive)
         both(tick - GATHER_LAG, lambda l, p, up_way, down_way: relay(l, p))
         both(tick - 2 * GATHER_LAG, lambda l, p, up_way, down_way: finish(l, p))
 
-    def settle(l, carry):
-        for p in range(parts):
-            for kind in (0, 1):
+    def settle_part(l, p):
+        for kind in (0, 1):
+            core(l, p, kind, 1 - c).wait_recv()
+            core(l, p, kind, c).wait_send()
+        y_direct(l, p, y).wait_send()
+
+        @pl.when(wide(l))
+        def _():
+            for kind in (2, 3):
                 core(l, p, kind, 1 - c).wait_recv()
                 core(l, p, kind, c).wait_send()
-            y_direct(l, p, y).wait_send()
-
-            @pl.when(wide(l))
-            def _(p=p):
-                for kind in (2, 3):
-                    core(l, p, kind, 1 - c).wait_recv()
-                    core(l, p, kind, c).wait_send()
-                x_direct(l, p, x).wait_send()
-                relayed(l, p).wait_send()
-
-            @pl.when((l <= z) & (z < last))
-            def _(p=p):
-                up(l, p).wait_send()
-
-            @pl.when((l >= z) & (z > 0))
-            def _(p=p):
-                down(l, p).wait_send()
-
+            x_direct(l, p, x).wait_send()
+            relayed(l, p).wait_send()
+
+        @pl.when((l <= z) & (z < last))
+        def _():
+            up(l, p).wait_send()
+
+        @pl.when((l >= z) & (z > 0))
+        def _():
+            down(l, p).wait_send()
+
+    def settle(l, carry):
+        for p in range(number):
+            pl.when(held(l, p))(functools.partial(settle_part, l, p))
         return carry
 
     lax.fori_loop(0, LAYERS, settle, 0)
 
 
-def gather_all(values, parts, skip, collective_id, name):
+def gather_all(values, parts, by_x, skip, middle, collective_id, name):
     rows = values.shape[0]
+    number = len(parts)
 
     def sems(*shape):
         return pltpu.SemaphoreType.DMA(shape)
 
     return pl.pallas_call(
-        functools.partial(gather_kernel, rows, parts, skip),
+        functools.partial(gather_kernel, parts, by_x, skip, middle),
         out_shape=jax.ShapeDtypeStruct((MP, 4 * LAYERS, rows, BS), values.dtype),
         in_specs=[pl.BlockSpec(memory_space=pl.ANY)],
         out_specs=pl.BlockSpec(memory_space=pl.ANY),
         scratch_shapes=[
             pltpu.SemaphoreType.DMA,
-            sems(LAYERS, parts),
-            sems(LAYERS, parts),
-            sems(LAYERS, parts),
-            sems(LAYERS, parts, 2),
-            sems(LAYERS, parts, 2),
-            sems(LAYERS, parts, 2),
-            sems(LAYERS, parts, 2),
-            sems(LAYERS, parts, 4),
-            sems(LAYERS, parts, 4),
+            sems(LAYERS, number),
+            sems(LAYERS, number),
+            sems(LAYERS, number),
+            sems(LAYERS, number, 2),
+            sems(LAYERS, number, 2),
+            sems(LAYERS, number, 2),
+            sems(LAYERS, number, 2),
+            sems(LAYERS, number, 4),
+            sems(LAYERS, number, 4),
         ],
         compiler_params=pltpu.CompilerParams(
             collective_id=collective_id, has_side_effects=True, vmem_limit_bytes=32 * MIB
@@ -1111,8 +1122,7 @@
     )(gathered)
 
 
-def blocks_kernel(first_block, per_row, step_rows, transposed, has_buffer, *refs):
-    x_ref, g_ref = refs[:2]
+def blocks_kernel(first_block, per_row, step_rows, transposed, pairs, *refs):
     out_ref, tiles, sems = refs[-3:]
     m, i = pl.program_id(0), pl.program_id(1)
     steps = pl.num_programs(1)
@@ -1127,7 +1137,12 @@
     def _():
         drain(slot)
 
-    tiles[slot] = dot(x_ref[...], g_ref[...], ((0,), (1,) if transposed else (0,)))
+    total_product = None
+    for pair in range(pairs):
+        x_ref, g_ref = refs[2 * pair], refs[2 * pair + 1]
+        term = dot(x_ref[...], g_ref[...], ((0,), (1,) if transposed else (0,)))
+        total_product = term if total_product is None else total_product + term
+    tiles[slot] = total_product
     for r in range(step_rows):
         for c in range(per_row):
             block = first_block + (i * step_rows + r) * per_row + c
@@ -1147,10 +1162,10 @@
             drain(1 - slot)
 
 
-def grad_blocks(x, g, parts, rows, per_row, step_rows, first_block, split_x, split_g, buffer, name, chunks, depth, transposed=False, x_stride=None):
+def grad_blocks(xs, gs, parts, rows, per_row, step_rows, first_block, split_x, split_g, buffer, name, chunks, depth, transposed=False, x_stride=None):
     steps = rows // step_rows
     x_stride = x_stride or steps
-    tokens = x.shape[0]
+    tokens = xs[0].shape[0]
     width = per_row * BS
     x_spec = pl.BlockSpec(
         (tokens, step_rows * BS), (lambda m, i: (0, m * x_stride + i)) if split_x else (lambda m, i: (0, i))
@@ -1160,23 +1175,23 @@
     else:
         g_spec = pl.BlockSpec((tokens, width), (lambda m, i: (0, m)) if split_g else (lambda m, i: (0, 0)))
     anywhere = pl.BlockSpec(memory_space=pl.ANY)
-    operands = [x, g] + ([] if buffer is None else [buffer])
+    operands = [array for pair in zip(xs, gs) for array in pair] + ([] if buffer is None else [buffer])
     return pl.pallas_call(
         functools.partial(
-            blocks_kernel, first_block, per_row, step_rows, transposed, buffer is not None
+            blocks_kernel, first_block, per_row, step_rows, transposed, len(xs)
         ),
         grid=(parts, steps),
         out_shape=jax.ShapeDtypeStruct((parts, chunks, depth, BS), jnp.float32),
-        in_specs=[x_spec, g_spec] + ([] if buffer is None else [anywhere]),
+        in_specs=[x_spec, g_spec] * len(xs) + ([] if buffer is None else [anywhere]),
         out_specs=anywhere,
-        input_output_aliases={} if buffer is None else {2: 0},
+        input_output_aliases={} if buffer is None else {2 * len(xs): 0},
         scratch_shapes=[
             pltpu.VMEM((2, step_rows * BS, width), jnp.float32),
             pltpu.SemaphoreType.DMA((2,)),
         ],
         compiler_params=pltpu.CompilerParams(vmem_limit_bytes=32 * MIB),
         cost_estimate=pl.CostEstimate(
-            flops=2 * tokens * parts * rows * BS * width,
+            flops=2 * len(xs) * tokens * parts * rows * BS * width,
             bytes_accessed=parts * rows * BS * width * 4,
             transcendentals=0,
         ),
@@ -1231,7 +1246,7 @@
 def gather_weights(blocks):
     low = blocks.astype(jnp.bfloat16)[0, 0]
     if fast_mesh():
-        gathered = gather_all(low.reshape(-1, BS), 3, True, 2, "gather_weights")
+        gathered = gather_all(low.reshape(-1, BS), THIRDS, 1, True, (), 2, "gather_weights")
     else:
         gathered = lax.all_gather(low, ("dp", "mp"), axis=0, tiled=False)
         gathered = gathered.reshape((-1, MP) + low.shape).swapaxes(0, 1)
@@ -1274,6 +1289,158 @@
     )[0]
 
 
+TALL = NTOK + 16
+TILES = D // BS
+CONV_AT = TILES * TALL
+HEAD_AT = CONV_AT + 27 * CF
+SMALL_AT = HEAD_AT + CF
+DECONV_AT = SMALL_AT + CF
+PACKED = DECONV_AT + DEC
+AUX_ROOM = 8 * MP * AUX_ROWS
+FLAT_ROWS = -(-NAUX // (8 * BS)) * 8
+
+
+def pack_kernel(zero_ref, *refs):
+    vectors, up_ref, conv_ref, head_ref, small_ref, deconv_ref = refs[:8], *refs[8:13]
+    out_ref, rows_ref, sems = refs[14:]
+    for j in range(TILES):
+        lanes_at = slice(j * BS, (j + 1) * BS)
+        base = j * TALL
+        rows_ref[base : base + NTOK] = zero_ref[:, lanes_at]
+        small_rows = [vector[:, lanes_at] for vector in vectors]
+        small_rows += [up_ref[:, i * D + j * BS : i * D + (j + 1) * BS] for i in range(FF // D)]
+        small_rows += [jnp.zeros((16 - len(small_rows), BS), jnp.float32)]
+        rows_ref[base + NTOK : base + TALL] = jnp.concatenate(small_rows, 0)
+    lane = lax.broadcasted_iota(jnp.int32, (CF, BS), 1)
+    wide_lane = lax.broadcasted_iota(jnp.int32, (DEC, BS), 1)
+    rows_ref[CONV_AT:HEAD_AT] = conv_ref[...]
+    rows_ref[HEAD_AT:SMALL_AT] = head_ref[...]
+    rows_ref[SMALL_AT:DECONV_AT] = jnp.where(lane < 2, small_ref[...], 0.0)
+    rows_ref[DECONV_AT:PACKED] = jnp.where(wide_lane < 1, deconv_ref[...], 0.0)
+    rows_ref[PACKED:AUX_ROOM] = jnp.zeros((AUX_ROOM - PACKED, BS), jnp.float32)
+    copies = [
+        pltpu.make_async_copy(
+            rows_ref.at[pl.ds((m * 8 + chunk) * AUX_ROWS, AUX_ROWS)],
+            out_ref.at[m, chunk, pl.ds(BLOCK_ROWS, AUX_ROWS)],
+            sems.at[m * 8 + chunk],
+        )
+        for m in range(MP)
+        for chunk in range(8)
+    ]
+    for copy in copies:
+        copy.start()
+    for copy in copies:
+        copy.wait()
+
+
+def pack_aux(zero, vectors, up_bias, conv, head, small, deconv, buffer):
+    whole = pl.BlockSpec(memory_space=pltpu.VMEM)
+    anywhere = pl.BlockSpec(memory_space=pl.ANY)
+    operands = [zero] + [vector.reshape(1, D) for vector in vectors]
+    operands += [up_bias.reshape(1, FF), conv, head, small, deconv]
+    return pl.pallas_call(
+        pack_kernel,
+        out_shape=jax.ShapeDtypeStruct(buffer.shape, jnp.float32),
+        in_specs=[whole] * len(operands) + [anywhere],
+        out_specs=anywhere,
+        input_output_aliases={len(operands): 0},
+        scratch_shapes=[
+            pltpu.VMEM((AUX_ROOM, BS), jnp.float32),
+            pltpu.SemaphoreType.DMA((8 * MP,)),
+        ],
+        compiler_params=pltpu.CompilerParams(vmem_limit_bytes=32 * MIB),
+        cost_estimate=pl.CostEstimate(flops=0, bytes_accessed=4 * MIB, transcendentals=0),
+        name="pack_aux",
+    )(*operands, buffer)
+
+
+def unpack_kernel(sums_ref, rows_ref, norm_ref, turned):
+    def pieces(start, stop):
+        at = start
+        while at < stop:
+            m, chunk = at // (8 * AUX_ROWS), at // AUX_ROWS % 8
+            end = min(stop, (at // AUX_ROWS + 1) * AUX_ROWS)
+            first = at % AUX_ROWS
+            yield at - start, sums_ref[m, 4 + chunk, first : first + end - at]
+            at = end
+
+    def packed(start, stop):
+        found = [piece for _, piece in pieces(start, stop)]
+        return found[0] if len(found) == 1 else jnp.concatenate(found, 0)
+
+    square = jnp.zeros((8, BS), jnp.float32)
+    for m in range(MP):
+        for owner in range(4 * LAYERS):
+            square += sums_ref[m, owner, AUX_ROWS:]
+    rows_ref[FLAT_ROWS - 16 :] = jnp.zeros((16, BS), jnp.float32)
+    after = NTOK * TILES
+    for j in range(TILES):
+        token_sum = jnp.zeros((1, BS), jnp.float32)
+        for offset, piece in pieces(j * TALL, j * TALL + NTOK):
+            rows_ref[pl.ds(offset * TILES + j, piece.shape[0], stride=TILES)] = piece
+            token_sum += jnp.sum(piece, 0, keepdims=True)
+            square += jnp.sum((piece * piece).reshape(-1, 8, BS), 0)
+        vectors = packed(j * TALL + NTOK, (j + 1) * TALL)
+        square += jnp.sum((vectors * vectors).reshape(-1, 8, BS), 0)
+        square += jnp.concatenate([token_sum * token_sum, jnp.zeros((7, BS), jnp.float32)], 0)
+        rows_ref[after + j : after + j + 1] = token_sum
+        order = list(range(7)) + list(range(8, 8 + FF // D)) + [7]
+        for place, which in enumerate(order):
+            at = after + TILES * (1 + place) + j
+            rows_ref[at : at + 1] = vectors[which : which + 1]
+    at = after + TILES * 13
+    deconv = packed(DECONV_AT, PACKED)
+    square += jnp.sum((deconv * deconv).reshape(-1, 8, BS), 0)
+    rows_ref[at : at + 1] = deconv.T[0:1]
+    at += 1
+    for o in range(27):
+        conv = packed(CONV_AT + o * CF, CONV_AT + (o + 1) * CF)
+        square += jnp.sum((conv * conv).reshape(-1, 8, BS), 0)
+        turned[:, 0:CF] = conv.T
+        for f in range(8):
+            rows_ref[at + o * CF : at + (o + 1) * CF, f * CF : (f + 1) * CF] = turned[
+                pl.ds(f, CF, stride=8), 0:CF
+            ]
+    at += 27 * CF
+    head = packed(HEAD_AT, SMALL_AT)
+    small = packed(SMALL_AT, DECONV_AT)
+    square += jnp.sum((head * head + small * small).reshape(-1, 8, BS), 0)
+    turned_small = small.T
+    segments = [(turned_small[1:2], CF)]
+    segments += [(head[row : row + 1], NCLS) for row in range(CF)]
+    segments += [(turned_small[0:1], NCLS)]
+    lane = 0
+    for values, length in segments:
+        taken = 0
+        while taken < length:
+            row, col = lane // BS, lane % BS
+            part = min(length - taken, BS - col)
+            rows_ref[at + row : at + row + 1, col : col + part] = values[:, taken : taken + part]
+            taken += part
+            lane += part
+    norm = jnp.sqrt(jnp.sum(jnp.sum(square, 0, keepdims=True), 1, keepdims=True))
+    clip = clip_value / jnp.maximum(norm, clip_value)
+    lanes_of = lax.broadcasted_iota(jnp.int32, (8, BS), 1)
+    norm_ref[...] = jnp.where(lanes_of == 0, norm, clip)
+
+
+def unpack_aux(gathered):
+    whole = pl.BlockSpec(memory_space=pltpu.VMEM)
+    return pl.pallas_call(
+        unpack_kernel,
+        out_shape=(
+            jax.ShapeDtypeStruct((FLAT_ROWS, BS), jnp.float32),
+            jax.ShapeDtypeStruct((8, BS), jnp.float32),
+        ),
+        in_specs=[whole],
+        out_specs=(whole, whole),
+        scratch_shapes=[pltpu.VMEM((BS, BS), jnp.float32)],
+        compiler_params=pltpu.CompilerParams(vmem_limit_bytes=32 * MIB),
+        cost_estimate=pl.CostEstimate(flops=0, bytes_accessed=7 * MIB, transcendentals=0),
+        name="unpack_aux",
+    )(gathered)
+
+
 def layer_norm(values):
     center = values - jnp.mean(values, -1, keepdims=True)
     spread = jnp.mean(center * center, -1, keepdims=True)
@@ -1288,25 +1455,59 @@
     return inverse * (scaled - mean - normal * along)
 
 
-def shampoo_step(blocks, grads, stat_pair, root_pair, moment, veloc):
-    stat_left = beta_stat * stat_pair[0] + (1 - beta_stat) * jnp.einsum(
-        "cij,ckj->cik", grads, grads, precision=HIGHEST
-    )
-    stat_right = beta_stat * stat_pair[1] + (1 - beta_stat) * jnp.einsum(
-        "cji,cjk->cik", grads, grads, precision=HIGHEST
-    )
-    moment_new = beta_one * moment + (1 - beta_one) * grads
-    veloc_new = beta_two * veloc + (1 - beta_two) * grads * grads
-    moment_hat = moment_new / (1 - beta_one**STEP)
-    adam_dir = moment_hat / (jnp.sqrt(veloc_new / (1 - beta_two**STEP)) + 1e-08)
-    left_side = jnp.einsum("cij,cjk->cik", root_pair[0], moment_hat, precision=HIGHEST)
-    precond = jnp.einsum("cij,cjk->cik", left_side, root_pair[1], precision=HIGHEST)
-    ratio = jnp.sqrt(
-        (jnp.mean(adam_dir * adam_dir, (-2, -1), keepdims=True) + 1e-06)
-        / (jnp.mean(precond * precond, (-2, -1), keepdims=True) + 1e-06)
-    )
-    block_new = blocks - learn_rate * (precond * ratio + decay_rate * blocks)
-    return (block_new, jnp.stack([stat_left, stat_right]), moment_new, veloc_new)
+def shampoo_kernel(per_step, clip_ref, g_ref, b_ref, s_ref, r_ref, m_ref, v_ref, nb_ref, ns_ref, nm_ref, nv_ref):
+    def exact(a, b, dims):
+        return lax.dot_general(
+            a, b, (dims, ((), ())), precision=HIGHEST, preferred_element_type=jnp.float32
+        )
+
+    def mean_square(values):
+        total = jnp.sum(jnp.sum(values * values, 0, keepdims=True), 1, keepdims=True)
+        return total * (1.0 / (BS * BS))
+
+    for i in range(per_step):
+        grads = g_ref[i * BS : (i + 1) * BS] * clip_ref[0, 0]
+        ns_ref[0, i] = beta_stat * s_ref[0, i] + (1 - beta_stat) * exact(grads, grads, ((1,), (1,)))
+        ns_ref[1, i] = beta_stat * s_ref[1, i] + (1 - beta_stat) * exact(grads, grads, ((0,), (0,)))
+        moment = beta_one * m_ref[i] + (1 - beta_one) * grads
+        velocity = beta_two * v_ref[i] + (1 - beta_two) * grads * grads
+        nm_ref[i] = moment
+        nv_ref[i] = velocity
+        hat = moment / (1 - beta_one**STEP)
+        adam = hat / (jnp.sqrt(velocity / (1 - beta_two**STEP)) + 1e-08)
+        left = exact(r_ref[0, i], hat, ((1,), (0,)))
+        precond = exact(left, r_ref[1, i], ((1,), (0,)))
+        ratio = jnp.sqrt((mean_square(adam) + 1e-06) / (mean_square(precond) + 1e-06))
+        blocks = b_ref[i]
+        nb_ref[i] = blocks - learn_rate * (precond * ratio + decay_rate * blocks)
+
+
+def shampoo_step(clip, owned, blocks, stat_pair, root_pair, moment, velocity):
+    number = blocks.shape[0]
+    per_step = 3
+    one = pl.BlockSpec((per_step, BS, BS), lambda i: (i, 0, 0))
+    pair = pl.BlockSpec((2, per_step, BS, BS), lambda i: (0, i, 0, 0))
+    single = jax.ShapeDtypeStruct((number, BS, BS), jnp.float32)
+    return pl.pallas_call(
+        functools.partial(shampoo_kernel, per_step),
+        grid=(number // per_step,),
+        out_shape=(single, jax.ShapeDtypeStruct((2, number, BS, BS), jnp.float32), single, single),
+        in_specs=[
+            pl.BlockSpec(memory_space=pltpu.SMEM),
+            pl.BlockSpec((per_step * BS, BS), lambda i: (i, 0)),
+            one,
+            pair,
+            pair,
+            one,
+            one,
+        ],
+        out_specs=(one, pair, one, one),
+        compiler_params=pltpu.CompilerParams(vmem_limit_bytes=32 * MIB),
+        cost_estimate=pl.CostEstimate(
+            flops=number * 8 * BS**3 * 6, bytes_accessed=number * 12 * BS * BS * 4, transcendentals=0
+        ),
+        name="shampoo",
+    )(clip.reshape(1, 1), owned, blocks, stat_pair, root_pair, moment, velocity)
 
 
 def adam_step(param, grads, moment, veloc):
@@ -1344,6 +1545,11 @@
     (w_embed,) = unblock(gathered, True)
     w_qkv, w_proj, w_up, w_down, w_deconv = unblock(gathered, False)
 
+    def columns(array, which, width, start):
+        return lax.dynamic_slice_in_dim(array, which * width + start, width - start, 1)
+
+    down_start = 2 * FF // MP // 3
+
     other_rows = lax.dynamic_slice_in_dim(patches, (1 - part) * NTOK, NTOK, 0)
     own_rows = lax.dynamic_slice_in_dim(patches, part * NTOK, NTOK, 0)
     received = swap_mp(dot_nn(other_rows, w_embed))
@@ -1358,31 +1564,23 @@
         [q_bias[:HALF], nothing, v_bias[:HALF], q_bias[HALF:], nothing, v_bias[HALF:]]
     )
     qkv = (dot_nn(normed_one, w_qkv) + qkv_bias).astype(jnp.bfloat16)
+    zero_stream = stream_zero.astype(jnp.bfloat16)
+    zero_half = swap_mp(columns(zero_stream, 1 - part, HALF, 0))
     mixed, lse = attention_forward(qkv)
+    mixed, zero_half = lax.optimization_barrier((mixed, zero_half))
     stream_one = stream_zero + dot_nn(mixed, w_proj) + pieces["proj_bias"]
+    one_stream = stream_one.astype(jnp.bfloat16)
+    one_half = swap_mp(columns(one_stream, 1 - part, HALF, 0))
     normal_two, inverse_two = layer_norm(stream_one)
     normed_two = (normal_two * gain[1] + shift[1]).astype(jnp.bfloat16)
     hidden = dot_nn(normed_two, w_up) + pieces["up_bias"]
     active_value, hidden_slope = gelu_and_slope(hidden)
     active = active_value.astype(jnp.bfloat16)
     stream_two = stream_one + dot_nn(active, w_down) + pieces["down_bias"]
-    streams = [s.astype(jnp.bfloat16) for s in (stream_zero, stream_one, stream_two)]
+    streams = [zero_stream, one_stream, stream_two.astype(jnp.bfloat16)]
     stacked = jnp.concatenate([halves(s)[m] for m in range(MP) for s in streams], 1)
     up_t = dot(w_deconv, stacked, ((0,), (1,)))
-
-    def columns(array, which, width, start):
-        return lax.dynamic_slice_in_dim(array, which * width + start, width - start, 1)
-
-    down_start = 2 * FF // MP // 3
-    stacked_pair = jnp.concatenate(
-        [columns(stacked, part, 3 * HALF, 0), swap_mp(columns(stacked, 1 - part, 3 * HALF, 0))]
-    )
-    active_pair = jnp.concatenate(
-        [
-            columns(active, part, FF // MP, down_start),
-            swap_mp(columns(active, 1 - part, FF // MP, down_start)),
-        ]
-    )
+    active_other = swap_mp(columns(active, 1 - part, FF // MP, down_start))
 
     conv_weight = pieces["conv_weight"].astype(jnp.bfloat16).reshape(27, DEC, CF)
     conv_low = conv_weight.transpose(0, 2, 1).reshape(27 * CF, DEC)
@@ -1403,7 +1601,11 @@
         grid_labels,
         batch,
     )
-    sums = sum_sums(sums)
+    conv_in, one_half = lax.optimization_barrier((conv_in, one_half))
+    sums, two_stream, active_other = lax.optimization_barrier(
+        (sum_sums(sums), streams[2], active_other)
+    )
+    two_half = swap_mp(columns(two_stream, 1 - part, HALF, 0))
     gu_t, conv_grad, head_grad, small, deconv_bias_grad = decoder_backward(
         all_crops,
         sums,
@@ -1419,7 +1621,7 @@
     )
     loss_value = small[0, 2]
 
-    gu_pair = jnp.concatenate([gu_t, swap_mp(gu_t)], 1)
+    gu_other = swap_mp(gu_t)
     stacked_back = dot(gu_t, w_deconv, ((0,), (1,)))
     back_zero_s, back_one_s, back_two = [
         jnp.concatenate([stacked_back[:, (3 * m + s) * HALF : (3 * m + s + 1) * HALF] for m in range(MP)], 1)
@@ -1427,7 +1629,7 @@
     ]
     grad_down_bias = jnp.sum(back_two, 0)
     two_low = back_two.astype(jnp.bfloat16)
-    two_pair = jnp.concatenate([two_low, swap_mp(two_low)])
+    two_other = swap_mp(two_low)
     back_hidden = (hidden_slope * dot_nt(two_low, w_down)).astype(jnp.bfloat16)
     grad_up_bias = jnp.sum(back_hidden.astype(jnp.float32), 0)
     back_normed_two = dot_nt(back_hidden, w_up)
@@ -1448,24 +1650,25 @@
     back_normed_one = dot_nt(back_qkv, w_qkv)
     grad_gain_one = jnp.sum(back_normed_one * normal_one, 0)
     grad_shift_one = jnp.sum(back_normed_one, 0)
+    back_normed_one, two_half, gu_other, two_other = lax.optimization_barrier(
+        (back_normed_one, two_half, gu_other, two_other)
+    )
     back_zero = (
         back_one + back_zero_s + layer_norm_back(back_normed_one, normal_one, inverse_one, gain[0])
     )
     zero_low = back_zero.astype(jnp.bfloat16)
     other_low = swap_mp(zero_low)
-    zero_pair = jnp.where(
-        part == 0,
-        jnp.concatenate([zero_low, other_low]),
-        jnp.concatenate([other_low, zero_low]),
-    )
 
     fast = fast_mesh()
     depth = CHUNK if fast else BLOCK_ROWS
+    stacked_own = jnp.concatenate([columns(stream, part, HALF, 0) for stream in streams], 1)
+    stacked_other = jnp.concatenate([zero_half, one_half, two_half], 1)
+    active_own = columns(active, part, FF // MP, down_start)
     final_grads = grad_blocks(
-        stacked_pair, gu_pair, 1, 9, 8, 3, 24, True, False, None, "grad_deconv", 4, BLOCK_ROWS, True
+        [stacked_own, stacked_other], [gu_t, gu_other], 1, 9, 8, 3, 24, True, False, None, "grad_deconv", 4, BLOCK_ROWS, True
     )
     final_grads = grad_blocks(
-        active_pair, two_pair, 1, 4, 6, 4, 0, True, False, final_grads, "grad_down_last", 4, BLOCK_ROWS
+        [active_own, active_other], [two_low, two_other], 1, 4, 6, 4, 0, True, False, final_grads, "grad_down_last", 4, BLOCK_ROWS
     )
     rest_grads = None
     for name, x, g, rows, per_row, step_rows, start, split_x, split_g, stride in (
@@ -1475,81 +1678,75 @@
         ("grad_qkv", normed_one, back_qkv, 6, 9, 3, 0, False, True, None),
     ):
         rest_grads = grad_blocks(
-            x, g, MP, rows, per_row, step_rows, start, split_x, split_g, rest_grads, name, 8, depth,
+            [x], [g], MP, rows, per_row, step_rows, start, split_x, split_g, rest_grads, name, 8, depth,
             x_stride=stride,
         )
     first_grads = grad_blocks(
-        patches, zero_pair, 1, 16, 6, 4, 0, False, False, None, "grad_embed", 4, BLOCK_ROWS
-    )
-    vectors = jnp.concatenate(
-        [
-            jnp.stack(
-                [
-                    grad_gain_one,
-                    grad_gain_two,
-                    grad_shift_one,
-                    grad_shift_two,
-                    grad_query_bias,
-                    grad_value_bias,
-                    grad_proj_bias,
-                    grad_down_bias,
-                ]
-            ),
-            jnp.pad(grad_up_bias.reshape(FF // D, D), ((0, 8 - FF // D), (0, 0))),
-        ]
-    )
-    wide = jnp.concatenate([back_zero, vectors])
-    tall = wide.shape[0]
-    aux_rows = jnp.concatenate(
-        [wide[:, j * BS : (j + 1) * BS] for j in range(D // BS)]
-        + [conv_grad, jnp.pad(head_grad, ((0, 0), (0, BS - CF))), small, deconv_bias_grad]
-    )
+        [own_rows, other_rows], [zero_low, other_low], 1, 16, 6, 4, 0, False, False, None, "grad_embed", 4, BLOCK_ROWS
+    )
+    vectors = [
+        grad_gain_one,
+        grad_gain_two,
+        grad_shift_one,
+        grad_shift_two,
+        grad_query_bias,
+        grad_value_bias,
+        grad_proj_bias,
+        grad_down_bias,
+    ]
     if fast:
-        room = 8 * MP * AUX_ROWS
-        placed = jnp.pad(aux_rows, ((0, room - aux_rows.shape[0]), (0, 0)))
-        placed = placed.reshape(MP, 8, AUX_ROWS, BS)
-        rest_grads = lax.dynamic_update_slice(rest_grads, placed, (0, 0, BLOCK_ROWS, 0))
-        reduced, squares = reduce_to_owners(
+        head_wide = jnp.pad(head_grad, ((0, 0), (0, BS - CF)))
+        rest_grads = pack_aux(
+            back_zero, vectors, grad_up_bias, conv_grad, head_wide, small, deconv_bias_grad, rest_grads
+        )
+        owned, squares = reduce_to_owners(
             rest_grads.reshape(MP, 2, 2, 2, CHUNK, BS),
             first_grads.reshape(2, 2, BLOCK_ROWS, BS),
             final_grads.reshape(2, 2, BLOCK_ROWS, BS),
         )
-        owned = reduced[:BLOCK_ROWS].reshape(24, BS, BS)
         gathered_aux = gather_all(
-            jnp.concatenate([reduced[BLOCK_ROWS:], squares]), 1, False, 4, "gather_aux"
+            jnp.concatenate([owned[BLOCK_ROWS:], squares]),
+            ((0, AUX_ROWS), (AUX_ROWS, 8)),
+            1,
+            False,
+            (0,),
+            4,
+            "gather_aux",
         )
-        block_square = jnp.sum(gathered_aux[:, :, AUX_ROWS:])
-        aux_sum = gathered_aux[:, 4:12, :AUX_ROWS].reshape(-1, BS)
+        in_rows, norm_clip = unpack_aux(gathered_aux)
+        aux_total = in_rows.reshape(-1)[:NAUX]
+        grad_norm, clip_scale = norm_clip[0, 0], norm_clip[0, 1]
     else:
         owned = reduce_plain(rest_grads.reshape(MP, -1, BS, BS), first_grads, final_grads)
-        aux_sum = lax.psum(aux_rows, ("dp", "mp"))
+        owned = owned.reshape(-1, BS)
+        positions_sum, small_sum = lax.psum(
+            (
+                back_zero,
+                jnp.concatenate(
+                    vectors[:7]
+                    + [
+                        grad_up_bias,
+                        grad_down_bias,
+                        deconv_bias_grad[:, 0],
+                        conv_grad.reshape(27, CF, DEC).transpose(0, 2, 1).reshape(-1),
+                        small[:, 1],
+                        head_grad[:, :NCLS].reshape(-1),
+                        small[:NCLS, 0],
+                    ]
+                ),
+            ),
+            ("dp", "mp"),
+        )
+        aux_total = jnp.concatenate(
+            [positions_sum.reshape(-1), jnp.sum(positions_sum, 0), small_sum]
+        )
         block_square = lax.psum(jnp.sum(owned * owned), ("dp", "mp"))
-    wide_sum = jnp.concatenate([aux_sum[j * tall : (j + 1) * tall] for j in range(D // BS)], 1)
-    after = D // BS * tall
-    conv_sum = aux_sum[after : after + 27 * CF]
-    head_sum = aux_sum[after + 27 * CF : after + 28 * CF]
-    small_sum = aux_sum[after + 28 * CF : after + 29 * CF]
-    deconv_sum = aux_sum[after + 29 * CF : after + 29 * CF + DEC, 0]
-    positions_sum = wide_sum[:NTOK]
-    aux_total = jnp.concatenate(
-        [
-            positions_sum.reshape(-1),
-            jnp.sum(positions_sum, 0),
-            wide_sum[NTOK : NTOK + 7].reshape(-1),
-            wide_sum[NTOK + 8 : NTOK + 8 + FF // D].reshape(-1),
-            wide_sum[NTOK + 7],
-            deconv_sum,
-            conv_sum.reshape(27, CF, DEC).transpose(0, 2, 1).reshape(-1),
-            small_sum[:, 1],
-            head_sum[:, :NCLS].reshape(-1),
-            small_sum[:NCLS, 0],
-        ]
-    )
-    grad_norm = jnp.sqrt(block_square + jnp.sum(aux_total * aux_total))
-    clip_scale = clip_value / jnp.maximum(grad_norm, clip_value)
+        grad_norm = jnp.sqrt(block_square + jnp.sum(aux_total * aux_total))
+        clip_scale = clip_value / jnp.maximum(grad_norm, clip_value)
     block_new, stat_new, moment_new, veloc_new = shampoo_step(
+        clip_scale,
+        owned,
         blocks[0, 0],
-        owned * clip_scale,
         statistics[:, 0, 0],
         roots[:, 0, 0],
         moments[0, 0],

time: 605 us -> 539 us (0.89)
  local copies, waits for them, and re-layouts: 98.4 us -> 57.7 us
  other arithmetic: 31.2 us -> 15.2 us
  Pallas kernels: 388 us -> 402 us
  matrix products: 51 us -> 38.7 us
  waiting for transfers between devices: 13.7 us -> 4.48 us
    concatenate x5 -> x0, local copies, waits for them, and re-layouts: 18.6 us -> none  [the longest x1 12.7 us: local(): jnp.concatenate([positions_sum.reshape(-1), jnp.sum(positions_sum, 0), wi...]
    pallas_call x2 -> x5, Pallas kernels: 130 us -> 144 us  [the longest x2 126 us: gather_all(): pl.pallas_call(functools.partial(gather_kernel, parts, by_x, skip, middle...]
    unnamed x202 -> x185, local copies, waits for them, and re-layouts: 44.6 us -> 32.7 us
    dot_general x4 -> x0, matrix products: 10 us -> none  [the longest x1 3.41 us: shampoo_step(): jnp.einsum('cij,ckj->cik', grads, grads, precision=HIGHEST)]
    ppermute x6 -> x8, waiting for transfers between devices: 13.7 us -> 4.48 us  [swap_mp(): return lax.ppermute(values, 'mp', [(0, 1), (1, 0)])]
  transfers between devices with their start and end apart: 6 -> 8, of which waited for: 1 -> 1; matrix products, arithmetic and copies ran while one was open for 12% -> 8% of each run, Pallas kernels for 8% -> 14%
where the time goes in v4:
time: 539 us; the launch traced here: 530 us
  Pallas kernels  402 us (75%)
  local copies, waits for them, and re-layouts  57.7 us (11%)
  matrix products  38.7 us (7%)
  other arithmetic  15.2 us (3%)
  starting transfers between devices  9.32 us (2%)
    pallas_call x1, Pallas kernels, reduce_to_owners(): pl.pallas_call(reduce_kernel, out_shape=(jax.ShapeDtypeStruct((CHUNK, BS)...  173 us
    pallas_call x2, Pallas kernels, gather_all(): pl.pallas_call(functools.partial(gather_kernel, parts, by_x, skip, middle...  126 us
    dot_general x12, matrix products, dot(): lax.dot_general(a, b, (dims, ((), ())), preferred_element_type=jnp.float32)  38.7 us
    unnamed x185, local copies, waits for them, and re-layouts  32.7 us
    pallas_call x7, Pallas kernels, grad_blocks(): pl.pallas_call(functools.partial(blocks_kernel, first_block, per_row, ste...  31.5 us
    pallas_call x1, Pallas kernels, shampoo_step(): pl.pallas_call(functools.partial(shampoo_kernel, per_step), grid=(number...  15.2 us
    pallas_call x1, Pallas kernels, sum_sums(): pl.pallas_call(functools.partial(sum_kernel, devices), out_shape=jax.Shap...  13.5 us
    pallas_call x1, Pallas kernels, attention_backward(): pl.pallas_call(attention_backward_kernel, grid=(6,), out_shape=(jax.Shape...  12.5 us
  transfers between devices with their start and end apart: 8, of which 1 were waited for; matrix products, arithmetic and copies ran while one was open for 8% of the time, Pallas kernels for 14%

profile of v4, /device:TPU:0, one launch (start us, length us, event | category | flops | bytes accessed | tf_op | source)
XLA Modules:
  0.0 530.4 jit_solution(6049741197638019699)
XLA Ops:
  0.6 1.5 convert_element_type.60
  2.2 100.6 %gather_weights.1 = bf16[2,16,3072,128]{3,2,1,0:T(8,128)(2,1)} custom-call(bf16[3072,128]{1,0:T(8,128)(2,1)S(1)} %bitcast.67), custom_call_target="tpu_custom_call" | custom-call | bytes 50331648 | tf_op jit(solution)/shard_map/gather_weights/pallas_call | solution.py:635
  102.8 2.1 unblock_embedding.1
  104.9 1.7 copy-done.11
  106.5 2.8 constant_dynamic-slice_fusion.9
  109.7 2.9 fusion.23
  114.4 9.5 %unblock.1 = (bf16[768,2304]{1,0:T(8,128)(2,1)S(1)}, bf16[768,768]{1,0:T(8,128)(2,1)S(1)}, bf16[768,3072]{1,0:T(8,128)(2,1)S(1)}, bf16[3072,768]{1,0:T(8,128)(2,1)S(1)}, bf16[2304,1024]{1,0:T(8,128)(2,1)S(1)}) custom-call(bf16[2,384,128,128]{3,2,1,0:T(8,128)(2,1)} %bitcast.87), custom_call_target="tpu_custom_call" | custom-call | bytes 39845888 | tf_op jit(solution)/shard_map/unblock/pallas_call | solution.py:1106
  123.9 2.1 copy-done.38
  126.1 2.1 copy-done.39
  128.2 2.1 copy-done.40
  130.3 1.8 copy-done.41
  133.8 1.6 convert.7
  136.3 2.8 reshape.167
  142.2 2.0 reshape.173
  144.2 2.9 copy.35
  152.0 4.7 fusion.21
  157.9 1.6 collective-permute-start.1
  159.4 2.0 fusion.6.qkv_q.qkv_k.qkv_v
  161.5 9.2 %attention_forward.1 = (bf16[512,768]{1,0:T(8,128)(2,1)S(1)}, f32[6,2,512]{2,1,0:T(2,128)S(1)}) custom-call(bf16[512,2304]{1,0:T(8,128)(2,1)S(1)} %fusion.6.qkv_q.qkv_k.qkv_v, bf16[512,2304]{1,0:T(8,128)(2,1)S(1)} %fusion.6.qkv_q.qkv_k.qkv_v, bf16[512,2304]{1,0:T(8,128)(2,1)S(1)} %fusion.6.qkv_q.qkv_k.qkv_v), custom_call_target="tpu_custom_call" | custom-call | flops 805306368 | bytes 3145728 | tf_op jit(solution)/shard_map/attention_forward/pallas_call | solution.py:137
  173.8 5.4 %multiply_convert_fusion = (bf16[512,3072]{1,0:T(8,128)(2,1)S(1)}, f32[512,3072]{1,0:T(8,128)}) fusion(f32[3072]{0:T(1024)S(1)} %slice.171, bf16[512,768]{1,0:T(8,128)(2,1)S(1)} %get-tuple-element.140.refs_0_, bf16[768,3072]{1,0:T(8,128)(2,1)S(1)} %bitcast.76), kind=kOutput, calls=%fused_computation.8 | convolution fusion | flops 2425356288 | bytes 14954496 | tf_op jit(solution)/shard_map/dot_general | solution.py:43
  179.3 2.6 add_convert_fusion
  187.9 2.6 convolution_bitcast_fusion.up_ref
  190.6 4.3 decoder_forward.1
  199.9 13.5 %sum_sums.1.sums_ref = f32[16,128]{1,0:T(8,128)} custom-call(f32[16,128]{1,0:T(8,128)} %copy-done.35), custom_call_target="tpu_custom_call" | custom-call | tf_op jit(solution)/shard_map/sum_sums/pallas_call | solution.py:1261
  213.4 1.5 pad_maximum_fusion.1.refs_0_
  218.4 2.2 decoder_backward.1
  220.6 5.1 fusion.24
  225.6 1.7 collective-permute-start.5
  229.5 6.7 %convert_reduce_fusion = (f32[3072]{0:T(1024)S(1)}, bf16[512,3072]{1,0:T(8,128)(2,1)S(1)}) fusion(bf16[512,768]{1,0:T(8,128)(2,1)S(1)} %fusion.11.refs_1_, bf16[3072,768]{1,0:T(8,128)(2,1)S(1)} %bitcast.82, f32[512,3072]{1,0:T(8,128)} %get-tuple-element.162, f32[3072]{0:T(1024)S(1)} %copy-done.75), kind=kOutput, calls=%fused_computation.7 | convolution fusion | flops 2436363264 | bytes 14966784 | tf_op jit(solution)/shard_map/dot_general | solution.py:43
  236.2 3.0 multiply_reduce_fusion
  242.2 12.5 %attention_backward.1 = (bf16[512,768]{1,0:T(8,128)(2,1)S(1)}, bf16[512,768]{1,0:T(8,128)(2,1)S(1)}, bf16[512,768]{1,0:T(8,128)(2,1)S(1)}) custom-call(bf16[512,2304]{1,0:T(8,128)(2,1)S(1)} %fusion.6.qkv_q.qkv_k.qkv_v, bf16[512,2304]{1,0:T(8,128)(2,1)S(1)} %fusion.6.qkv_q.qkv_k.qkv_v, bf16[512,2304]{1,0:T(8,128)(2,1)S(1)} %fusion.6.qkv_q.qkv_k.qkv_v, ...), custom_call_target="tpu_custom_call" | custom-call | flops 2013265920 | bytes 5505024 | tf_op jit(solution)/shard_map/attention_backward/pallas_call | solution.py:161
  255.1 1.6 copy-done.43
  256.8 2.0 fusion.25
  261.2 4.5 grad_down.1.refs_2_
  265.7 5.9 %grad_up.1.refs_2_ = f32[2,8,3328,128]{3,2,1,0:T(8,128)} custom-call(bf16[512,768]{1,0:T(8,128)(2,1)S(1)} %copy-done.10, bf16[512,3072]{1,0:T(8,128)(2,1)S(1)} %get-tuple-element.165.refs_1_, f32[2,8,3328,128]{3,2,1,0:T(8,128)} %grad_down.1.refs_2_), custom_call_target="tpu_custom_call", output_to_operand_aliasing={{}: (2, {})} | custom-call | flops 2415919104 | bytes 9437184 | tf_op jit(solution)/shard_map/grad_up/pallas_call | solution.py:1179
  271.7 4.5 collective-permute-done.4
  277.5 1.7 collective-permute-start.7
  279.2 2.2 grad_proj.1.refs_2_
  281.4 5.1 grad_qkv.1.refs_13_
  286.6 1.7 pack_aux.1
  289.5 4.9 grad_deconv.1.refs_4_
  294.4 2.4 grad_down_last.1
  296.8 6.4 %grad_embed.1 = f32[1,4,3072,128]{3,2,1,0:T(8,128)S(1)} custom-call(bf16[512,2048]{1,0:T(8,128)(2,1)S(1)} %copy-done.3, bf16[512,768]{1,0:T(8,128)(2,1)S(1)} %get-tuple-element.118.refs_1_, bf16[512,2048]{1,0:T(8,128)(2,1)S(1)} %copy-done.5, bf16[512,768]{1,0:T(8,128)(2,1)S(1)} %collective-permute-done.7.refs_3_), custom_call_target="tpu_custom_call" | custom-call | flops 3221225472 | bytes 6291456 | tf_op jit(solution)/shard_map/grad_embed/pallas_call | solution.py:1179
  303.3 2.6 copy-done.1
  305.9 172.9 %reduce_to_owners.1 = (f32[3328,128]{1,0:T(8,128)}, f32[8,128]{1,0:T(8,128)}) custom-call(f32[2,2,2,2,3328,128]{5,4,3,2,1,0:T(8,128)} %bitcast.85, f32[2,2,3072,128]{3,2,1,0:T(8,128)} %bitcast.65, f32[2,2,3072,128]{3,2,1,0:T(8,128)} %bitcast.64), custom_call_target="tpu_custom_call" | custom-call | bytes 104857600 | tf_op jit(solution)/shard_map/reduce_to_owners/pallas_call | solution.py:982
  480.5 25.5 %gather_aux.1.sums_ref = f32[2,16,264,128]{3,2,1,0:T(8,128)S(1)} custom-call(f32[264,128]{1,0:T(8,128)S(1)} %pad_maximum_fusion.3.in_ref), custom_call_target="tpu_custom_call" | custom-call | bytes 4325376 | tf_op jit(solution)/shard_map/gather_aux/pallas_call | solution.py:635
  508.1 4.1 multiply_subtract_fusion
  514.7 15.2 %shampoo.1 = (f32[24,128,128]{2,1,0:T(8,128)}, f32[2,24,128,128]{3,2,1,0:T(8,128)}, f32[24,128,128]{2,1,0:T(8,128)}, f32[24,128,128]{2,1,0:T(8,128)}) custom-call(f32[1,1]{1,0:T(1,128)} %get-tuple-element.153.clip_ref, f32[3328,128]{1,0:T(8,128)S(1)} %copy-done.18, f32[24,128,128]{2,1,0:T(8,128)S(1)} %bitcast.66, f32[2,24,128,128]{3,2,1,0:T(8,128)S(1)} %bitcast.68, ...), custom_call_target="tpu_custom_call" | custom-call | flops 2415919104 | bytes 18874368 | tf_op jit(solution)/shard_map/shampoo/pallas_call | solution.py:1491
  (262 shorter events, 47.2 us)
Async XLA Ops:
  109.3 42.7 %copy-start.2 = (bf16[512,2048]{1,0:T(8,128)(2,1)}, bf16[512,2048]{1,0:T(8,128)(2,1)S(1)}, u32[]{:S(2)}) copy-start(bf16[512,2048]{1,0:T(8,128)(2,1)S(1)} %get-tuple-element.128.refs_0_) | copy-start | bytes 6291460
  112.6 39.4 %collective-permute-start = (f32[512,768]{1,0:T(8,128)}, f32[512,768]{1,0:T(8,128)}, u32[]{:S(2)}, u32[]{:S(2)}) collective-permute-start(f32[512,768]{1,0:T(8,128)} %fusion.23), channel_id=1, source_target_pairs={{0,1},{1,0},{2,3},{3,2},{4,5},{5,4},{6,7},{7,6},{8,9},{9,8},{10,11... | collective-permute-start | bytes 4718600 | tf_op jit(solution)/shard_map/ppermute | solution.py:1277
  133.8 39.9 %copy-start.74 = (f32[3072]{0:T(1024)}, f32[3072]{0:T(1024)S(1)}, u32[]{:S(2)}) copy-start(f32[3072]{0:T(1024)S(1)} %slice.171) | copy-start | bytes 36868
  152.0 5.1 copy-start.61
  152.0 21.0 %copy-start.65 = (f32[768]{0:T(1024)}, f32[768]{0:T(1024)S(1)}, u32[]{:S(2)}) copy-start(f32[768]{0:T(1024)S(1)} %get-tuple-element.134) | copy-start | bytes 9220
  156.7 15.0 %copy-start.47 = (f32[512,768]{1,0:T(8,128)}, f32[512,768]{1,0:T(8,128)S(1)}, u32[]{:S(2)}) copy-start(f32[512,768]{1,0:T(8,128)S(1)} %get-tuple-element.158) | copy-start | bytes 4718596
  157.9 12.9 %collective-permute-start.1 = (bf16[512,384]{1,0:T(8,128)(2,1)S(1)}, bf16[512,384]{1,0:T(8,128)(2,1)S(1)}, u32[]{:S(2)}, u32[]{:S(2)}) collective-permute-start(bf16[512,384]{1,0:T(8,128)(2,1)S(1)} %get-tuple-element.151), channel_id=1, source_target_pairs={{0,1},{1,0},{2,3},{3,2},{4,5},{5,4},{6,7},{7,6},{8,9},{9,8},{10,11... | collective-permute-start | bytes 1179656 | tf_op jit(solution)/shard_map/ppermute | solution.py:1277
  161.5 10.3 %copy-start.45 = (bf16[768,768]{1,0:T(8,128)(2,1)S(1)}, bf16[768,768]{1,0:T(8,128)(2,1)}, u32[]{:S(2)}) copy-start(bf16[768,768]{1,0:T(8,128)(2,1)} %copy-done.44) | copy-start | bytes 3538948
  161.5 12.3 %slice-start = ((s8[4718592]{0:T(1024)(128)(4,1)}), s8[4194304]{0:T(1024)(128)(4,1)S(1)}, s32[]{:S(2)}) async-start(s8[4718592]{0:T(1024)(128)(4,1)} %bitcast.75), calls=%async_computation | async-start | bytes 8388608
  172.6 6.6 %copy-start.51 = (f32[512,768]{1,0:T(8,128)}, f32[512,768]{1,0:T(8,128)S(1)}, u32[]{:S(2)}) copy-start(f32[512,768]{1,0:T(8,128)S(1)} %get-tuple-element.160) | copy-start | bytes 4718596
  173.0 6.3 %slice-start.4 = ((s8[4718592]{0:T(1024)(128)(4,1)}), s8[4194304]{0:T(1024)(128)(4,1)S(1)}, s32[]{:S(2)}) async-start(s8[4718592]{0:T(1024)(128)(4,1)} %bitcast.79), calls=%async_computation.4 | async-start | bytes 8388608
  173.7 5.6 %copy-start.9 = (bf16[512,768]{1,0:T(8,128)(2,1)}, bf16[512,768]{1,0:T(8,128)(2,1)S(1)}, u32[]{:S(2)}) copy-start(bf16[512,768]{1,0:T(8,128)(2,1)S(1)} %get-tuple-element.140.refs_0_) | copy-start | bytes 2359300
  173.8 5.5 %slice-start.5 = ((s8[4718592]{0:T(1024)(128)(4,1)}), s8[524288]{0:T(1024)(128)(4,1)S(1)}, s32[]{:S(2)}) async-start(s8[4718592]{0:T(1024)(128)(4,1)} %bitcast.79), calls=%async_computation.5 | async-start | bytes 1048576
  173.8 14.1 %slice-start.8 = ((s8[4718592]{0:T(1024)(128)(4,1)}), s8[524288]{0:T(1024)(128)(4,1)S(1)}, s32[]{:S(2)}) async-start(s8[4718592]{0:T(1024)(128)(4,1)} %bitcast.83), calls=%async_computation.8 | async-start | bytes 1048576
  179.2 5.6 %copy-start.7 = (bf16[512,3072]{1,0:T(8,128)(2,1)}, bf16[512,3072]{1,0:T(8,128)(2,1)S(1)}, u32[]{:S(2)}) copy-start(bf16[512,3072]{1,0:T(8,128)(2,1)S(1)} %get-tuple-element.161.refs_0_) | copy-start | bytes 9437188
  179.3 8.6 %slice-start.9 = ((s8[4718592]{0:T(1024)(128)(4,1)}), s8[4194304]{0:T(1024)(128)(4,1)S(1)}, s32[]{:S(2)}) async-start(s8[4718592]{0:T(1024)(128)(4,1)} %bitcast.83), calls=%async_computation.9 | async-start | bytes 8388608
  185.9 29.0 %collective-permute-start.2 = (bf16[512,512]{1,0:T(8,128)(2,1)}, bf16[512,512]{1,0:T(8,128)(2,1)}, u32[]{:S(2)}, u32[]{:S(2)}) collective-permute-start(bf16[512,512]{1,0:T(8,128)(2,1)} %get-tuple-element.131), channel_id=1, source_target_pairs={{0,1},{1,0},{2,3},{3,2},{4,5},{5,4},{6,7},{7,6},{8,9},{9,8},{10,11... | collective-permute-start | bytes 1572872 | tf_op jit(solution)/shard_map/ppermute | solution.py:1277
  187.3 27.6 %collective-permute-start.3 = (bf16[512,384]{1,0:T(8,128)(2,1)}, bf16[512,384]{1,0:T(8,128)(2,1)}, u32[]{:S(2)}, u32[]{:S(2)}) collective-permute-start(bf16[512,384]{1,0:T(8,128)(2,1)} %get-tuple-element.147), channel_id=1, source_target_pairs={{0,1},{1,0},{2,3},{3,2},{4,5},{5,4},{6,7},{7,6},{8,9},{9,8},{10,11... | collective-permute-start | bytes 1179656 | tf_op jit(solution)/shard_map/ppermute | solution.py:1277
  190.6 4.3 copy-start.36
  199.9 15.0 %copy-start.26 = (f32[16,4096]{1,0:T(8,128)S(1)}, f32[16,4096]{1,0:T(8,128)}, u32[]{:S(2)}) copy-start(f32[16,4096]{1,0:T(8,128)} %copy-done.25) | copy-start | bytes 786436
  218.4 10.9 %slice-start.6 = ((s8[4718592]{0:T(1024)(128)(4,1)}), s8[4194304]{0:T(1024)(128)(4,1)S(1)}, s32[]{:S(2)}) async-start(s8[4718592]{0:T(1024)(128)(4,1)} %bitcast.81), calls=%async_computation.6 | async-start | bytes 8388608
  220.5 8.8 %slice-start.7 = ((s8[4718592]{0:T(1024)(128)(4,1)}), s8[524288]{0:T(1024)(128)(4,1)S(1)}, s32[]{:S(2)}) async-start(s8[4718592]{0:T(1024)(128)(4,1)} %bitcast.81), calls=%async_computation.7 | async-start | bytes 1048576
  225.6 50.5 %collective-permute-start.5 = (bf16[1024,512]{1,0:T(8,128)(2,1)S(1)}, bf16[1024,512]{1,0:T(8,128)(2,1)S(1)}, u32[]{:S(2)}, u32[]{:S(2)}) collective-permute-start(bf16[1024,512]{1,0:T(8,128)(2,1)S(1)} %get-tuple-element.65.refs_1_), channel_id=1, source_target_pairs={{0,1},{1,0},{2,3},{3,2},{4,5},{5,4},{6,7},{7,6},{8,9},{9,8},{10,11... | collective-permute-start | bytes 3145736 | tf_op jit(solution)/shard_map/ppermute | solution.py:1277
  228.7 7.4 %slice-start.2 = ((s8[4718592]{0:T(1024)(128)(4,1)}), s8[4194304]{0:T(1024)(128)(4,1)S(1)}, s32[]{:S(2)}) async-start(s8[4718592]{0:T(1024)(128)(4,1)} %bitcast.77), calls=%async_computation.2 | async-start | bytes 8388608
  228.8 47.3 %collective-permute-start.6 = (bf16[512,768]{1,0:T(8,128)(2,1)S(1)}, bf16[512,768]{1,0:T(8,128)(2,1)S(1)}, u32[]{:S(2)}, u32[]{:S(2)}) collective-permute-start(bf16[512,768]{1,0:T(8,128)(2,1)S(1)} %fusion.11.refs_1_), channel_id=1, source_target_pairs={{0,1},{1,0},{2,3},{3,2},{4,5},{5,4},{6,7},{7,6},{8,9},{9,8},{10,11... | collective-permute-start | bytes 2359304 | tf_op jit(solution)/shard_map/ppermute | solution.py:1277
  229.4 6.7 %slice-start.3 = ((s8[4718592]{0:T(1024)(128)(4,1)}), s8[524288]{0:T(1024)(128)(4,1)S(1)}, s32[]{:S(2)}) async-start(s8[4718592]{0:T(1024)(128)(4,1)} %bitcast.77), calls=%async_computation.3 | async-start | bytes 1048576
  229.4 6.7 %copy-start.52 = (f32[512,768]{1,0:T(8,128)S(1)}, f32[512,768]{1,0:T(8,128)}, u32[]{:S(2)}) copy-start(f32[512,768]{1,0:T(8,128)} %copy-done.51) | copy-start | bytes 4718596
  229.5 6.7 %copy-start.66 = (f32[768]{0:T(1024)S(1)}, f32[768]{0:T(1024)}, u32[]{:S(2)}) copy-start(f32[768]{0:T(1024)} %copy-done.65) | copy-start | bytes 9220
  229.5 6.7 %copy-start.70 = (f32[512]{0:T(512)S(1)}, f32[512]{0:T(512)}, u32[]{:S(2)}) copy-start(f32[512]{0:T(512)} %copy-done.69) | copy-start | bytes 6148
  229.5 6.7 %copy-start.72 = (f32[512]{0:T(512)S(1)}, f32[512]{0:T(512)}, u32[]{:S(2)}) copy-start(f32[512]{0:T(512)} %copy-done.71) | copy-start | bytes 6148
  256.8 4.4 copy-start.8
  258.9 17.3 %collective-permute-start.4 = (bf16[512,384]{1,0:T(8,128)(2,1)S(1)}, bf16[512,384]{1,0:T(8,128)(2,1)S(1)}, u32[]{:S(2)}, u32[]{:S(2)}) collective-permute-start(bf16[512,384]{1,0:T(8,128)(2,1)S(1)} %constant_dynamic-slice_fusion.4), channel_id=1, source_target_pairs={{0,1},{1,0},{2,3},{3,2},{4,5},{5,4},{6,7},{7,6},{8,9},{9,8},{10,11... | collective-permute-start | bytes 1179656 | tf_op jit(solution)/shard_map/ppermute | solution.py:1277
  261.2 4.5 copy-start.10
  265.7 10.5 %copy-start.48 = (f32[512,768]{1,0:T(8,128)S(1)}, f32[512,768]{1,0:T(8,128)}, u32[]{:S(2)}) copy-start(f32[512,768]{1,0:T(8,128)} %copy-done.47) | copy-start | bytes 4718596
  265.7 10.4 %copy-start.62 = (f32[768]{0:T(1024)S(1)}, f32[768]{0:T(1024)}, u32[]{:S(2)}) copy-start(f32[768]{0:T(1024)} %copy-done.61) | copy-start | bytes 9220
  265.7 10.4 %copy-start.64 = (f32[512]{0:T(512)S(1)}, f32[512]{0:T(512)}, u32[]{:S(2)}) copy-start(f32[512]{0:T(512)} %copy-done.63) | copy-start | bytes 6148
  265.7 10.4 %copy-start.68 = (f32[512]{0:T(512)S(1)}, f32[512]{0:T(512)}, u32[]{:S(2)}) copy-start(f32[512]{0:T(512)} %copy-done.67) | copy-start | bytes 6148
  271.7 5.3 copy-start.53
  271.7 5.3 copy-start.54
  277.5 19.3 %collective-permute-start.7 = (bf16[512,768]{1,0:T(8,128)(2,1)S(1)}, bf16[512,768]{1,0:T(8,128)(2,1)S(1)}, u32[]{:S(2)}, u32[]{:S(2)}) collective-permute-start(bf16[512,768]{1,0:T(8,128)(2,1)S(1)} %get-tuple-element.118.refs_1_), channel_id=1, source_target_pairs={{0,1},{1,0},{2,3},{3,2},{4,5},{5,4},{6,7},{7,6},{8,9},{9,8},{10,11... | collective-permute-start | bytes 2359304 | tf_op jit(solution)/shard_map/ppermute | solution.py:1277
  289.4 4.9 copy-start.17
  296.8 6.5 %copy-start = (f32[1,4,3072,128]{3,2,1,0:T(8,128)}, f32[1,4,3072,128]{3,2,1,0:T(8,128)S(1)}, u32[]{:S(2)}) copy-start(f32[1,4,3072,128]{3,2,1,0:T(8,128)S(1)} %grad_down_last.1) | copy-start | bytes 18874372
  478.8 29.2 %copy-start.58 = (f32[458878]{0:T(1024)S(1)}, f32[458878]{0:T(1024)}, u32[]{:S(2)}) copy-start(f32[458878]{0:T(1024)} %param.21) | copy-start | bytes 5506540
  508.1 4.1 copy-start.13
  508.1 5.3 %copy-start.14 = (f32[2,1,1,24,128,128]{5,4,3,2,1,0:T(8,128)S(1)}, f32[2,1,1,24,128,128]{5,4,3,2,1,0:T(8,128)}, u32[]{:S(2)}) copy-start(f32[2,1,1,24,128,128]{5,4,3,2,1,0:T(8,128)} %param.16) | copy-start | bytes 9437188
  508.1 5.8 %copy-start.18 = (f32[3328,128]{1,0:T(8,128)S(1)}, f32[3328,128]{1,0:T(8,128)}, u32[]{:S(2)}) copy-start(f32[3328,128]{1,0:T(8,128)} %get-tuple-element.81.g_ref) | copy-start | bytes 5111812
  508.1 6.2 %copy-start.19 = (f32[1,1,24,128,128]{4,3,2,1,0:T(8,128)S(1)}, f32[1,1,24,128,128]{4,3,2,1,0:T(8,128)}, u32[]{:S(2)}) copy-start(f32[1,1,24,128,128]{4,3,2,1,0:T(8,128)} %param.17) | copy-start | bytes 4718596
  508.1 6.6 %copy-start.20 = (f32[1,1,24,128,128]{4,3,2,1,0:T(8,128)S(1)}, f32[1,1,24,128,128]{4,3,2,1,0:T(8,128)}, u32[]{:S(2)}) copy-start(f32[1,1,24,128,128]{4,3,2,1,0:T(8,128)} %param.18) | copy-start | bytes 4718596
  (46 other events, 80.2 us)

commit v5 on v4

--- a/solution.py
+++ b/solution.py
@@ -985,7 +985,7 @@
             jax.ShapeDtypeStruct((CHUNK, BS), jnp.float32),
             jax.ShapeDtypeStruct((8, BS), jnp.float32),
         ),
-        in_specs=[pl.BlockSpec(memory_space=pl.ANY)] * 3,
+        in_specs=[pl.BlockSpec(memory_space=pltpu.HBM)] * 3,
         out_specs=(pl.BlockSpec(memory_space=pltpu.VMEM),) * 2,
         scratch_shapes=[
             room(3, 2, 2, ROWS_N),
@@ -1203,46 +1203,6 @@
     return lax.axis_size("dp") == 4 * LAYERS and lax.axis_size("mp") == MP
 
 
-def sum_kernel(devices, in_ref, out_ref, slots, send_sem, recv_sem):
-    me = lax.axis_index("dp") * MP + lax.axis_index("mp")
-    barrier = pltpu.get_barrier_semaphore()
-
-    def place(k):
-        peer = lax.rem(me + k, devices)
-        return (peer // MP, lax.rem(peer, MP))
-
-    def greet(k, carry):
-        pl.semaphore_signal(barrier, inc=1, device_id=place(k), device_id_type=MESH)
-        return carry
-
-    def copy(k, slot):
-        return remote(in_ref, slots.at[slot], send_sem.at[k], recv_sem.at[slot], place(k))
-
-    lax.fori_loop(1, devices, greet, 0)
-    slots[me] = in_ref[...]
-    pl.semaphore_wait(barrier, devices - 1)
-
-    def push(k, carry):
-        copy(k, me).start()
-        return carry
-
-    def pull(k, carry):
-        copy(k, lax.rem(me + devices - k, devices)).wait_recv()
-        return carry
-
-    def settle(k, carry):
-        copy(k, me).wait_send()
-        return carry
-
-    lax.fori_loop(1, devices, push, 0)
-    lax.fori_loop(1, devices, pull, 0)
-    total = slots[0]
-    for i in range(1, devices):
-        total = total + slots[i]
-    out_ref[...] = total
-    lax.fori_loop(1, devices, settle, 0)
-
-
 def gather_weights(blocks):
     low = blocks.astype(jnp.bfloat16)[0, 0]
     if fast_mesh():
@@ -1251,26 +1211,6 @@
         gathered = lax.all_gather(low, ("dp", "mp"), axis=0, tiled=False)
         gathered = gathered.reshape((-1, MP) + low.shape).swapaxes(0, 1)
     return gathered.reshape(MP, -1, BS, BS)
-
-
-def sum_sums(values):
-    if not fast_mesh():
-        return lax.psum(values, ("dp", "mp"))
-    devices = 4 * LAYERS * MP
-    whole = pl.BlockSpec(memory_space=pltpu.VMEM)
-    return pl.pallas_call(
-        functools.partial(sum_kernel, devices),
-        out_shape=jax.ShapeDtypeStruct(values.shape, jnp.float32),
-        in_specs=[whole],
-        out_specs=whole,
-        scratch_shapes=[
-            pltpu.VMEM((devices,) + values.shape, jnp.float32),
-            pltpu.SemaphoreType.DMA((devices,)),
-            pltpu.SemaphoreType.DMA((devices,)),
-        ],
-        compiler_params=pltpu.CompilerParams(collective_id=3, has_side_effects=True),
-        name="sum_sums",
-    )(values)
 
 
 def swap_mp(values):
@@ -1441,6 +1381,160 @@
     )(gathered)
 
 
+def greet_all(devices):
+    me = lax.axis_index("dp") * MP + lax.axis_index("mp")
+    barrier = pltpu.get_barrier_semaphore()
+
+    def greet(k, carry):
+        peer = lax.rem(me + k, devices)
+        place = (peer // MP, lax.rem(peer, MP))
+        pl.semaphore_signal(barrier, inc=1, device_id=place, device_id_type=MESH)
+        return carry
+
+    lax.fori_loop(1, devices, greet, 0)
+
+
+def sum_over_all(devices, in_ref, out_ref, slots, send_sem, recv_sem):
+    me = lax.axis_index("dp") * MP + lax.axis_index("mp")
+
+    def copy(k, slot):
+        peer = lax.rem(me + k, devices)
+        place = (peer // MP, lax.rem(peer, MP))
+        return remote(in_ref, slots.at[slot], send_sem.at[k], recv_sem.at[slot], place)
+
+    slots[me] = in_ref[...]
+    pl.semaphore_wait(pltpu.get_barrier_semaphore(), devices - 1)
+
+    def push(k, carry):
+        copy(k, me).start()
+        return carry
+
+    def pull(k, carry):
+        copy(k, lax.rem(me + devices - k, devices)).wait_recv()
+        return carry
+
+    def settle(k, carry):
+        copy(k, me).wait_send()
+        return carry
+
+    lax.fori_loop(1, devices, push, 0)
+    lax.fori_loop(1, devices, pull, 0)
+    total = slots[0]
+    for i in range(1, devices):
+        total = total + slots[i]
+    out_ref[...] = total
+    lax.fori_loop(1, devices, settle, 0)
+
+
+def decoder_kernel(
+    all_crops,
+    devices,
+    up_ref,
+    deconv_bias_ref,
+    conv_ref,
+    conv_bias_ref,
+    head_ref,
+    head_bias_ref,
+    labels_ref,
+    batch_ref,
+    conv_t_ref,
+    head_t_ref,
+    gu_ref,
+    conv_grad_ref,
+    head_grad_ref,
+    small_ref,
+    deconv_grad_ref,
+    conv_in,
+    grid_slope,
+    conv_slope,
+    features,
+    chance,
+    sums,
+    conved,
+    spread,
+    total,
+    slots,
+    send_sem,
+    recv_sem,
+):
+    greet_all(devices)
+    decoder_forward_kernel(
+        up_ref,
+        deconv_bias_ref,
+        conv_ref,
+        conv_bias_ref,
+        head_ref,
+        head_bias_ref,
+        labels_ref,
+        batch_ref,
+        conv_in,
+        grid_slope,
+        conv_slope,
+        features,
+        chance,
+        sums,
+        conved,
+    )
+    sum_over_all(devices, sums, total, slots, send_sem, recv_sem)
+    decoder_backward_kernel(
+        all_crops,
+        total,
+        batch_ref,
+        labels_ref,
+        chance,
+        features,
+        conv_slope,
+        grid_slope,
+        conv_in,
+        conv_t_ref,
+        head_t_ref,
+        gu_ref,
+        conv_grad_ref,
+        head_grad_ref,
+        small_ref,
+        deconv_grad_ref,
+        spread,
+    )
+
+
+def decoder(all_crops, *operands):
+    devices = 4 * LAYERS * MP
+    shapes = (
+        jax.ShapeDtypeStruct((8 * DEC, NTOK), jnp.bfloat16),
+        jax.ShapeDtypeStruct((27 * CF, DEC), jnp.float32),
+        jax.ShapeDtypeStruct((CF, CF), jnp.float32),
+        jax.ShapeDtypeStruct((CF, BS), jnp.float32),
+        jax.ShapeDtypeStruct((DEC, BS), jnp.float32),
+    )
+    return pl.pallas_call(
+        functools.partial(decoder_kernel, all_crops, devices),
+        out_shape=shapes,
+        in_specs=whole_specs(10),
+        out_specs=tuple(whole_specs(5)),
+        scratch_shapes=[
+            pltpu.VMEM((DEC, CELLS), jnp.bfloat16),
+            pltpu.VMEM((DEC, CELLS), jnp.float32),
+            pltpu.VMEM((CF, CELLS), jnp.float32),
+            pltpu.VMEM((CF, CELLS), jnp.bfloat16),
+            pltpu.VMEM((CF, CELLS), jnp.float32),
+            pltpu.VMEM((CF, BS), jnp.float32),
+            pltpu.VMEM((CF, CELLS), jnp.float32),
+            pltpu.VMEM((27 * CF, CELLS), jnp.bfloat16),
+            pltpu.VMEM((CF, BS), jnp.float32),
+            pltpu.VMEM((devices, CF, BS), jnp.float32),
+            pltpu.SemaphoreType.DMA((devices,)),
+            pltpu.SemaphoreType.DMA((devices,)),
+        ],
+        compiler_params=pltpu.CompilerParams(
+            collective_id=3, has_side_effects=True, vmem_limit_bytes=40 * MIB
+        ),
+        cost_estimate=pl.CostEstimate(
+            flops=6 * 27 * CF * DEC * CELLS, bytes_accessed=6 * MIB, transcendentals=DEC * CELLS
+        ),
+        name="decoder",
+    )(*operands)
+
+
 def layer_norm(values):
     center = values - jnp.mean(values, -1, keepdims=True)
     spread = jnp.mean(center * center, -1, keepdims=True)
@@ -1576,11 +1670,12 @@
     hidden = dot_nn(normed_two, w_up) + pieces["up_bias"]
     active_value, hidden_slope = gelu_and_slope(hidden)
     active = active_value.astype(jnp.bfloat16)
+    active, one_half = lax.optimization_barrier((active, one_half))
+    active_other = swap_mp(columns(active, 1 - part, FF // MP, down_start))
     stream_two = stream_one + dot_nn(active, w_down) + pieces["down_bias"]
     streams = [zero_stream, one_stream, stream_two.astype(jnp.bfloat16)]
     stacked = jnp.concatenate([halves(s)[m] for m in range(MP) for s in streams], 1)
     up_t = dot(w_deconv, stacked, ((0,), (1,)))
-    active_other = swap_mp(columns(active, 1 - part, FF // MP, down_start))
 
     conv_weight = pieces["conv_weight"].astype(jnp.bfloat16).reshape(27, DEC, CF)
     conv_low = conv_weight.transpose(0, 2, 1).reshape(27 * CF, DEC)
@@ -1591,7 +1686,7 @@
         labels.reshape(GS, 2, GS, 2, GS, 2).transpose(1, 3, 5, 0, 2, 4).reshape(8, NTOK)
     )
     batch = jnp.broadcast_to(batch_ids.reshape(1, 1), (1, BS))
-    conv_in, grid_slope, conv_slope, features, chance, sums = decoder_forward(
+    operands = (
         up_t,
         pieces["deconv_bias"].reshape(DEC, 1),
         conv_low,
@@ -1601,24 +1696,27 @@
         grid_labels,
         batch,
     )
-    conv_in, one_half = lax.optimization_barrier((conv_in, one_half))
-    sums, two_stream, active_other = lax.optimization_barrier(
-        (sum_sums(sums), streams[2], active_other)
-    )
+    if fast_mesh():
+        gu_t, conv_grad, head_grad, small, deconv_bias_grad = decoder(
+            all_crops, *operands, conv_t, head_weight
+        )
+    else:
+        conv_in, grid_slope, conv_slope, features, chance, sums = decoder_forward(*operands)
+        gu_t, conv_grad, head_grad, small, deconv_bias_grad = decoder_backward(
+            all_crops,
+            lax.psum(sums, ("dp", "mp")),
+            batch,
+            grid_labels,
+            chance,
+            features,
+            conv_slope,
+            grid_slope,
+            conv_in,
+            conv_t,
+            head_weight,
+        )
+    gu_t, two_stream, active_other = lax.optimization_barrier((gu_t, streams[2], active_other))
     two_half = swap_mp(columns(two_stream, 1 - part, HALF, 0))
-    gu_t, conv_grad, head_grad, small, deconv_bias_grad = decoder_backward(
-        all_crops,
-        sums,
-        batch,
-        grid_labels,
-        chance,
-        features,
-        conv_slope,
-        grid_slope,
-        conv_in,
-        conv_t,
-        head_weight,
-    )
     loss_value = small[0, 2]
 
     gu_other = swap_mp(gu_t)

time: 539 us -> 530 us (0.983)
  local copies, waits for them, and re-layouts: 57.7 us -> 50.1 us
  Pallas kernels: 402 us -> 395 us
    unnamed x185 -> x112, local copies, waits for them, and re-layouts: 32.7 us -> 23.9 us
    pallas_call x3 -> x1, Pallas kernels: 19.9 us -> 14.2 us  [decoder(): pl.pallas_call(functools.partial(decoder_kernel, all_crops, devices), out...]
  transfers between devices with their start and end apart: 8 -> 8, of which waited for: 1 -> 3; matrix products, arithmetic and copies ran while one was open for 8% -> 10% of each run, Pallas kernels for 14% -> 14%
where the time goes in v5:
time: 530 us; the launch traced here: 522 us
  Pallas kernels  395 us (75%)
  local copies, waits for them, and re-layouts  50.1 us (9%)
  matrix products  42.4 us (8%)
  other arithmetic  13 us (2%)
  starting transfers between devices  10.8 us (2%)
  waiting for transfers between devices  8 us (2%)
    pallas_call x1, Pallas kernels, reduce_to_owners(): pl.pallas_call(reduce_kernel, out_shape=(jax.ShapeDtypeStruct((CHUNK, BS)...  174 us
    pallas_call x2, Pallas kernels, gather_all(): pl.pallas_call(functools.partial(gather_kernel, parts, by_x, skip, middle...  125 us
    dot_general x12, matrix products, dot(): lax.dot_general(a, b, (dims, ((), ())), preferred_element_type=jnp.float32)  42.4 us
    pallas_call x7, Pallas kernels, grad_blocks(): pl.pallas_call(functools.partial(blocks_kernel, first_block, per_row, ste...  30.5 us
    unnamed x112, local copies, waits for them, and re-layouts  23.9 us
    pallas_call x1, Pallas kernels, shampoo_step(): pl.pallas_call(functools.partial(shampoo_kernel, per_step), grid=(number...  15.2 us
    pallas_call x1, Pallas kernels, decoder(): pl.pallas_call(functools.partial(decoder_kernel, all_crops, devices), out...  14.2 us
    pallas_call x1, Pallas kernels, attention_backward(): pl.pallas_call(attention_backward_kernel, grid=(6,), out_shape=(jax.Shape...  12.3 us
  transfers between devices with their start and end apart: 8, of which 3 were waited for; matrix products, arithmetic and copies ran while one was open for 10% of the time, Pallas kernels for 14%

profile of v5, /device:TPU:0, one launch (start us, length us, event | category | flops | bytes accessed | tf_op | source)
XLA Modules:
  0.0 522.1 jit_solution(13105984791571750125)
XLA Ops:
  2.2 100.6 %gather_weights.1 = bf16[2,16,3072,128]{3,2,1,0:T(8,128)(2,1)} custom-call(bf16[3072,128]{1,0:T(8,128)(2,1)S(1)} %bitcast.67), custom_call_target="tpu_custom_call" | custom-call | bytes 50331648 | tf_op jit(solution)/shard_map/gather_weights/pallas_call | solution.py:635
  102.8 2.1 unblock_embedding.1
  104.9 1.7 copy-done.5
  106.5 2.9 constant_dynamic-slice_fusion.9
  109.7 2.9 fusion.23
  114.5 9.5 %unblock.1 = (bf16[768,2304]{1,0:T(8,128)(2,1)S(1)}, bf16[768,768]{1,0:T(8,128)(2,1)S(1)}, bf16[768,3072]{1,0:T(8,128)(2,1)S(1)}, bf16[3072,768]{1,0:T(8,128)(2,1)S(1)}, bf16[2304,1024]{1,0:T(8,128)(2,1)S(1)}) custom-call(bf16[2,384,128,128]{3,2,1,0:T(8,128)(2,1)} %bitcast.85), custom_call_target="tpu_custom_call" | custom-call | bytes 39845888 | tf_op jit(solution)/shard_map/unblock/pallas_call | solution.py:1106
  123.9 2.1 copy-done.12
  126.1 2.2 copy-done.13
  128.3 2.1 copy-done.14
  130.4 1.8 copy-done.15
  133.9 1.6 convert.7
  136.4 3.1 reshape.167
  142.1 2.0 reshape.173
  144.1 2.9 copy.35
  151.8 4.7 fusion.21
  157.4 1.6 collective-permute-start.1
  159.1 2.0 fusion.6.qkv_q.qkv_k.qkv_v
  161.2 9.2 %attention_forward.1 = (bf16[512,768]{1,0:T(8,128)(2,1)S(1)}, f32[6,2,512]{2,1,0:T(2,128)S(1)}) custom-call(bf16[512,2304]{1,0:T(8,128)(2,1)S(1)} %fusion.6.qkv_q.qkv_k.qkv_v, bf16[512,2304]{1,0:T(8,128)(2,1)S(1)} %fusion.6.qkv_q.qkv_k.qkv_v, bf16[512,2304]{1,0:T(8,128)(2,1)S(1)} %fusion.6.qkv_q.qkv_k.qkv_v), custom_call_target="tpu_custom_call" | custom-call | flops 805306368 | bytes 3145728 | tf_op jit(solution)/shard_map/attention_forward/pallas_call | solution.py:137
  172.2 1.6 collective-permute-start.2
  173.8 5.3 %multiply_convert_fusion = (bf16[512,3072]{1,0:T(8,128)(2,1)S(1)}, f32[512,3072]{1,0:T(8,128)}) fusion(f32[3072]{0:T(1024)S(1)} %slice.171, bf16[512,768]{1,0:T(8,128)(2,1)S(1)} %get-tuple-element.128.refs_0_, bf16[768,3072]{1,0:T(8,128)(2,1)S(1)} %bitcast.76), kind=kOutput, calls=%fused_computation.8 | convolution fusion | flops 2425356288 | bytes 14954496 | tf_op jit(solution)/shard_map/dot_general | solution.py:43
  179.2 4.2 collective-permute-done.2
  184.2 2.7 add_convert_fusion
  190.3 1.6 collective-permute-start.3
  191.9 4.3 convolution_bitcast_fusion.up_ref
  196.2 14.2 %decoder.1 = (bf16[1024,512]{1,0:T(8,128)(2,1)S(1)}, f32[432,128]{1,0:T(8,128)S(1)}, f32[16,16]{1,0:T(8,128)S(1)}, f32[16,128]{1,0:T(8,128)S(1)}, f32[128,128]{1,0:T(8,128)S(1)}) custom-call(f32[1024,512]{1,0:T(8,128)S(1)} %convolution_bitcast_fusion.up_ref, f32[128,1]{1,0:T(8,128)S(1)} %copy.37.deconv_bias_ref, bf16[432,128]{1,0:T(8,128)(2,1)S(1)} %bitcast.73, ...), custom_call_target="tpu_custom_call" | custom-call | flops 1358954496 | bytes 6291456 | tf_op jit(solution)/shard_map/decoder/pallas_call | solution.py:1509
  211.1 6.8 %fusion.24 = f32[512,2304]{1,0:T(8,128)} fusion(bf16[1024,512]{1,0:T(8,128)(2,1)S(1)} %get-tuple-element.53.refs_1_, bf16[2304,1024]{1,0:T(8,128)(2,1)} %copy-done.14), kind=kOutput, calls=%fused_computation.95 | convolution fusion | flops 2415919104 | bytes 10485760 | tf_op jit(solution)/shard_map/dot_general | solution.py:43
  217.9 1.6 collective-permute-start.5
  219.6 4.0 fusion.17
  225.1 6.7 %convert_reduce_fusion = (f32[3072]{0:T(1024)S(1)}, bf16[512,3072]{1,0:T(8,128)(2,1)S(1)}) fusion(bf16[512,768]{1,0:T(8,128)(2,1)S(1)} %fusion.11.refs_1_, bf16[3072,768]{1,0:T(8,128)(2,1)S(1)} %bitcast.80, f32[512,3072]{1,0:T(8,128)} %get-tuple-element.151, f32[3072]{0:T(1024)S(1)} %slice.171), kind=kOutput, calls=%fused_computation.7 | convolution fusion | flops 2436363264 | bytes 14966784 | tf_op jit(solution)/shard_map/dot_general | solution.py:43
  231.8 3.1 multiply_reduce_fusion
  236.8 12.3 %attention_backward.1 = (bf16[512,768]{1,0:T(8,128)(2,1)S(1)}, bf16[512,768]{1,0:T(8,128)(2,1)S(1)}, bf16[512,768]{1,0:T(8,128)(2,1)S(1)}) custom-call(bf16[512,2304]{1,0:T(8,128)(2,1)S(1)} %fusion.6.qkv_q.qkv_k.qkv_v, bf16[512,2304]{1,0:T(8,128)(2,1)S(1)} %fusion.6.qkv_q.qkv_k.qkv_v, bf16[512,2304]{1,0:T(8,128)(2,1)S(1)} %fusion.6.qkv_q.qkv_k.qkv_v, ...), custom_call_target="tpu_custom_call" | custom-call | flops 2013265920 | bytes 5505024 | tf_op jit(solution)/shard_map/attention_backward/pallas_call | solution.py:161
  249.5 1.6 copy-done.17
  251.1 2.0 fusion.25
  253.2 1.7 collective-permute-start.4
  255.3 4.6 grad_down.1.refs_2_
  259.9 6.0 %grad_up.1.refs_2_ = f32[2,8,3328,128]{3,2,1,0:T(8,128)} custom-call(bf16[512,768]{1,0:T(8,128)(2,1)S(1)} %get-tuple-element.128.refs_0_, bf16[512,3072]{1,0:T(8,128)(2,1)S(1)} %get-tuple-element.154.refs_1_, f32[2,8,3328,128]{3,2,1,0:T(8,128)} %grad_down.1.refs_2_), custom_call_target="tpu_custom_call", output_to_operand_aliasing={{}: (2, {})} | custom-call | flops 2415919104 | bytes 9437184 | tf_op jit(solution)/shard_map/grad_up/pallas_call | solution.py:1179
  265.9 2.5 collective-permute-done.4
  270.0 1.7 collective-permute-start.7
  271.6 2.6 grad_proj.1.refs_2_
  274.3 5.1 grad_qkv.1.refs_13_
  279.5 1.8 pack_aux.1
  281.4 4.9 grad_deconv.1.refs_4_
  288.7 6.2 %grad_embed.1 = f32[1,4,3072,128]{3,2,1,0:T(8,128)S(1)} custom-call(bf16[512,2048]{1,0:T(8,128)(2,1)S(1)} %get-tuple-element.116.refs_0_, bf16[512,768]{1,0:T(8,128)(2,1)S(1)} %get-tuple-element.106.refs_1_, bf16[512,2048]{1,0:T(8,128)(2,1)S(1)} %copy-done.3, bf16[512,768]{1,0:T(8,128)(2,1)S(1)} %collective-permute-done.7.refs_3_), custom_call_target="tpu_custom_call" | custom-call | flops 3221225472 | bytes 6291456 | tf_op jit(solution)/shard_map/grad_embed/pallas_call | solution.py:1179
  294.9 2.6 copy-done.1
  297.5 173.9 %reduce_to_owners.1 = (f32[3328,128]{1,0:T(8,128)}, f32[8,128]{1,0:T(8,128)}) custom-call(f32[2,2,2,2,3328,128]{5,4,3,2,1,0:T(8,128)} %bitcast.83, f32[2,2,3072,128]{3,2,1,0:T(8,128)} %bitcast.65, f32[2,2,3072,128]{3,2,1,0:T(8,128)} %bitcast.64), custom_call_target="tpu_custom_call" | custom-call | bytes 104857600 | tf_op jit(solution)/shard_map/reduce_to_owners/pallas_call | solution.py:982
  473.1 24.9 %gather_aux.1.sums_ref = f32[2,16,264,128]{3,2,1,0:T(8,128)S(1)} custom-call(f32[264,128]{1,0:T(8,128)S(1)} %pad_maximum_fusion.3.in_ref), custom_call_target="tpu_custom_call" | custom-call | bytes 4325376 | tf_op jit(solution)/shard_map/gather_aux/pallas_call | solution.py:635
  500.1 4.1 multiply_subtract_fusion
  506.7 15.2 %shampoo.1 = (f32[24,128,128]{2,1,0:T(8,128)}, f32[2,24,128,128]{3,2,1,0:T(8,128)}, f32[24,128,128]{2,1,0:T(8,128)}, f32[24,128,128]{2,1,0:T(8,128)}) custom-call(f32[1,1]{1,0:T(1,128)} %get-tuple-element.142.clip_ref, f32[3328,128]{1,0:T(8,128)S(1)} %copy-done.9, f32[24,128,128]{2,1,0:T(8,128)S(1)} %bitcast.66, f32[2,24,128,128]{3,2,1,0:T(8,128)S(1)} %bitcast.68, ...), custom_call_target="tpu_custom_call" | custom-call | flops 2415919104 | bytes 18874368 | tf_op jit(solution)/shard_map/shampoo/pallas_call | solution.py:1585
  (187 shorter events, 34.8 us)
Async XLA Ops:
  106.5 3.2 copy-start.6
  109.5 3.2 copy-start.2
  109.7 3.5 copy-start.22
  112.6 39.2 %collective-permute-start = (f32[512,768]{1,0:T(8,128)}, f32[512,768]{1,0:T(8,128)}, u32[]{:S(2)}, u32[]{:S(2)}) collective-permute-start(f32[512,768]{1,0:T(8,128)} %fusion.23), channel_id=1, source_target_pairs={{0,1},{1,0},{2,3},{3,2},{4,5},{5,4},{6,7},{7,6},{8,9},{9,8},{10,11... | collective-permute-start | bytes 4718600 | tf_op jit(solution)/shard_map/ppermute | solution.py:1217
  123.9 2.1 copy-start.12
  126.1 2.2 copy-start.13
  128.3 2.1 copy-start.14
  156.6 13.8 %copy-start.20 = (f32[512,768]{1,0:T(8,128)}, f32[512,768]{1,0:T(8,128)S(1)}, u32[]{:S(2)}) copy-start(f32[512,768]{1,0:T(8,128)S(1)} %get-tuple-element.147) | copy-start | bytes 4718596
  156.9 2.2 copy-start.16
  157.4 13.0 %collective-permute-start.1 = (bf16[512,384]{1,0:T(8,128)(2,1)S(1)}, bf16[512,384]{1,0:T(8,128)(2,1)S(1)}, u32[]{:S(2)}, u32[]{:S(2)}) collective-permute-start(bf16[512,384]{1,0:T(8,128)(2,1)S(1)} %get-tuple-element.140), channel_id=1, source_target_pairs={{0,1},{1,0},{2,3},{3,2},{4,5},{5,4},{6,7},{7,6},{8,9},{9,8},{10,11... | collective-permute-start | bytes 1179656 | tf_op jit(solution)/shard_map/ppermute | solution.py:1217
  161.1 9.3 %copy-start.19 = (bf16[768,768]{1,0:T(8,128)(2,1)S(1)}, bf16[768,768]{1,0:T(8,128)(2,1)}, u32[]{:S(2)}) copy-start(bf16[768,768]{1,0:T(8,128)(2,1)} %copy-done.18) | copy-start | bytes 3538948
  161.1 12.6 %slice-start = ((s8[4718592]{0:T(1024)(128)(4,1)}), s8[4194304]{0:T(1024)(128)(4,1)S(1)}, s32[]{:S(2)}) async-start(s8[4718592]{0:T(1024)(128)(4,1)} %bitcast.75), calls=%async_computation | async-start | bytes 8388608
  170.4 3.4 slice-start.1
  171.3 12.8 %copy-start.24 = (f32[512,768]{1,0:T(8,128)}, f32[512,768]{1,0:T(8,128)S(1)}, u32[]{:S(2)}) copy-start(f32[512,768]{1,0:T(8,128)S(1)} %get-tuple-element.149) | copy-start | bytes 4718596
  172.1 12.1 %slice-start.2 = ((s8[4718592]{0:T(1024)(128)(4,1)}), s8[4194304]{0:T(1024)(128)(4,1)S(1)}, s32[]{:S(2)}) async-start(s8[4718592]{0:T(1024)(128)(4,1)} %bitcast.77), calls=%async_computation.2 | async-start | bytes 8388608
  172.2 11.2 %collective-permute-start.2 = (bf16[512,384]{1,0:T(8,128)(2,1)S(1)}, bf16[512,384]{1,0:T(8,128)(2,1)S(1)}, u32[]{:S(2)}, u32[]{:S(2)}) collective-permute-start(bf16[512,384]{1,0:T(8,128)(2,1)S(1)} %get-tuple-element.138), channel_id=1, source_target_pairs={{0,1},{1,0},{2,3},{3,2},{4,5},{5,4},{6,7},{7,6},{8,9},{9,8},{10,11... | collective-permute-start | bytes 1179656 | tf_op jit(solution)/shard_map/ppermute | solution.py:1217
  173.8 10.4 %slice-start.3 = ((s8[4718592]{0:T(1024)(128)(4,1)}), s8[524288]{0:T(1024)(128)(4,1)S(1)}, s32[]{:S(2)}) async-start(s8[4718592]{0:T(1024)(128)(4,1)} %bitcast.77), calls=%async_computation.3 | async-start | bytes 1048576
  173.8 18.1 %slice-start.6 = ((s8[4718592]{0:T(1024)(128)(4,1)}), s8[4194304]{0:T(1024)(128)(4,1)S(1)}, s32[]{:S(2)}) async-start(s8[4718592]{0:T(1024)(128)(4,1)} %bitcast.81), calls=%async_computation.6 | async-start | bytes 8388608
  184.2 7.7 %slice-start.7 = ((s8[4718592]{0:T(1024)(128)(4,1)}), s8[524288]{0:T(1024)(128)(4,1)S(1)}, s32[]{:S(2)}) async-start(s8[4718592]{0:T(1024)(128)(4,1)} %bitcast.81), calls=%async_computation.7 | async-start | bytes 1048576
  186.8 2.5 copy-start.32
  190.3 20.8 %collective-permute-start.3 = (bf16[512,512]{1,0:T(8,128)(2,1)S(1)}, bf16[512,512]{1,0:T(8,128)(2,1)S(1)}, u32[]{:S(2)}, u32[]{:S(2)}) collective-permute-start(bf16[512,512]{1,0:T(8,128)(2,1)S(1)} %get-tuple-element.119), channel_id=1, source_target_pairs={{0,1},{1,0},{2,3},{3,2},{4,5},{5,4},{6,7},{7,6},{8,9},{9,8},{10,11... | collective-permute-start | bytes 1572872 | tf_op jit(solution)/shard_map/ppermute | solution.py:1217
  211.0 14.1 %slice-start.4 = ((s8[4718592]{0:T(1024)(128)(4,1)}), s8[4194304]{0:T(1024)(128)(4,1)S(1)}, s32[]{:S(2)}) async-start(s8[4718592]{0:T(1024)(128)(4,1)} %bitcast.79), calls=%async_computation.4 | async-start | bytes 8388608
  211.1 14.0 %slice-start.5 = ((s8[4718592]{0:T(1024)(128)(4,1)}), s8[524288]{0:T(1024)(128)(4,1)S(1)}, s32[]{:S(2)}) async-start(s8[4718592]{0:T(1024)(128)(4,1)} %bitcast.79), calls=%async_computation.5 | async-start | bytes 1048576
  217.9 50.5 %collective-permute-start.5 = (bf16[1024,512]{1,0:T(8,128)(2,1)S(1)}, bf16[1024,512]{1,0:T(8,128)(2,1)S(1)}, u32[]{:S(2)}, u32[]{:S(2)}) collective-permute-start(bf16[1024,512]{1,0:T(8,128)(2,1)S(1)} %get-tuple-element.53.refs_1_), channel_id=1, source_target_pairs={{0,1},{1,0},{2,3},{3,2},{4,5},{5,4},{6,7},{7,6},{8,9},{9,8},{10,11... | collective-permute-start | bytes 3145736 | tf_op jit(solution)/shard_map/ppermute | solution.py:1217
  224.6 43.8 %collective-permute-start.6 = (bf16[512,768]{1,0:T(8,128)(2,1)S(1)}, bf16[512,768]{1,0:T(8,128)(2,1)S(1)}, u32[]{:S(2)}, u32[]{:S(2)}) collective-permute-start(bf16[512,768]{1,0:T(8,128)(2,1)S(1)} %fusion.11.refs_1_), channel_id=1, source_target_pairs={{0,1},{1,0},{2,3},{3,2},{4,5},{5,4},{6,7},{7,6},{8,9},{9,8},{10,11... | collective-permute-start | bytes 2359304 | tf_op jit(solution)/shard_map/ppermute | solution.py:1217
  225.1 6.7 %copy-start.25 = (f32[512,768]{1,0:T(8,128)S(1)}, f32[512,768]{1,0:T(8,128)}, u32[]{:S(2)}) copy-start(f32[512,768]{1,0:T(8,128)} %copy-done.24) | copy-start | bytes 4718596
  231.8 3.1 copy-start.27
  231.8 3.1 copy-start.30
  231.8 3.1 copy-start.31
  249.1 2.0 copy-start.17
  251.1 2.0 copy-start.33
  253.2 15.2 %collective-permute-start.4 = (bf16[512,384]{1,0:T(8,128)(2,1)S(1)}, bf16[512,384]{1,0:T(8,128)(2,1)S(1)}, u32[]{:S(2)}, u32[]{:S(2)}) collective-permute-start(bf16[512,384]{1,0:T(8,128)(2,1)S(1)} %constant_dynamic-slice_fusion.4), channel_id=1, source_target_pairs={{0,1},{1,0},{2,3},{3,2},{4,5},{5,4},{6,7},{7,6},{8,9},{9,8},{10,11... | collective-permute-start | bytes 1179656 | tf_op jit(solution)/shard_map/ppermute | solution.py:1217
  259.9 8.5 %copy-start.21 = (f32[512,768]{1,0:T(8,128)S(1)}, f32[512,768]{1,0:T(8,128)}, u32[]{:S(2)}) copy-start(f32[512,768]{1,0:T(8,128)} %copy-done.20) | copy-start | bytes 4718596
  265.8 3.4 copy-start.28
  265.9 3.4 copy-start.29
  270.0 18.8 %collective-permute-start.7 = (bf16[512,768]{1,0:T(8,128)(2,1)S(1)}, bf16[512,768]{1,0:T(8,128)(2,1)S(1)}, u32[]{:S(2)}, u32[]{:S(2)}) collective-permute-start(bf16[512,768]{1,0:T(8,128)(2,1)S(1)} %get-tuple-element.106.refs_1_), channel_id=1, source_target_pairs={{0,1},{1,0},{2,3},{3,2},{4,5},{5,4},{6,7},{7,6},{8,9},{9,8},{10,11... | collective-permute-start | bytes 2359304 | tf_op jit(solution)/shard_map/ppermute | solution.py:1217
  286.3 2.4 copy-start.3
  287.5 7.4 %copy-start = (f32[1,4,3072,128]{3,2,1,0:T(8,128)}, f32[1,4,3072,128]{3,2,1,0:T(8,128)S(1)}, u32[]{:S(2)}) copy-start(f32[1,4,3072,128]{3,2,1,0:T(8,128)S(1)} %grad_down_last.1) | copy-start | bytes 18874372
  294.9 2.6 copy-start.1
  473.1 26.8 %copy-start.35 = (f32[458878]{0:T(1024)S(1)}, f32[458878]{0:T(1024)}, u32[]{:S(2)}) copy-start(f32[458878]{0:T(1024)} %param.21) | copy-start | bytes 5506540
  498.0 1.9 copy-start.23
  498.0 2.0 copy-start.34
  500.0 4.1 copy-start.4
  500.0 4.1 copy-start.7
  500.0 5.3 %copy-start.8 = (f32[2,1,1,24,128,128]{5,4,3,2,1,0:T(8,128)S(1)}, f32[2,1,1,24,128,128]{5,4,3,2,1,0:T(8,128)}, u32[]{:S(2)}) copy-start(f32[2,1,1,24,128,128]{5,4,3,2,1,0:T(8,128)} %param.16) | copy-start | bytes 9437188
  500.0 5.8 %copy-start.9 = (f32[3328,128]{1,0:T(8,128)S(1)}, f32[3328,128]{1,0:T(8,128)}, u32[]{:S(2)}) copy-start(f32[3328,128]{1,0:T(8,128)} %get-tuple-element.69.g_ref) | copy-start | bytes 5111812
  500.1 6.2 %copy-start.10 = (f32[1,1,24,128,128]{4,3,2,1,0:T(8,128)S(1)}, f32[1,1,24,128,128]{4,3,2,1,0:T(8,128)}, u32[]{:S(2)}) copy-start(f32[1,1,24,128,128]{4,3,2,1,0:T(8,128)} %param.17) | copy-start | bytes 4718596
  500.1 6.6 %copy-start.11 = (f32[1,1,24,128,128]{4,3,2,1,0:T(8,128)S(1)}, f32[1,1,24,128,128]{4,3,2,1,0:T(8,128)}, u32[]{:S(2)}) copy-start(f32[1,1,24,128,128]{4,3,2,1,0:T(8,128)} %param.18) | copy-start | bytes 4718596
  (10 other events, 14.1 us)

commit v6 on v5

--- a/solution.py
+++ b/solution.py
@@ -1044,13 +1044,12 @@
 def unblock_kernel(plan, kinds, blocks_ref, *refs):
     outs, tiles = refs[:kinds], refs[kinds : 2 * kinds]
     loaded, load_sem, store_sem = refs[2 * kinds :]
-    part = lax.axis_index("mp")
 
     def load(i):
         kind, m, first, rows, per_row, row, col = plan[i]
         number = rows * per_row
         return pltpu.make_async_copy(
-            blocks_ref.at[part if m is None else m, pl.ds(first, number)],
+            blocks_ref.at[m, pl.ds(first, number)],
             loaded.at[i % LOADS, pl.ds(0, number)],
             load_sem.at[i % LOADS],
         )
@@ -1085,22 +1084,16 @@
             store(*entry).wait()
 
 
-def unblock(gathered, embedding):
+def unblock(gathered):
     plan, shapes, tiles = [], [], []
-    if embedding:
-        plan = [(0, None, 24 * i, 4, 6, 4 * BS * i, 0) for i in range(4)]
-        shapes, tiles = [(PV // MP, D)], [(4 * BS, D)]
-    else:
-        for kind, (first, rows, per_row, step, beside) in enumerate(MATRICES):
-            tall, wide = rows * BS, per_row * BS
-            shapes.append((tall, MP * wide) if beside else (MP * tall, wide))
-            tiles.append((step * BS, wide))
-            for m in range(MP):
-                for at in range(0, rows, step):
-                    row = at * BS + (0 if beside else m * tall)
-                    plan.append(
-                        (kind, m, first + at * per_row, step, per_row, row, m * wide if beside else 0)
-                    )
+    for kind, (first, rows, per_row, step, beside) in enumerate(MATRICES):
+        tall, wide = rows * BS, per_row * BS
+        shapes.append((tall, MP * wide) if beside else (MP * tall, wide))
+        tiles.append((step * BS, wide))
+        for m in range(MP):
+            for at in range(0, rows, step):
+                row = at * BS + (0 if beside else m * tall)
+                plan.append((kind, m, first + at * per_row, step, per_row, row, m * wide if beside else 0))
     anywhere = pl.BlockSpec(memory_space=pl.ANY)
     largest = max(entry[3] * entry[4] for entry in plan)
     return pl.pallas_call(
@@ -1114,12 +1107,89 @@
             pltpu.SemaphoreType.DMA((LOADS,)),
             pltpu.SemaphoreType.DMA((len(shapes), 2)),
         ],
-        compiler_params=pltpu.CompilerParams(vmem_limit_bytes=32 * MIB),
+        compiler_params=pltpu.CompilerParams(vmem_limit_bytes=60 * MIB),
         cost_estimate=pl.CostEstimate(
-            flops=0, bytes_accessed=(6 if embedding else 38) * MIB, transcendentals=0
+            flops=0, bytes_accessed=38 * MIB, transcendentals=0
         ),
-        name="unblock_embedding" if embedding else "unblock",
+        name="unblock",
     )(gathered)
+
+
+def embed_kernel(which_ref, rows_ref, blocks_ref, out_ref, matrix_ref):
+    step = pl.program_id(0)
+    for r in range(4):
+        for c in range(6):
+            matrix_ref[r * BS : (r + 1) * BS, c * BS : (c + 1) * BS] = blocks_ref[0, r * 6 + c]
+    product = dot_nn(rows_ref[...], matrix_ref[...])
+
+    @pl.when(step == 0)
+    def _():
+        out_ref[...] = product
+
+    @pl.when(step > 0)
+    def _():
+        out_ref[...] += product
+
+
+def embed_other(patches, gathered):
+    part = lax.axis_index("mp")
+    tall = 4 * BS
+    return pl.pallas_call(
+        embed_kernel,
+        grid_spec=pltpu.PrefetchScalarGridSpec(
+            num_scalar_prefetch=1,
+            grid=(PV // MP // tall,),
+            in_specs=[
+                pl.BlockSpec((NTOK, tall), lambda k, which: (which[0], k)),
+                pl.BlockSpec((1, 24, BS, BS), lambda k, which: (which[1], k, 0, 0)),
+            ],
+            out_specs=(
+                pl.BlockSpec((NTOK, D), lambda k, which: (0, 0)),
+                pl.BlockSpec((tall, D), lambda k, which: (k, 0)),
+            ),
+        ),
+        out_shape=(
+            jax.ShapeDtypeStruct((NTOK, D), jnp.float32),
+            jax.ShapeDtypeStruct((PV // MP, D), jnp.bfloat16),
+        ),
+        compiler_params=pltpu.CompilerParams(vmem_limit_bytes=56 * MIB),
+        cost_estimate=pl.CostEstimate(
+            flops=2 * NTOK * D * PV // MP, bytes_accessed=10 * MIB, transcendentals=0
+        ),
+        name="embed_other",
+    )(jnp.stack([1 - part, part]).astype(jnp.int32), patches, gathered)
+
+
+def labels_kernel(labels_ref, out_ref):
+    side = 2 * GS
+    plane = side * side
+    rows = jnp.concatenate([labels_ref[:, z * plane : (z + 1) * plane] for z in range(side)], 0)
+    cell = lax.broadcasted_iota(jnp.int32, (plane, plane), 0)
+    place = lax.broadcasted_iota(jnp.int32, (plane, plane), 1)
+    parity, patch = place // (GS * GS), place % (GS * GS)
+    match = (cell // side == 2 * (patch // GS) + parity // 2) & (
+        cell % side == 2 * (patch % GS) + parity % 2
+    )
+    low = rows.astype(jnp.float32).astype(jnp.bfloat16)
+    moved = dot_nn(low, match.astype(jnp.float32).astype(jnp.bfloat16)).astype(jnp.int32)
+    width = GS * GS
+    for i in range(2):
+        for inner in range(4):
+            for a in range(GS):
+                out_ref[i * 4 + inner : i * 4 + inner + 1, a * width : (a + 1) * width] = moved[
+                    2 * a + i : 2 * a + i + 1, inner * width : (inner + 1) * width
+                ]
+
+
+def arrange_labels(labels):
+    return pl.pallas_call(
+        labels_kernel,
+        out_shape=jax.ShapeDtypeStruct((8, NTOK), jnp.int32),
+        in_specs=whole_specs(1),
+        out_specs=whole_specs(1)[0],
+        cost_estimate=pl.CostEstimate(flops=2 * 16 * 256 * 256, bytes_accessed=65536, transcendentals=0),
+        name="arrange_labels",
+    )(labels)
 
 
 def blocks_kernel(first_block, per_row, step_rows, transposed, pairs, *refs):
@@ -1174,7 +1244,7 @@
         g_spec = pl.BlockSpec((width, tokens), lambda m, i: (0, 0))
     else:
         g_spec = pl.BlockSpec((tokens, width), (lambda m, i: (0, m)) if split_g else (lambda m, i: (0, 0)))
-    anywhere = pl.BlockSpec(memory_space=pl.ANY)
+    anywhere = pl.BlockSpec(memory_space=pltpu.HBM)
     operands = [array for pair in zip(xs, gs) for array in pair] + ([] if buffer is None else [buffer])
     return pl.pallas_call(
         functools.partial(
@@ -1636,8 +1706,8 @@
     gain, shift = pieces["norm_gain"], pieces["norm_bias"]
 
     gathered = gather_weights(blocks)
-    (w_embed,) = unblock(gathered, True)
-    w_qkv, w_proj, w_up, w_down, w_deconv = unblock(gathered, False)
+    other_embedding, w_embed = embed_other(patches, gathered)
+    w_qkv, w_proj, w_up, w_down, w_deconv = unblock(gathered)
 
     def columns(array, which, width, start):
         return lax.dynamic_slice_in_dim(array, which * width + start, width - start, 1)
@@ -1646,7 +1716,7 @@
 
     other_rows = lax.dynamic_slice_in_dim(patches, (1 - part) * NTOK, NTOK, 0)
     own_rows = lax.dynamic_slice_in_dim(patches, part * NTOK, NTOK, 0)
-    received = swap_mp(dot_nn(other_rows, w_embed))
+    received = swap_mp(other_embedding)
     stream_zero = (
         dot_nn(own_rows, w_embed) + received + pieces["positions"] + pieces["embed_bias"]
     )
@@ -1682,9 +1752,7 @@
     conv_t = conv_weight.transpose(1, 0, 2).reshape(DEC, 27 * CF)
     head_weight = jnp.pad(pieces["head_weight"], ((0, 0), (0, CF - NCLS))).astype(jnp.bfloat16)
     head_bias = jnp.pad(pieces["head_bias"], (0, CF - NCLS)).reshape(CF, 1)
-    grid_labels = (
-        labels.reshape(GS, 2, GS, 2, GS, 2).transpose(1, 3, 5, 0, 2, 4).reshape(8, NTOK)
-    )
+    grid_labels = arrange_labels(labels)
     batch = jnp.broadcast_to(batch_ids.reshape(1, 1), (1, BS))
     operands = (
         up_t,

time: 530 us -> 520 us (0.981)
  local copies, waits for them, and re-layouts: 50.1 us -> 23 us
  Pallas kernels: 395 us -> 410 us
  waiting for transfers between devices: 8 us -> 21.7 us
  matrix products: 42.4 us -> 36.9 us
    unnamed x112 -> x75, local copies, waits for them, and re-layouts: 23.9 us -> 10.1 us
    ppermute x8, waiting for transfers between devices: 8 us -> 21.7 us  [swap_mp(): return lax.ppermute(values, 'mp', [(0, 1), (1, 0)])]
    pallas_call x0 -> x2, Pallas kernels: none -> 8.98 us  [the longest x1 7.37 us: embed_other(): pl.pallas_call(embed_kernel, grid_spec=pltpu.PrefetchScalarGridSpec(num_s...]
    dot_general x12 -> x11, matrix products: 42.4 us -> 36.9 us  [dot(): lax.dot_general(a, b, (dims, ((), ())), preferred_element_type=jnp.float32)]
    pallas_call x2 -> x1, Pallas kernels: 11.6 us -> 14.4 us  [unblock(): pl.pallas_call(functools.partial(unblock_kernel, plan, len(shapes)), out_...]
  transfers between devices with their start and end apart: 8 -> 8, of which waited for: 3 -> 4; matrix products, arithmetic and copies ran while one was open for 10% -> 7% of each run, Pallas kernels for 14% -> 16%
where the time goes in v6:
time: 520 us; the launch traced here: 511 us
  Pallas kernels  410 us (79%)
  matrix products  36.9 us (7%)
  local copies, waits for them, and re-layouts  23 us (4%)
  waiting for transfers between devices  21.7 us (4%)
  other arithmetic  11.3 us (2%)
  starting transfers between devices  5.99 us (1%)
    pallas_call x1, Pallas kernels, reduce_to_owners(): pl.pallas_call(reduce_kernel, out_shape=(jax.ShapeDtypeStruct((CHUNK, BS)...  173 us
    pallas_call x2, Pallas kernels, gather_all(): pl.pallas_call(functools.partial(gather_kernel, parts, by_x, skip, middle...  126 us
    dot_general x11, matrix products, dot(): lax.dot_general(a, b, (dims, ((), ())), preferred_element_type=jnp.float32)  36.9 us
    pallas_call x7, Pallas kernels, grad_blocks(): pl.pallas_call(functools.partial(blocks_kernel, first_block, per_row, ste...  30.3 us
    ppermute x8, waiting for transfers between devices, swap_mp(): return lax.ppermute(values, 'mp', [(0, 1), (1, 0)])  21.7 us
    pallas_call x1, Pallas kernels, decoder(): pl.pallas_call(functools.partial(decoder_kernel, all_crops, devices), out...  16.3 us
    pallas_call x1, Pallas kernels, shampoo_step(): pl.pallas_call(functools.partial(shampoo_kernel, per_step), grid=(number...  15.2 us
    pallas_call x1, Pallas kernels, unblock(): pl.pallas_call(functools.partial(unblock_kernel, plan, len(shapes)), out_...  14.4 us
  transfers between devices with their start and end apart: 8, of which 4 were waited for; matrix products, arithmetic and copies ran while one was open for 7% of the time, Pallas kernels for 16%

profile of v6, /device:TPU:0, one launch (start us, length us, event | category | flops | bytes accessed | tf_op | source)
XLA Modules:
  0.0 510.9 jit_solution(7279592162506180184)
XLA Ops:
  0.6 1.5 convert_element_type.60
  2.2 100.6 %gather_weights.1 = bf16[2,16,3072,128]{3,2,1,0:T(8,128)(2,1)} custom-call(bf16[3072,128]{1,0:T(8,128)(2,1)S(1)} %bitcast.64), custom_call_target="tpu_custom_call" | custom-call | bytes 50331648 | tf_op jit(solution)/shard_map/gather_weights/pallas_call | solution.py:635
  103.4 7.4 %embed_other.1 = (f32[512,768]{1,0:T(8,128)}, bf16[2048,768]{1,0:T(8,128)(2,1)}) custom-call(s32[2]{0:T(128)} %pad_add_fusion.which_ref, bf16[1024,2048]{1,0:T(8,128)(2,1)} %rows_ref.1, bf16[2,384,128,128]{3,2,1,0:T(8,128)(2,1)} %bitcast.73), custom_call_target="tpu_custom_call" | custom-call | flops 1610612736 | bytes 10485760 | tf_op jit(solution)/shard_map/embed_other/pallas_call | solution.py:1137
  111.3 14.4 %unblock.1 = (bf16[768,2304]{1,0:T(8,128)(2,1)}, bf16[768,768]{1,0:T(8,128)(2,1)}, bf16[768,3072]{1,0:T(8,128)(2,1)}, bf16[3072,768]{1,0:T(8,128)(2,1)}, bf16[2304,1024]{1,0:T(8,128)(2,1)}) custom-call(bf16[2,384,128,128]{3,2,1,0:T(8,128)(2,1)} %bitcast.74), custom_call_target="tpu_custom_call" | custom-call | bytes 39845888 | tf_op jit(solution)/shard_map/unblock/pallas_call | solution.py:1099
  125.7 1.2 slice.158
  127.3 2.6 reshape.161
  131.2 1.6 arrange_labels.1.labels_ref
  134.0 3.0 constant_dynamic-slice_fusion.4
  137.0 10.7 %collective-permute-done = f32[512,768]{1,0:T(8,128)} collective-permute-done((f32[512,768]{1,0:T(8,128)}, f32[512,768]{1,0:T(8,128)}, u32[]{:S(2)}, u32[]{:S(2)}) %collective-permute-start) | collective-permute-done | bytes 1572896 | tf_op jit(solution)/shard_map/ppermute | solution.py:1287
  147.7 3.3 fusion.21
  152.5 0.9 copy-done.21
  153.4 2.0 fusion.6.qkv_q.qkv_k.qkv_v
  155.4 9.7 %attention_forward.1 = (bf16[512,768]{1,0:T(8,128)(2,1)S(1)}, f32[6,2,512]{2,1,0:T(2,128)S(1)}) custom-call(bf16[512,2304]{1,0:T(8,128)(2,1)S(1)} %fusion.6.qkv_q.qkv_k.qkv_v, bf16[512,2304]{1,0:T(8,128)(2,1)S(1)} %fusion.6.qkv_q.qkv_k.qkv_v, bf16[512,2304]{1,0:T(8,128)(2,1)S(1)} %fusion.6.qkv_q.qkv_k.qkv_v), custom_call_target="tpu_custom_call" | custom-call | flops 805306368 | bytes 3145728 | tf_op jit(solution)/shard_map/attention_forward/pallas_call | solution.py:137
  165.1 0.9 fusion.22
  167.5 5.0 multiply_convert_fusion
  172.5 5.0 collective-permute-done.2
  177.6 2.6 add_convert_fusion
  182.0 2.6 convolution_bitcast_fusion.up_ref
  184.6 16.3 %decoder.1 = (bf16[1024,512]{1,0:T(8,128)(2,1)S(1)}, f32[432,128]{1,0:T(8,128)S(1)}, f32[16,16]{1,0:T(8,128)S(1)}, f32[16,128]{1,0:T(8,128)S(1)}, f32[128,128]{1,0:T(8,128)S(1)}) custom-call(f32[1024,512]{1,0:T(8,128)S(1)} %convolution_bitcast_fusion.up_ref, f32[128,1]{1,0:T(8,128)S(1)} %copy.35.deconv_bias_ref, bf16[432,128]{1,0:T(8,128)(2,1)S(1)} %bitcast.70, ...), custom_call_target="tpu_custom_call" | custom-call | flops 1358954496 | bytes 6291456 | tf_op jit(solution)/shard_map/decoder/pallas_call | solution.py:1579
  201.6 5.0 fusion.23
  207.3 1.2 fusion.17
  208.6 1.5 collective-permute-start.6
  210.1 7.3 %convert_reduce_fusion = (f32[3072]{0:T(1024)S(1)}, bf16[512,3072]{1,0:T(8,128)(2,1)S(1)}) fusion(bf16[512,768]{1,0:T(8,128)(2,1)S(1)} %fusion.11.refs_1_, bf16[3072,768]{1,0:T(8,128)(2,1)} %get-tuple-element.53, f32[512,3072]{1,0:T(8,128)} %get-tuple-element.155, f32[3072]{0:T(1024)S(1)} %slice.171), kind=kOutput, calls=%fused_computation.7 | convolution fusion | flops 2436363264 | bytes 14966784 | tf_op jit(solution)/shard_map/dot_general | solution.py:43
  217.3 5.4 %multiply_reduce_fusion = (f32[768]{0:T(1024)S(1)}, f32[512]{0:T(512)S(1)}, f32[512]{0:T(512)S(1)}, f32[768]{0:T(1024)S(1)}, f32[512,768]{1,0:T(8,128)S(1)}) fusion(f32[512,768]{1,0:T(8,128)S(1)} %copy-done.12, f32[512]{0:T(512)S(1)} %add_rsqrt_fusion, f32[512]{0:T(512)S(1)} %broadcast_multiply_fusion.4, f32[768]{0:T(1024)S(1)} %get-tuple-element.126, ...), kind=kOutput, calls=%fused_computation.25 | convolution fusion | flops 2419455488 | bytes 11027456 | tf_op jit(solution)/shard_map/dot_general | solution.py:43
  222.7 0.9 fusion.15
  223.7 1.2 copy-done.25
  224.9 0.8 convolution_convert_fusion.gm_ref
  225.7 12.5 %attention_backward.1 = (bf16[512,768]{1,0:T(8,128)(2,1)S(1)}, bf16[512,768]{1,0:T(8,128)(2,1)S(1)}, bf16[512,768]{1,0:T(8,128)(2,1)S(1)}) custom-call(bf16[512,2304]{1,0:T(8,128)(2,1)S(1)} %fusion.6.qkv_q.qkv_k.qkv_v, bf16[512,2304]{1,0:T(8,128)(2,1)S(1)} %fusion.6.qkv_q.qkv_k.qkv_v, bf16[512,2304]{1,0:T(8,128)(2,1)S(1)} %fusion.6.qkv_q.qkv_k.qkv_v, ...), custom_call_target="tpu_custom_call" | custom-call | flops 2013265920 | bytes 5505024 | tf_op jit(solution)/shard_map/attention_backward/pallas_call | solution.py:161
  238.7 1.6 copy-done.22
  240.3 2.0 fusion.24
  243.5 4.6 grad_down.1.refs_2_
  248.0 5.9 %grad_up.1.refs_2_ = f32[2,8,3328,128]{3,2,1,0:T(8,128)} custom-call(bf16[512,768]{1,0:T(8,128)(2,1)S(1)} %get-tuple-element.132.refs_0_, bf16[512,3072]{1,0:T(8,128)(2,1)S(1)} %get-tuple-element.158.refs_1_, f32[2,8,3328,128]{3,2,1,0:T(8,128)} %grad_down.1.refs_2_), custom_call_target="tpu_custom_call", output_to_operand_aliasing={{}: (2, {})} | custom-call | flops 2415919104 | bytes 9437184 | tf_op jit(solution)/shard_map/grad_up/pallas_call | solution.py:1249
  254.0 3.1 collective-permute-done.4
  259.3 2.2 grad_proj.1.refs_2_
  261.5 5.1 grad_qkv.1.refs_13_
  266.7 1.7 pack_aux.1
  268.4 4.9 grad_deconv.1.refs_4_
  273.4 1.2 grad_down_last.1
  274.6 2.8 collective-permute-done.7.refs_3_
  277.4 6.4 %grad_embed.1 = f32[1,4,3072,128]{3,2,1,0:T(8,128)S(1)} custom-call(bf16[512,2048]{1,0:T(8,128)(2,1)S(1)} %get-tuple-element.121.refs_0_, bf16[512,768]{1,0:T(8,128)(2,1)S(1)} %get-tuple-element.110.refs_1_, bf16[512,2048]{1,0:T(8,128)(2,1)S(1)} %get-tuple-element.120.refs_2_, bf16[512,768]{1,0:T(8,128)(2,1)S(1)} %collective-permute-done.7.refs_3_), custom_call_target="tpu_custom_call" | custom-call | flops 3221225472 | bytes 6291456 | tf_op jit(solution)/shard_map/grad_embed/pallas_call | solution.py:1249
  283.8 2.6 copy-done.1
  286.4 173.0 %reduce_to_owners.1 = (f32[3328,128]{1,0:T(8,128)}, f32[8,128]{1,0:T(8,128)}) custom-call(f32[2,2,2,2,3328,128]{5,4,3,2,1,0:T(8,128)} %bitcast.72, f32[2,2,3072,128]{3,2,1,0:T(8,128)} %bitcast.62, f32[2,2,3072,128]{3,2,1,0:T(8,128)} %bitcast.61), custom_call_target="tpu_custom_call" | custom-call | bytes 104857600 | tf_op jit(solution)/shard_map/reduce_to_owners/pallas_call | solution.py:982
  459.4 0.9 slice.195
  461.0 25.6 %gather_aux.1.sums_ref = f32[2,16,264,128]{3,2,1,0:T(8,128)S(1)} custom-call(f32[264,128]{1,0:T(8,128)S(1)} %pad_maximum_fusion.3.in_ref), custom_call_target="tpu_custom_call" | custom-call | bytes 4325376 | tf_op jit(solution)/shard_map/gather_aux/pallas_call | solution.py:635
  486.6 1.3 unpack_aux.1
  488.7 4.0 multiply_subtract_fusion
  492.7 1.3 copy-done.4
  495.3 15.2 %shampoo.1 = (f32[24,128,128]{2,1,0:T(8,128)}, f32[2,24,128,128]{3,2,1,0:T(8,128)}, f32[24,128,128]{2,1,0:T(8,128)}, f32[24,128,128]{2,1,0:T(8,128)}) custom-call(f32[1,1]{1,0:T(1,128)} %get-tuple-element.146.clip_ref, f32[3328,128]{1,0:T(8,128)S(1)} %copy-done.5, f32[24,128,128]{2,1,0:T(8,128)S(1)} %bitcast.63, f32[2,24,128,128]{3,2,1,0:T(8,128)S(1)} %bitcast.65, ...), custom_call_target="tpu_custom_call" | custom-call | flops 2415919104 | bytes 18874368 | tf_op jit(solution)/shard_map/shampoo/pallas_call | solution.py:1655
  (146 shorter events, 15.8 us)
Async XLA Ops:
  110.7 37.0 %collective-permute-start = (f32[512,768]{1,0:T(8,128)}, f32[512,768]{1,0:T(8,128)}, u32[]{:S(2)}, u32[]{:S(2)}) collective-permute-start(f32[512,768]{1,0:T(8,128)} %get-tuple-element.46), channel_id=1, source_target_pairs={{0,1},{1,0},{2,3},{3,2},{4,5},{5,4},{6,7},{7,6},{8,9},{9,8},{10,11... | collective-permute-start | bytes 4718600 | tf_op jit(solution)/shard_map/ppermute | solution.py:1287
  111.3 14.4 %copy-start.9 = (f32[458878]{0:T(1024)S(1)}, f32[458878]{0:T(1024)}, u32[]{:S(2)}) copy-start(f32[458878]{0:T(1024)} %param.19) | copy-start | bytes 5506540
  134.0 13.7 %copy-start.18 = (f32[512,768]{1,0:T(8,128)S(1)}, f32[512,768]{1,0:T(8,128)}, u32[]{:S(2)}) copy-start(f32[512,768]{1,0:T(8,128)} %reshape.161) | copy-start | bytes 4718596
  134.0 13.7 %copy-start.23 = (bf16[2048,768]{1,0:T(8,128)(2,1)S(1)}, bf16[2048,768]{1,0:T(8,128)(2,1)}, u32[]{:S(2)}) copy-start(bf16[2048,768]{1,0:T(8,128)(2,1)} %get-tuple-element.45) | copy-start | bytes 9437188
  151.4 2.0 copy-start.21
  151.9 13.2 %collective-permute-start.1 = (bf16[512,384]{1,0:T(8,128)(2,1)S(1)}, bf16[512,384]{1,0:T(8,128)(2,1)S(1)}, u32[]{:S(2)}, u32[]{:S(2)}) collective-permute-start(bf16[512,384]{1,0:T(8,128)(2,1)S(1)} %get-tuple-element.144), channel_id=1, source_target_pairs={{0,1},{1,0},{2,3},{3,2},{4,5},{5,4},{6,7},{7,6},{8,9},{9,8},{10,11... | collective-permute-start | bytes 1179656 | tf_op jit(solution)/shard_map/ppermute | solution.py:1287
  155.4 9.7 %copy-start.24 = (bf16[768,768]{1,0:T(8,128)(2,1)S(1)}, bf16[768,768]{1,0:T(8,128)(2,1)}, u32[]{:S(2)}) copy-start(bf16[768,768]{1,0:T(8,128)(2,1)} %get-tuple-element.50) | copy-start | bytes 3538948
  155.4 12.1 %slice-start = ((s8[4718592]{0:T(1024)(128)(4,1)}), s8[4194304]{0:T(1024)(128)(4,1)S(1)}, s32[]{:S(2)}) async-start(s8[4718592]{0:T(1024)(128)(4,1)} %bitcast.78), calls=%async_computation | async-start | bytes 8388608
  165.1 2.4 slice-start.1
  166.0 11.5 %copy-start.11 = (f32[512,768]{1,0:T(8,128)}, f32[512,768]{1,0:T(8,128)S(1)}, u32[]{:S(2)}) copy-start(f32[512,768]{1,0:T(8,128)S(1)} %get-tuple-element.153) | copy-start | bytes 4718596
  166.7 10.8 %slice-start.2 = ((s8[4718592]{0:T(1024)(128)(4,1)}), s8[4194304]{0:T(1024)(128)(4,1)S(1)}, s32[]{:S(2)}) async-start(s8[4718592]{0:T(1024)(128)(4,1)} %bitcast.80), calls=%async_computation.2 | async-start | bytes 8388608
  166.9 10.6 %collective-permute-start.2 = (bf16[512,384]{1,0:T(8,128)(2,1)S(1)}, bf16[512,384]{1,0:T(8,128)(2,1)S(1)}, u32[]{:S(2)}, u32[]{:S(2)}) collective-permute-start(bf16[512,384]{1,0:T(8,128)(2,1)S(1)} %get-tuple-element.142), channel_id=1, source_target_pairs={{0,1},{1,0},{2,3},{3,2},{4,5},{5,4},{6,7},{7,6},{8,9},{9,8},{10,11... | collective-permute-start | bytes 1179656 | tf_op jit(solution)/shard_map/ppermute | solution.py:1287
  167.5 10.0 %slice-start.3 = ((s8[4718592]{0:T(1024)(128)(4,1)}), s8[524288]{0:T(1024)(128)(4,1)S(1)}, s32[]{:S(2)}) async-start(s8[4718592]{0:T(1024)(128)(4,1)} %bitcast.80), calls=%async_computation.3 | async-start | bytes 1048576
  167.5 14.4 %slice-start.4 = ((s8[4718592]{0:T(1024)(128)(4,1)}), s8[524288]{0:T(1024)(128)(4,1)S(1)}, s32[]{:S(2)}) async-start(s8[4718592]{0:T(1024)(128)(4,1)} %bitcast.82), calls=%async_computation.4 | async-start | bytes 1048576
  177.5 2.7 copy-start.19
  177.5 4.4 slice-start.5
  180.2 0.9 copy-start.14
  181.3 20.3 %collective-permute-start.3 = (bf16[512,512]{1,0:T(8,128)(2,1)S(1)}, bf16[512,512]{1,0:T(8,128)(2,1)S(1)}, u32[]{:S(2)}, u32[]{:S(2)}) collective-permute-start(bf16[512,512]{1,0:T(8,128)(2,1)S(1)} %get-tuple-element.123), channel_id=1, source_target_pairs={{0,1},{1,0},{2,3},{3,2},{4,5},{5,4},{6,7},{7,6},{8,9},{9,8},{10,11... | collective-permute-start | bytes 1572872 | tf_op jit(solution)/shard_map/ppermute | solution.py:1287
  182.0 2.7 copy-start.8
  206.6 50.5 %collective-permute-start.5 = (bf16[1024,512]{1,0:T(8,128)(2,1)S(1)}, bf16[1024,512]{1,0:T(8,128)(2,1)S(1)}, u32[]{:S(2)}, u32[]{:S(2)}) collective-permute-start(bf16[1024,512]{1,0:T(8,128)(2,1)S(1)} %get-tuple-element.57.refs_1_), channel_id=1, source_target_pairs={{0,1},{1,0},{2,3},{3,2},{4,5},{5,4},{6,7},{7,6},{8,9},{9,8},{10,11... | collective-permute-start | bytes 3145736 | tf_op jit(solution)/shard_map/ppermute | solution.py:1287
  208.6 48.6 %collective-permute-start.6 = (bf16[512,768]{1,0:T(8,128)(2,1)S(1)}, bf16[512,768]{1,0:T(8,128)(2,1)S(1)}, u32[]{:S(2)}, u32[]{:S(2)}) collective-permute-start(bf16[512,768]{1,0:T(8,128)(2,1)S(1)} %fusion.11.refs_1_), channel_id=1, source_target_pairs={{0,1},{1,0},{2,3},{3,2},{4,5},{5,4},{6,7},{7,6},{8,9},{9,8},{10,11... | collective-permute-start | bytes 2359304 | tf_op jit(solution)/shard_map/ppermute | solution.py:1287
  210.1 7.3 %copy-start.12 = (f32[512,768]{1,0:T(8,128)S(1)}, f32[512,768]{1,0:T(8,128)}, u32[]{:S(2)}) copy-start(f32[512,768]{1,0:T(8,128)} %copy-done.11) | copy-start | bytes 4718596
  223.6 1.3 copy-start.25
  238.3 2.0 copy-start.22
  240.3 2.0 copy-start.15
  242.4 14.7 %collective-permute-start.4 = (bf16[512,384]{1,0:T(8,128)(2,1)S(1)}, bf16[512,384]{1,0:T(8,128)(2,1)S(1)}, u32[]{:S(2)}, u32[]{:S(2)}) collective-permute-start(bf16[512,384]{1,0:T(8,128)(2,1)S(1)} %constant_dynamic-slice_fusion.5), channel_id=1, source_target_pairs={{0,1},{1,0},{2,3},{3,2},{4,5},{5,4},{6,7},{7,6},{8,9},{9,8},{10,11... | collective-permute-start | bytes 1179656 | tf_op jit(solution)/shard_map/ppermute | solution.py:1287
  254.0 3.9 copy-start.13
  258.6 18.8 %collective-permute-start.7 = (bf16[512,768]{1,0:T(8,128)(2,1)S(1)}, bf16[512,768]{1,0:T(8,128)(2,1)S(1)}, u32[]{:S(2)}, u32[]{:S(2)}) collective-permute-start(bf16[512,768]{1,0:T(8,128)(2,1)S(1)} %get-tuple-element.110.refs_1_), channel_id=1, source_target_pairs={{0,1},{1,0},{2,3},{3,2},{4,5},{5,4},{6,7},{7,6},{8,9},{9,8},{10,11... | collective-permute-start | bytes 2359304 | tf_op jit(solution)/shard_map/ppermute | solution.py:1287
  266.6 1.7 copy-start.20
  274.6 9.2 %copy-start = (f32[1,4,3072,128]{3,2,1,0:T(8,128)}, f32[1,4,3072,128]{3,2,1,0:T(8,128)S(1)}, u32[]{:S(2)}) copy-start(f32[1,4,3072,128]{3,2,1,0:T(8,128)S(1)} %grad_down_last.1) | copy-start | bytes 18874372
  283.8 2.6 copy-start.1
  286.4 202.2 %copy-start.17 = (f32[458878]{0:T(1024)S(1)}, f32[458878]{0:T(1024)}, u32[]{:S(2)}) copy-start(f32[458878]{0:T(1024)} %param.21) | copy-start | bytes 5506540
  486.6 1.9 copy-start.10
  486.6 2.0 copy-start.16
  488.7 4.0 copy-start.2
  488.7 4.0 copy-start.3
  488.7 5.3 %copy-start.4 = (f32[2,1,1,24,128,128]{5,4,3,2,1,0:T(8,128)S(1)}, f32[2,1,1,24,128,128]{5,4,3,2,1,0:T(8,128)}, u32[]{:S(2)}) copy-start(f32[2,1,1,24,128,128]{5,4,3,2,1,0:T(8,128)} %param.16) | copy-start | bytes 9437188
  488.7 5.8 %copy-start.5 = (f32[3328,128]{1,0:T(8,128)S(1)}, f32[3328,128]{1,0:T(8,128)}, u32[]{:S(2)}) copy-start(f32[3328,128]{1,0:T(8,128)} %get-tuple-element.73.g_ref) | copy-start | bytes 5111812
  488.7 6.2 %copy-start.6 = (f32[1,1,24,128,128]{4,3,2,1,0:T(8,128)S(1)}, f32[1,1,24,128,128]{4,3,2,1,0:T(8,128)}, u32[]{:S(2)}) copy-start(f32[1,1,24,128,128]{4,3,2,1,0:T(8,128)} %param.17) | copy-start | bytes 4718596
  488.7 6.6 %copy-start.7 = (f32[1,1,24,128,128]{4,3,2,1,0:T(8,128)S(1)}, f32[1,1,24,128,128]{4,3,2,1,0:T(8,128)}, u32[]{:S(2)}) copy-start(f32[1,1,24,128,128]{4,3,2,1,0:T(8,128)} %param.18) | copy-start | bytes 4718596

commit v7 on v6

--- a/solution.py
+++ b/solution.py
@@ -421,8 +421,8 @@
 CHUNK = BLOCK_ROWS + AUX_ROWS
 ROWS_N = 2 * CHUNK // PIECES
 ROWS_F = BLOCK_ROWS // PIECES
-LAG = 2
-HOP_LAG = 2
+LAG = 1
+HOP_LAG = 1
 AHEAD = 3
 CORE_SLOTS = 8
 SEND_SLOTS = 4
@@ -1648,7 +1648,7 @@
 
 def shampoo_step(clip, owned, blocks, stat_pair, root_pair, moment, velocity):
     number = blocks.shape[0]
-    per_step = 3
+    per_step = 3 if number % 4 else 4
     one = pl.BlockSpec((per_step, BS, BS), lambda i: (i, 0, 0))
     pair = pl.BlockSpec((2, per_step, BS, BS), lambda i: (0, i, 0, 0))
     single = jax.ShapeDtypeStruct((number, BS, BS), jnp.float32)
@@ -1666,7 +1666,7 @@
             one,
         ],
         out_specs=(one, pair, one, one),
-        compiler_params=pltpu.CompilerParams(vmem_limit_bytes=32 * MIB),
+        compiler_params=pltpu.CompilerParams(vmem_limit_bytes=60 * MIB),
         cost_estimate=pl.CostEstimate(
             flops=number * 8 * BS**3 * 6, bytes_accessed=number * 12 * BS * BS * 4, transcendentals=0
         ),

time: 520 us -> 515 us (level)
  no operation moved by 1% of the time
where the time goes in v7:
time: 515 us; the launch traced here: 505 us
  Pallas kernels  407 us (79%)
  matrix products  36.9 us (7%)
  waiting for transfers between devices  21.7 us (4%)
  local copies, waits for them, and re-layouts  20.3 us (4%)
  other arithmetic  11.2 us (2%)
  starting transfers between devices  5.99 us (1%)
    pallas_call x1, Pallas kernels, reduce_to_owners(): pl.pallas_call(reduce_kernel, out_shape=(jax.ShapeDtypeStruct((CHUNK, BS)...  170 us
    pallas_call x2, Pallas kernels, gather_all(): pl.pallas_call(functools.partial(gather_kernel, parts, by_x, skip, middle...  125 us
    dot_general x11, matrix products, dot(): lax.dot_general(a, b, (dims, ((), ())), preferred_element_type=jnp.float32)  36.9 us
    pallas_call x7, Pallas kernels, grad_blocks(): pl.pallas_call(functools.partial(blocks_kernel, first_block, per_row, ste...  30.4 us
    ppermute x8, waiting for transfers between devices, swap_mp(): return lax.ppermute(values, 'mp', [(0, 1), (1, 0)])  21.7 us
    pallas_call x1, Pallas kernels, decoder(): pl.pallas_call(functools.partial(decoder_kernel, all_crops, devices), out...  16.3 us
    pallas_call x1, Pallas kernels, shampoo_step(): pl.pallas_call(functools.partial(shampoo_kernel, per_step), grid=(number...  16 us
    pallas_call x1, Pallas kernels, unblock(): pl.pallas_call(functools.partial(unblock_kernel, plan, len(shapes)), out_...  14.3 us
  transfers between devices with their start and end apart: 8, of which 4 were waited for; matrix products, arithmetic and copies ran while one was open for 7% of the time, Pallas kernels for 16%

profile of v7, /device:TPU:0, one launch (start us, length us, event | category | flops | bytes accessed | tf_op | source)
XLA Modules:
  0.0 505.2 jit_solution(925651255122395360)
XLA Ops:
  0.6 1.5 convert_element_type.60
  2.2 100.6 %gather_weights.1 = bf16[2,16,3072,128]{3,2,1,0:T(8,128)(2,1)} custom-call(bf16[3072,128]{1,0:T(8,128)(2,1)S(1)} %bitcast.63), custom_call_target="tpu_custom_call" | custom-call | bytes 50331648 | tf_op jit(solution)/shard_map/gather_weights/pallas_call | solution.py:635
  103.4 7.4 %embed_other.1 = (f32[512,768]{1,0:T(8,128)}, bf16[2048,768]{1,0:T(8,128)(2,1)}) custom-call(s32[2]{0:T(128)} %pad_add_fusion.which_ref, bf16[1024,2048]{1,0:T(8,128)(2,1)} %rows_ref.1, bf16[2,384,128,128]{3,2,1,0:T(8,128)(2,1)} %bitcast.68), custom_call_target="tpu_custom_call" | custom-call | flops 1610612736 | bytes 10485760 | tf_op jit(solution)/shard_map/embed_other/pallas_call | solution.py:1137
  111.3 14.3 %unblock.1 = (bf16[768,2304]{1,0:T(8,128)(2,1)}, bf16[768,768]{1,0:T(8,128)(2,1)}, bf16[768,3072]{1,0:T(8,128)(2,1)}, bf16[3072,768]{1,0:T(8,128)(2,1)}, bf16[2304,1024]{1,0:T(8,128)(2,1)}) custom-call(bf16[2,384,128,128]{3,2,1,0:T(8,128)(2,1)} %bitcast.69), custom_call_target="tpu_custom_call" | custom-call | bytes 39845888 | tf_op jit(solution)/shard_map/unblock/pallas_call | solution.py:1099
  125.7 1.2 slice.158
  127.2 2.6 reshape.161
  131.1 1.6 arrange_labels.1.labels_ref
  133.9 3.0 constant_dynamic-slice_fusion.4
  136.9 10.8 %collective-permute-done = f32[512,768]{1,0:T(8,128)} collective-permute-done((f32[512,768]{1,0:T(8,128)}, f32[512,768]{1,0:T(8,128)}, u32[]{:S(2)}, u32[]{:S(2)}) %collective-permute-start) | collective-permute-done | bytes 1572896 | tf_op jit(solution)/shard_map/ppermute | solution.py:1287
  147.7 3.3 fusion.21
  152.5 0.9 copy-done.15
  153.4 2.0 fusion.6.qkv_q.qkv_k.qkv_v
  155.4 9.7 %attention_forward.1 = (bf16[512,768]{1,0:T(8,128)(2,1)S(1)}, f32[6,2,512]{2,1,0:T(2,128)S(1)}) custom-call(bf16[512,2304]{1,0:T(8,128)(2,1)S(1)} %fusion.6.qkv_q.qkv_k.qkv_v, bf16[512,2304]{1,0:T(8,128)(2,1)S(1)} %fusion.6.qkv_q.qkv_k.qkv_v, bf16[512,2304]{1,0:T(8,128)(2,1)S(1)} %fusion.6.qkv_q.qkv_k.qkv_v), custom_call_target="tpu_custom_call" | custom-call | flops 805306368 | bytes 3145728 | tf_op jit(solution)/shard_map/attention_forward/pallas_call | solution.py:137
  165.1 0.9 fusion.22
  167.5 5.0 multiply_convert_fusion
  172.6 5.0 collective-permute-done.2
  177.6 2.6 add_convert_fusion
  182.0 2.6 convolution_bitcast_fusion.up_ref
  184.6 16.3 %decoder.1 = (bf16[1024,512]{1,0:T(8,128)(2,1)S(1)}, f32[432,128]{1,0:T(8,128)S(1)}, f32[16,16]{1,0:T(8,128)S(1)}, f32[16,128]{1,0:T(8,128)S(1)}, f32[128,128]{1,0:T(8,128)S(1)}) custom-call(f32[1024,512]{1,0:T(8,128)S(1)} %convolution_bitcast_fusion.up_ref, f32[128,1]{1,0:T(8,128)S(1)} %copy.35.deconv_bias_ref, bf16[432,128]{1,0:T(8,128)(2,1)S(1)} %bitcast.65, ...), custom_call_target="tpu_custom_call" | custom-call | flops 1358954496 | bytes 6291456 | tf_op jit(solution)/shard_map/decoder/pallas_call | solution.py:1579
  201.6 5.0 fusion.23
  207.3 1.2 fusion.17
  208.6 1.5 collective-permute-start.6
  210.1 7.3 %convert_reduce_fusion = (f32[3072]{0:T(1024)S(1)}, bf16[512,3072]{1,0:T(8,128)(2,1)S(1)}) fusion(bf16[512,768]{1,0:T(8,128)(2,1)S(1)} %fusion.11.refs_1_, bf16[3072,768]{1,0:T(8,128)(2,1)} %get-tuple-element.53, f32[512,3072]{1,0:T(8,128)} %get-tuple-element.155, f32[3072]{0:T(1024)S(1)} %slice.171), kind=kOutput, calls=%fused_computation.7 | convolution fusion | flops 2436363264 | bytes 14966784 | tf_op jit(solution)/shard_map/dot_general | solution.py:43
  217.3 5.4 %multiply_reduce_fusion = (f32[768]{0:T(1024)S(1)}, f32[512]{0:T(512)S(1)}, f32[512]{0:T(512)S(1)}, f32[768]{0:T(1024)S(1)}, f32[512,768]{1,0:T(8,128)S(1)}) fusion(f32[512,768]{1,0:T(8,128)S(1)} %copy-done.6, f32[512]{0:T(512)S(1)} %add_rsqrt_fusion, f32[512]{0:T(512)S(1)} %broadcast_multiply_fusion.4, f32[768]{0:T(1024)S(1)} %get-tuple-element.126, ...), kind=kOutput, calls=%fused_computation.25 | convolution fusion | flops 2419455488 | bytes 11027456 | tf_op jit(solution)/shard_map/dot_general | solution.py:43
  222.7 0.9 fusion.15
  223.7 1.2 copy-done.19
  224.9 0.8 convolution_convert_fusion.gm_ref
  225.7 12.5 %attention_backward.1 = (bf16[512,768]{1,0:T(8,128)(2,1)S(1)}, bf16[512,768]{1,0:T(8,128)(2,1)S(1)}, bf16[512,768]{1,0:T(8,128)(2,1)S(1)}) custom-call(bf16[512,2304]{1,0:T(8,128)(2,1)S(1)} %fusion.6.qkv_q.qkv_k.qkv_v, bf16[512,2304]{1,0:T(8,128)(2,1)S(1)} %fusion.6.qkv_q.qkv_k.qkv_v, bf16[512,2304]{1,0:T(8,128)(2,1)S(1)} %fusion.6.qkv_q.qkv_k.qkv_v, ...), custom_call_target="tpu_custom_call" | custom-call | flops 2013265920 | bytes 5505024 | tf_op jit(solution)/shard_map/attention_backward/pallas_call | solution.py:161
  238.7 1.6 copy-done.16
  240.3 2.0 fusion.24
  243.5 4.6 grad_down.1.refs_2_
  248.1 6.0 %grad_up.1.refs_2_ = f32[2,8,3328,128]{3,2,1,0:T(8,128)} custom-call(bf16[512,768]{1,0:T(8,128)(2,1)S(1)} %get-tuple-element.132.refs_0_, bf16[512,3072]{1,0:T(8,128)(2,1)S(1)} %get-tuple-element.158.refs_1_, f32[2,8,3328,128]{3,2,1,0:T(8,128)} %grad_down.1.refs_2_), custom_call_target="tpu_custom_call", output_to_operand_aliasing={{}: (2, {})} | custom-call | flops 2415919104 | bytes 9437184 | tf_op jit(solution)/shard_map/grad_up/pallas_call | solution.py:1249
  254.0 3.1 collective-permute-done.4
  257.2 0.7 multiply_reduce_fusion.1
  259.3 2.2 grad_proj.1.refs_2_
  261.5 5.1 %grad_qkv.1.refs_13_ = f32[2,8,3328,128]{3,2,1,0:T(8,128)} custom-call(bf16[512,768]{1,0:T(8,128)(2,1)S(1)} %get-tuple-element.134.refs_0_, bf16[512,2304]{1,0:T(8,128)(2,1)S(1)} %slice_dynamic-update-slice_fusion.6.refs_1_, f32[2,8,3328,128]{3,2,1,0:T(8,128)} %grad_proj.1.refs_2_), custom_call_target="tpu_custom_call", output_to_operand_aliasing={{}: (2, {})} | custom-call | flops 1811939328 | bytes 7077888 | tf_op jit(solution)/shard_map/grad_qkv/pallas_call | solution.py:1249
  266.7 1.6 pack_aux.1
  268.4 4.9 grad_deconv.1.refs_4_
  273.3 1.2 grad_down_last.1
  274.5 2.8 collective-permute-done.7.refs_3_
  277.4 6.4 %grad_embed.1 = f32[1,4,3072,128]{3,2,1,0:T(8,128)S(1)} custom-call(bf16[512,2048]{1,0:T(8,128)(2,1)S(1)} %get-tuple-element.121.refs_0_, bf16[512,768]{1,0:T(8,128)(2,1)S(1)} %get-tuple-element.110.refs_1_, bf16[512,2048]{1,0:T(8,128)(2,1)S(1)} %get-tuple-element.120.refs_2_, bf16[512,768]{1,0:T(8,128)(2,1)S(1)} %collective-permute-done.7.refs_3_), custom_call_target="tpu_custom_call" | custom-call | flops 3221225472 | bytes 6291456 | tf_op jit(solution)/shard_map/grad_embed/pallas_call | solution.py:1249
  283.8 2.6 copy-done.1
  286.4 170.0 %reduce_to_owners.1 = (f32[3328,128]{1,0:T(8,128)}, f32[8,128]{1,0:T(8,128)}) custom-call(f32[2,2,2,2,3328,128]{5,4,3,2,1,0:T(8,128)} %bitcast.67, f32[2,2,3072,128]{3,2,1,0:T(8,128)} %bitcast.62, f32[2,2,3072,128]{3,2,1,0:T(8,128)} %bitcast.61), custom_call_target="tpu_custom_call" | custom-call | bytes 104857600 | tf_op jit(solution)/shard_map/reduce_to_owners/pallas_call | solution.py:982
  456.4 0.9 slice.195
  458.0 24.9 %gather_aux.1.sums_ref = f32[2,16,264,128]{3,2,1,0:T(8,128)S(1)} custom-call(f32[264,128]{1,0:T(8,128)S(1)} %pad_maximum_fusion.3.in_ref), custom_call_target="tpu_custom_call" | custom-call | bytes 4325376 | tf_op jit(solution)/shard_map/gather_aux/pallas_call | solution.py:635
  482.8 1.3 unpack_aux.1
  484.9 3.9 multiply_subtract_fusion
  488.8 16.0 %shampoo.1 = (f32[24,128,128]{2,1,0:T(8,128)}, f32[2,24,128,128]{3,2,1,0:T(8,128)}, f32[24,128,128]{2,1,0:T(8,128)}, f32[24,128,128]{2,1,0:T(8,128)}) custom-call(f32[1,1]{1,0:T(1,128)} %get-tuple-element.146.clip_ref, f32[3328,128]{1,0:T(8,128)} %get-tuple-element.73.g_ref, f32[24,128,128]{2,1,0:T(8,128)} %bitcast.72, f32[2,24,128,128]{3,2,1,0:T(8,128)} %bitcast.73, ...), custom_call_target="tpu_custom_call" | custom-call | flops 2415919104 | bytes 18874368 | tf_op jit(solution)/shard_map/shampoo/pallas_call | solution.py:1655
  (134 shorter events, 13.7 us)
Async XLA Ops:
  110.7 37.0 %collective-permute-start = (f32[512,768]{1,0:T(8,128)}, f32[512,768]{1,0:T(8,128)}, u32[]{:S(2)}, u32[]{:S(2)}) collective-permute-start(f32[512,768]{1,0:T(8,128)} %get-tuple-element.46), channel_id=1, source_target_pairs={{0,1},{1,0},{2,3},{3,2},{4,5},{5,4},{6,7},{7,6},{8,9},{9,8},{10,11... | collective-permute-start | bytes 4718600 | tf_op jit(solution)/shard_map/ppermute | solution.py:1287
  111.3 14.4 %copy-start.3 = (f32[458878]{0:T(1024)S(1)}, f32[458878]{0:T(1024)}, u32[]{:S(2)}) copy-start(f32[458878]{0:T(1024)} %param.19) | copy-start | bytes 5506540
  133.9 13.8 %copy-start.12 = (f32[512,768]{1,0:T(8,128)S(1)}, f32[512,768]{1,0:T(8,128)}, u32[]{:S(2)}) copy-start(f32[512,768]{1,0:T(8,128)} %reshape.161) | copy-start | bytes 4718596
  133.9 13.8 %copy-start.17 = (bf16[2048,768]{1,0:T(8,128)(2,1)S(1)}, bf16[2048,768]{1,0:T(8,128)(2,1)}, u32[]{:S(2)}) copy-start(bf16[2048,768]{1,0:T(8,128)(2,1)} %get-tuple-element.45) | copy-start | bytes 9437188
  151.4 2.0 copy-start.15
  151.9 13.2 %collective-permute-start.1 = (bf16[512,384]{1,0:T(8,128)(2,1)S(1)}, bf16[512,384]{1,0:T(8,128)(2,1)S(1)}, u32[]{:S(2)}, u32[]{:S(2)}) collective-permute-start(bf16[512,384]{1,0:T(8,128)(2,1)S(1)} %get-tuple-element.144), channel_id=1, source_target_pairs={{0,1},{1,0},{2,3},{3,2},{4,5},{5,4},{6,7},{7,6},{8,9},{9,8},{10,11... | collective-permute-start | bytes 1179656 | tf_op jit(solution)/shard_map/ppermute | solution.py:1287
  155.4 9.7 %copy-start.18 = (bf16[768,768]{1,0:T(8,128)(2,1)S(1)}, bf16[768,768]{1,0:T(8,128)(2,1)}, u32[]{:S(2)}) copy-start(bf16[768,768]{1,0:T(8,128)(2,1)} %get-tuple-element.50) | copy-start | bytes 3538948
  155.4 12.1 %slice-start = ((s8[4718592]{0:T(1024)(128)(4,1)}), s8[4194304]{0:T(1024)(128)(4,1)S(1)}, s32[]{:S(2)}) async-start(s8[4718592]{0:T(1024)(128)(4,1)} %bitcast.78), calls=%async_computation | async-start | bytes 8388608
  165.1 2.4 slice-start.1
  166.0 11.5 %copy-start.5 = (f32[512,768]{1,0:T(8,128)}, f32[512,768]{1,0:T(8,128)S(1)}, u32[]{:S(2)}) copy-start(f32[512,768]{1,0:T(8,128)S(1)} %get-tuple-element.153) | copy-start | bytes 4718596
  166.7 10.8 %slice-start.2 = ((s8[4718592]{0:T(1024)(128)(4,1)}), s8[4194304]{0:T(1024)(128)(4,1)S(1)}, s32[]{:S(2)}) async-start(s8[4718592]{0:T(1024)(128)(4,1)} %bitcast.80), calls=%async_computation.2 | async-start | bytes 8388608
  166.9 10.6 %collective-permute-start.2 = (bf16[512,384]{1,0:T(8,128)(2,1)S(1)}, bf16[512,384]{1,0:T(8,128)(2,1)S(1)}, u32[]{:S(2)}, u32[]{:S(2)}) collective-permute-start(bf16[512,384]{1,0:T(8,128)(2,1)S(1)} %get-tuple-element.142), channel_id=1, source_target_pairs={{0,1},{1,0},{2,3},{3,2},{4,5},{5,4},{6,7},{7,6},{8,9},{9,8},{10,11... | collective-permute-start | bytes 1179656 | tf_op jit(solution)/shard_map/ppermute | solution.py:1287
  167.5 10.0 %slice-start.3 = ((s8[4718592]{0:T(1024)(128)(4,1)}), s8[524288]{0:T(1024)(128)(4,1)S(1)}, s32[]{:S(2)}) async-start(s8[4718592]{0:T(1024)(128)(4,1)} %bitcast.80), calls=%async_computation.3 | async-start | bytes 1048576
  167.5 14.4 %slice-start.4 = ((s8[4718592]{0:T(1024)(128)(4,1)}), s8[524288]{0:T(1024)(128)(4,1)S(1)}, s32[]{:S(2)}) async-start(s8[4718592]{0:T(1024)(128)(4,1)} %bitcast.82), calls=%async_computation.4 | async-start | bytes 1048576
  177.5 2.7 copy-start.13
  177.5 4.4 slice-start.5
  180.2 0.9 copy-start.8
  181.3 20.3 %collective-permute-start.3 = (bf16[512,512]{1,0:T(8,128)(2,1)S(1)}, bf16[512,512]{1,0:T(8,128)(2,1)S(1)}, u32[]{:S(2)}, u32[]{:S(2)}) collective-permute-start(bf16[512,512]{1,0:T(8,128)(2,1)S(1)} %get-tuple-element.123), channel_id=1, source_target_pairs={{0,1},{1,0},{2,3},{3,2},{4,5},{5,4},{6,7},{7,6},{8,9},{9,8},{10,11... | collective-permute-start | bytes 1572872 | tf_op jit(solution)/shard_map/ppermute | solution.py:1287
  182.0 2.7 copy-start.2
  206.6 50.5 %collective-permute-start.5 = (bf16[1024,512]{1,0:T(8,128)(2,1)S(1)}, bf16[1024,512]{1,0:T(8,128)(2,1)S(1)}, u32[]{:S(2)}, u32[]{:S(2)}) collective-permute-start(bf16[1024,512]{1,0:T(8,128)(2,1)S(1)} %get-tuple-element.57.refs_1_), channel_id=1, source_target_pairs={{0,1},{1,0},{2,3},{3,2},{4,5},{5,4},{6,7},{7,6},{8,9},{9,8},{10,11... | collective-permute-start | bytes 3145736 | tf_op jit(solution)/shard_map/ppermute | solution.py:1287
  208.6 48.6 %collective-permute-start.6 = (bf16[512,768]{1,0:T(8,128)(2,1)S(1)}, bf16[512,768]{1,0:T(8,128)(2,1)S(1)}, u32[]{:S(2)}, u32[]{:S(2)}) collective-permute-start(bf16[512,768]{1,0:T(8,128)(2,1)S(1)} %fusion.11.refs_1_), channel_id=1, source_target_pairs={{0,1},{1,0},{2,3},{3,2},{4,5},{5,4},{6,7},{7,6},{8,9},{9,8},{10,11... | collective-permute-start | bytes 2359304 | tf_op jit(solution)/shard_map/ppermute | solution.py:1287
  210.1 7.3 %copy-start.6 = (f32[512,768]{1,0:T(8,128)S(1)}, f32[512,768]{1,0:T(8,128)}, u32[]{:S(2)}) copy-start(f32[512,768]{1,0:T(8,128)} %copy-done.5) | copy-start | bytes 4718596
  223.6 1.3 copy-start.19
  238.3 2.0 copy-start.16
  240.3 2.0 copy-start.9
  242.4 14.7 %collective-permute-start.4 = (bf16[512,384]{1,0:T(8,128)(2,1)S(1)}, bf16[512,384]{1,0:T(8,128)(2,1)S(1)}, u32[]{:S(2)}, u32[]{:S(2)}) collective-permute-start(bf16[512,384]{1,0:T(8,128)(2,1)S(1)} %constant_dynamic-slice_fusion.5), channel_id=1, source_target_pairs={{0,1},{1,0},{2,3},{3,2},{4,5},{5,4},{6,7},{7,6},{8,9},{9,8},{10,11... | collective-permute-start | bytes 1179656 | tf_op jit(solution)/shard_map/ppermute | solution.py:1287
  254.0 3.9 copy-start.7
  258.6 18.8 %collective-permute-start.7 = (bf16[512,768]{1,0:T(8,128)(2,1)S(1)}, bf16[512,768]{1,0:T(8,128)(2,1)S(1)}, u32[]{:S(2)}, u32[]{:S(2)}) collective-permute-start(bf16[512,768]{1,0:T(8,128)(2,1)S(1)} %get-tuple-element.110.refs_1_), channel_id=1, source_target_pairs={{0,1},{1,0},{2,3},{3,2},{4,5},{5,4},{6,7},{7,6},{8,9},{9,8},{10,11... | collective-permute-start | bytes 2359304 | tf_op jit(solution)/shard_map/ppermute | solution.py:1287
  266.6 1.6 copy-start.14
  274.5 9.2 %copy-start = (f32[1,4,3072,128]{3,2,1,0:T(8,128)}, f32[1,4,3072,128]{3,2,1,0:T(8,128)S(1)}, u32[]{:S(2)}) copy-start(f32[1,4,3072,128]{3,2,1,0:T(8,128)S(1)} %grad_down_last.1) | copy-start | bytes 18874372
  283.8 2.6 copy-start.1
  286.4 198.4 %copy-start.11 = (f32[458878]{0:T(1024)S(1)}, f32[458878]{0:T(1024)}, u32[]{:S(2)}) copy-start(f32[458878]{0:T(1024)} %param.21) | copy-start | bytes 5506540
  482.8 1.9 copy-start.4
  482.8 2.0 copy-start.10

commit v8 on v7

--- a/solution.py
+++ b/solution.py
@@ -590,10 +590,11 @@
         def _():
             run(z + r, p, False, True)
 
-    for tick in range(LAYERS * number + 2 * GATHER_LAG):
+    lag = 4 if middle else GATHER_LAG
+    for tick in range(LAYERS * number + 2 * lag):
         both(tick, arrive)
-        both(tick - GATHER_LAG, lambda l, p, up_way, down_way: relay(l, p))
-        both(tick - 2 * GATHER_LAG, lambda l, p, up_way, down_way: finish(l, p))
+        both(tick - lag, lambda l, p, up_way, down_way: relay(l, p))
+        both(tick - 2 * lag, lambda l, p, up_way, down_way: finish(l, p))
 
     def settle_part(l, p):
         for kind in (0, 1):

time: 515 us -> 512 us (level)
  transfers between devices with their start and end apart: 8 -> 8, of which waited for: 4 -> 4; matrix products, arithmetic and copies ran while one was open for 7% -> 8% of each run, Pallas kernels for 16% -> 16%
where the time goes in v8:
time: 512 us; the launch traced here: 503 us
  Pallas kernels  404 us (79%)
  matrix products  36.9 us (7%)
  waiting for transfers between devices  21.7 us (4%)
  local copies, waits for them, and re-layouts  20.3 us (4%)
  other arithmetic  11.2 us (2%)
  starting transfers between devices  5.99 us (1%)
    pallas_call x1, Pallas kernels, reduce_to_owners(): pl.pallas_call(reduce_kernel, out_shape=(jax.ShapeDtypeStruct((CHUNK, BS)...  170 us
    pallas_call x2, Pallas kernels, gather_all(): pl.pallas_call(functools.partial(gather_kernel, parts, by_x, skip, middle...  123 us
    dot_general x11, matrix products, dot(): lax.dot_general(a, b, (dims, ((), ())), preferred_element_type=jnp.float32)  36.9 us
    pallas_call x7, Pallas kernels, grad_blocks(): pl.pallas_call(functools.partial(blocks_kernel, first_block, per_row, ste...  30.4 us
    ppermute x8, waiting for transfers between devices, swap_mp(): return lax.ppermute(values, 'mp', [(0, 1), (1, 0)])  21.7 us
    pallas_call x1, Pallas kernels, decoder(): pl.pallas_call(functools.partial(decoder_kernel, all_crops, devices), out...  16.3 us
    pallas_call x1, Pallas kernels, shampoo_step(): pl.pallas_call(functools.partial(shampoo_kernel, per_step), grid=(number...  16 us
    pallas_call x1, Pallas kernels, unblock(): pl.pallas_call(functools.partial(unblock_kernel, plan, len(shapes)), out_...  14.3 us
  transfers between devices with their start and end apart: 8, of which 4 were waited for; matrix products, arithmetic and copies ran while one was open for 8% of the time, Pallas kernels for 16%

profile of v8, /device:TPU:0, one launch (start us, length us, event | category | flops | bytes accessed | tf_op | source)
XLA Modules:
  0.0 502.9 jit_solution(7081590914635357715)
XLA Ops:
  0.6 1.5 convert_element_type.60
  2.2 100.6 %gather_weights.1 = bf16[2,16,3072,128]{3,2,1,0:T(8,128)(2,1)} custom-call(bf16[3072,128]{1,0:T(8,128)(2,1)S(1)} %bitcast.63), custom_call_target="tpu_custom_call" | custom-call | bytes 50331648 | tf_op jit(solution)/shard_map/gather_weights/pallas_call | solution.py:636
  103.4 7.4 %embed_other.1 = (f32[512,768]{1,0:T(8,128)}, bf16[2048,768]{1,0:T(8,128)(2,1)}) custom-call(s32[2]{0:T(128)} %pad_add_fusion.which_ref, bf16[1024,2048]{1,0:T(8,128)(2,1)} %rows_ref.1, bf16[2,384,128,128]{3,2,1,0:T(8,128)(2,1)} %bitcast.68), custom_call_target="tpu_custom_call" | custom-call | flops 1610612736 | bytes 10485760 | tf_op jit(solution)/shard_map/embed_other/pallas_call | solution.py:1138
  111.3 14.3 %unblock.1 = (bf16[768,2304]{1,0:T(8,128)(2,1)}, bf16[768,768]{1,0:T(8,128)(2,1)}, bf16[768,3072]{1,0:T(8,128)(2,1)}, bf16[3072,768]{1,0:T(8,128)(2,1)}, bf16[2304,1024]{1,0:T(8,128)(2,1)}) custom-call(bf16[2,384,128,128]{3,2,1,0:T(8,128)(2,1)} %bitcast.69), custom_call_target="tpu_custom_call" | custom-call | bytes 39845888 | tf_op jit(solution)/shard_map/unblock/pallas_call | solution.py:1100
  125.7 1.2 slice.158
  127.2 2.6 reshape.161
  131.1 1.6 arrange_labels.1.labels_ref
  133.9 3.0 constant_dynamic-slice_fusion.4
  136.9 10.8 %collective-permute-done = f32[512,768]{1,0:T(8,128)} collective-permute-done((f32[512,768]{1,0:T(8,128)}, f32[512,768]{1,0:T(8,128)}, u32[]{:S(2)}, u32[]{:S(2)}) %collective-permute-start) | collective-permute-done | bytes 1572896 | tf_op jit(solution)/shard_map/ppermute | solution.py:1288
  147.7 3.3 fusion.21
  152.5 0.9 copy-done.15
  153.4 2.0 fusion.6.qkv_q.qkv_k.qkv_v
  155.4 9.7 %attention_forward.1 = (bf16[512,768]{1,0:T(8,128)(2,1)S(1)}, f32[6,2,512]{2,1,0:T(2,128)S(1)}) custom-call(bf16[512,2304]{1,0:T(8,128)(2,1)S(1)} %fusion.6.qkv_q.qkv_k.qkv_v, bf16[512,2304]{1,0:T(8,128)(2,1)S(1)} %fusion.6.qkv_q.qkv_k.qkv_v, bf16[512,2304]{1,0:T(8,128)(2,1)S(1)} %fusion.6.qkv_q.qkv_k.qkv_v), custom_call_target="tpu_custom_call" | custom-call | flops 805306368 | bytes 3145728 | tf_op jit(solution)/shard_map/attention_forward/pallas_call | solution.py:137
  165.1 0.9 fusion.22
  167.5 5.0 multiply_convert_fusion
  172.6 5.0 collective-permute-done.2
  177.6 2.6 add_convert_fusion
  182.0 2.6 convolution_bitcast_fusion.up_ref
  184.6 16.3 %decoder.1 = (bf16[1024,512]{1,0:T(8,128)(2,1)S(1)}, f32[432,128]{1,0:T(8,128)S(1)}, f32[16,16]{1,0:T(8,128)S(1)}, f32[16,128]{1,0:T(8,128)S(1)}, f32[128,128]{1,0:T(8,128)S(1)}) custom-call(f32[1024,512]{1,0:T(8,128)S(1)} %convolution_bitcast_fusion.up_ref, f32[128,1]{1,0:T(8,128)S(1)} %copy.35.deconv_bias_ref, bf16[432,128]{1,0:T(8,128)(2,1)S(1)} %bitcast.65, ...), custom_call_target="tpu_custom_call" | custom-call | flops 1358954496 | bytes 6291456 | tf_op jit(solution)/shard_map/decoder/pallas_call | solution.py:1580
  201.6 5.0 fusion.23
  207.3 1.2 fusion.17
  208.6 1.5 collective-permute-start.6
  210.1 7.3 %convert_reduce_fusion = (f32[3072]{0:T(1024)S(1)}, bf16[512,3072]{1,0:T(8,128)(2,1)S(1)}) fusion(bf16[512,768]{1,0:T(8,128)(2,1)S(1)} %fusion.11.refs_1_, bf16[3072,768]{1,0:T(8,128)(2,1)} %get-tuple-element.53, f32[512,3072]{1,0:T(8,128)} %get-tuple-element.155, f32[3072]{0:T(1024)S(1)} %slice.171), kind=kOutput, calls=%fused_computation.7 | convolution fusion | flops 2436363264 | bytes 14966784 | tf_op jit(solution)/shard_map/dot_general | solution.py:43
  217.3 5.4 %multiply_reduce_fusion = (f32[768]{0:T(1024)S(1)}, f32[512]{0:T(512)S(1)}, f32[512]{0:T(512)S(1)}, f32[768]{0:T(1024)S(1)}, f32[512,768]{1,0:T(8,128)S(1)}) fusion(f32[512,768]{1,0:T(8,128)S(1)} %copy-done.6, f32[512]{0:T(512)S(1)} %add_rsqrt_fusion, f32[512]{0:T(512)S(1)} %broadcast_multiply_fusion.4, f32[768]{0:T(1024)S(1)} %get-tuple-element.126, ...), kind=kOutput, calls=%fused_computation.25 | convolution fusion | flops 2419455488 | bytes 11027456 | tf_op jit(solution)/shard_map/dot_general | solution.py:43
  222.7 0.9 fusion.15
  223.7 1.2 copy-done.19
  224.9 0.8 convolution_convert_fusion.gm_ref
  225.7 12.5 %attention_backward.1 = (bf16[512,768]{1,0:T(8,128)(2,1)S(1)}, bf16[512,768]{1,0:T(8,128)(2,1)S(1)}, bf16[512,768]{1,0:T(8,128)(2,1)S(1)}) custom-call(bf16[512,2304]{1,0:T(8,128)(2,1)S(1)} %fusion.6.qkv_q.qkv_k.qkv_v, bf16[512,2304]{1,0:T(8,128)(2,1)S(1)} %fusion.6.qkv_q.qkv_k.qkv_v, bf16[512,2304]{1,0:T(8,128)(2,1)S(1)} %fusion.6.qkv_q.qkv_k.qkv_v, ...), custom_call_target="tpu_custom_call" | custom-call | flops 2013265920 | bytes 5505024 | tf_op jit(solution)/shard_map/attention_backward/pallas_call | solution.py:161
  238.7 1.6 copy-done.16
  240.3 2.0 fusion.24
  243.5 4.6 grad_down.1.refs_2_
  248.1 6.0 %grad_up.1.refs_2_ = f32[2,8,3328,128]{3,2,1,0:T(8,128)} custom-call(bf16[512,768]{1,0:T(8,128)(2,1)S(1)} %get-tuple-element.132.refs_0_, bf16[512,3072]{1,0:T(8,128)(2,1)S(1)} %get-tuple-element.158.refs_1_, f32[2,8,3328,128]{3,2,1,0:T(8,128)} %grad_down.1.refs_2_), custom_call_target="tpu_custom_call", output_to_operand_aliasing={{}: (2, {})} | custom-call | flops 2415919104 | bytes 9437184 | tf_op jit(solution)/shard_map/grad_up/pallas_call | solution.py:1250
  254.0 3.1 collective-permute-done.4
  257.2 0.7 multiply_reduce_fusion.1
  259.3 2.2 grad_proj.1.refs_2_
  261.5 5.1 %grad_qkv.1.refs_13_ = f32[2,8,3328,128]{3,2,1,0:T(8,128)} custom-call(bf16[512,768]{1,0:T(8,128)(2,1)S(1)} %get-tuple-element.134.refs_0_, bf16[512,2304]{1,0:T(8,128)(2,1)S(1)} %slice_dynamic-update-slice_fusion.6.refs_1_, f32[2,8,3328,128]{3,2,1,0:T(8,128)} %grad_proj.1.refs_2_), custom_call_target="tpu_custom_call", output_to_operand_aliasing={{}: (2, {})} | custom-call | flops 1811939328 | bytes 7077888 | tf_op jit(solution)/shard_map/grad_qkv/pallas_call | solution.py:1250
  266.7 1.6 pack_aux.1
  268.4 4.9 grad_deconv.1.refs_4_
  273.3 1.2 grad_down_last.1
  274.5 2.8 collective-permute-done.7.refs_3_
  277.4 6.4 %grad_embed.1 = f32[1,4,3072,128]{3,2,1,0:T(8,128)S(1)} custom-call(bf16[512,2048]{1,0:T(8,128)(2,1)S(1)} %get-tuple-element.121.refs_0_, bf16[512,768]{1,0:T(8,128)(2,1)S(1)} %get-tuple-element.110.refs_1_, bf16[512,2048]{1,0:T(8,128)(2,1)S(1)} %get-tuple-element.120.refs_2_, bf16[512,768]{1,0:T(8,128)(2,1)S(1)} %collective-permute-done.7.refs_3_), custom_call_target="tpu_custom_call" | custom-call | flops 3221225472 | bytes 6291456 | tf_op jit(solution)/shard_map/grad_embed/pallas_call | solution.py:1250
  283.8 2.6 copy-done.1
  286.4 170.0 %reduce_to_owners.1 = (f32[3328,128]{1,0:T(8,128)}, f32[8,128]{1,0:T(8,128)}) custom-call(f32[2,2,2,2,3328,128]{5,4,3,2,1,0:T(8,128)} %bitcast.67, f32[2,2,3072,128]{3,2,1,0:T(8,128)} %bitcast.62, f32[2,2,3072,128]{3,2,1,0:T(8,128)} %bitcast.61), custom_call_target="tpu_custom_call" | custom-call | bytes 104857600 | tf_op jit(solution)/shard_map/reduce_to_owners/pallas_call | solution.py:983
  456.4 0.9 slice.195
  458.0 22.6 %gather_aux.1.sums_ref = f32[2,16,264,128]{3,2,1,0:T(8,128)S(1)} custom-call(f32[264,128]{1,0:T(8,128)S(1)} %pad_maximum_fusion.3.in_ref), custom_call_target="tpu_custom_call" | custom-call | bytes 4325376 | tf_op jit(solution)/shard_map/gather_aux/pallas_call | solution.py:636
  480.6 1.3 unpack_aux.1
  482.6 3.9 multiply_subtract_fusion
  486.5 16.0 %shampoo.1 = (f32[24,128,128]{2,1,0:T(8,128)}, f32[2,24,128,128]{3,2,1,0:T(8,128)}, f32[24,128,128]{2,1,0:T(8,128)}, f32[24,128,128]{2,1,0:T(8,128)}) custom-call(f32[1,1]{1,0:T(1,128)} %get-tuple-element.146.clip_ref, f32[3328,128]{1,0:T(8,128)} %get-tuple-element.73.g_ref, f32[24,128,128]{2,1,0:T(8,128)} %bitcast.72, f32[2,24,128,128]{3,2,1,0:T(8,128)} %bitcast.73, ...), custom_call_target="tpu_custom_call" | custom-call | flops 2415919104 | bytes 18874368 | tf_op jit(solution)/shard_map/shampoo/pallas_call | solution.py:1656
  (134 shorter events, 13.7 us)
Async XLA Ops:
  110.7 37.0 %collective-permute-start = (f32[512,768]{1,0:T(8,128)}, f32[512,768]{1,0:T(8,128)}, u32[]{:S(2)}, u32[]{:S(2)}) collective-permute-start(f32[512,768]{1,0:T(8,128)} %get-tuple-element.46), channel_id=1, source_target_pairs={{0,1},{1,0},{2,3},{3,2},{4,5},{5,4},{6,7},{7,6},{8,9},{9,8},{10,11... | collective-permute-start | bytes 4718600 | tf_op jit(solution)/shard_map/ppermute | solution.py:1288
  111.3 14.4 %copy-start.3 = (f32[458878]{0:T(1024)S(1)}, f32[458878]{0:T(1024)}, u32[]{:S(2)}) copy-start(f32[458878]{0:T(1024)} %param.19) | copy-start | bytes 5506540
  133.9 13.8 %copy-start.12 = (f32[512,768]{1,0:T(8,128)S(1)}, f32[512,768]{1,0:T(8,128)}, u32[]{:S(2)}) copy-start(f32[512,768]{1,0:T(8,128)} %reshape.161) | copy-start | bytes 4718596
  133.9 13.8 %copy-start.17 = (bf16[2048,768]{1,0:T(8,128)(2,1)S(1)}, bf16[2048,768]{1,0:T(8,128)(2,1)}, u32[]{:S(2)}) copy-start(bf16[2048,768]{1,0:T(8,128)(2,1)} %get-tuple-element.45) | copy-start | bytes 9437188
  151.4 2.0 copy-start.15
  151.9 13.2 %collective-permute-start.1 = (bf16[512,384]{1,0:T(8,128)(2,1)S(1)}, bf16[512,384]{1,0:T(8,128)(2,1)S(1)}, u32[]{:S(2)}, u32[]{:S(2)}) collective-permute-start(bf16[512,384]{1,0:T(8,128)(2,1)S(1)} %get-tuple-element.144), channel_id=1, source_target_pairs={{0,1},{1,0},{2,3},{3,2},{4,5},{5,4},{6,7},{7,6},{8,9},{9,8},{10,11... | collective-permute-start | bytes 1179656 | tf_op jit(solution)/shard_map/ppermute | solution.py:1288
  155.4 9.7 %copy-start.18 = (bf16[768,768]{1,0:T(8,128)(2,1)S(1)}, bf16[768,768]{1,0:T(8,128)(2,1)}, u32[]{:S(2)}) copy-start(bf16[768,768]{1,0:T(8,128)(2,1)} %get-tuple-element.50) | copy-start | bytes 3538948
  155.4 12.1 %slice-start = ((s8[4718592]{0:T(1024)(128)(4,1)}), s8[4194304]{0:T(1024)(128)(4,1)S(1)}, s32[]{:S(2)}) async-start(s8[4718592]{0:T(1024)(128)(4,1)} %bitcast.78), calls=%async_computation | async-start | bytes 8388608
  165.1 2.4 slice-start.1
  166.0 11.5 %copy-start.5 = (f32[512,768]{1,0:T(8,128)}, f32[512,768]{1,0:T(8,128)S(1)}, u32[]{:S(2)}) copy-start(f32[512,768]{1,0:T(8,128)S(1)} %get-tuple-element.153) | copy-start | bytes 4718596
  166.7 10.8 %slice-start.2 = ((s8[4718592]{0:T(1024)(128)(4,1)}), s8[4194304]{0:T(1024)(128)(4,1)S(1)}, s32[]{:S(2)}) async-start(s8[4718592]{0:T(1024)(128)(4,1)} %bitcast.80), calls=%async_computation.2 | async-start | bytes 8388608
  166.9 10.6 %collective-permute-start.2 = (bf16[512,384]{1,0:T(8,128)(2,1)S(1)}, bf16[512,384]{1,0:T(8,128)(2,1)S(1)}, u32[]{:S(2)}, u32[]{:S(2)}) collective-permute-start(bf16[512,384]{1,0:T(8,128)(2,1)S(1)} %get-tuple-element.142), channel_id=1, source_target_pairs={{0,1},{1,0},{2,3},{3,2},{4,5},{5,4},{6,7},{7,6},{8,9},{9,8},{10,11... | collective-permute-start | bytes 1179656 | tf_op jit(solution)/shard_map/ppermute | solution.py:1288
  167.5 10.0 %slice-start.3 = ((s8[4718592]{0:T(1024)(128)(4,1)}), s8[524288]{0:T(1024)(128)(4,1)S(1)}, s32[]{:S(2)}) async-start(s8[4718592]{0:T(1024)(128)(4,1)} %bitcast.80), calls=%async_computation.3 | async-start | bytes 1048576
  167.5 14.4 %slice-start.4 = ((s8[4718592]{0:T(1024)(128)(4,1)}), s8[524288]{0:T(1024)(128)(4,1)S(1)}, s32[]{:S(2)}) async-start(s8[4718592]{0:T(1024)(128)(4,1)} %bitcast.82), calls=%async_computation.4 | async-start | bytes 1048576
  177.5 2.7 copy-start.13
  177.5 4.4 slice-start.5
  180.2 0.9 copy-start.8
  181.3 20.3 %collective-permute-start.3 = (bf16[512,512]{1,0:T(8,128)(2,1)S(1)}, bf16[512,512]{1,0:T(8,128)(2,1)S(1)}, u32[]{:S(2)}, u32[]{:S(2)}) collective-permute-start(bf16[512,512]{1,0:T(8,128)(2,1)S(1)} %get-tuple-element.123), channel_id=1, source_target_pairs={{0,1},{1,0},{2,3},{3,2},{4,5},{5,4},{6,7},{7,6},{8,9},{9,8},{10,11... | collective-permute-start | bytes 1572872 | tf_op jit(solution)/shard_map/ppermute | solution.py:1288
  182.0 2.7 copy-start.2
  206.6 50.5 %collective-permute-start.5 = (bf16[1024,512]{1,0:T(8,128)(2,1)S(1)}, bf16[1024,512]{1,0:T(8,128)(2,1)S(1)}, u32[]{:S(2)}, u32[]{:S(2)}) collective-permute-start(bf16[1024,512]{1,0:T(8,128)(2,1)S(1)} %get-tuple-element.57.refs_1_), channel_id=1, source_target_pairs={{0,1},{1,0},{2,3},{3,2},{4,5},{5,4},{6,7},{7,6},{8,9},{9,8},{10,11... | collective-permute-start | bytes 3145736 | tf_op jit(solution)/shard_map/ppermute | solution.py:1288
  208.6 48.6 %collective-permute-start.6 = (bf16[512,768]{1,0:T(8,128)(2,1)S(1)}, bf16[512,768]{1,0:T(8,128)(2,1)S(1)}, u32[]{:S(2)}, u32[]{:S(2)}) collective-permute-start(bf16[512,768]{1,0:T(8,128)(2,1)S(1)} %fusion.11.refs_1_), channel_id=1, source_target_pairs={{0,1},{1,0},{2,3},{3,2},{4,5},{5,4},{6,7},{7,6},{8,9},{9,8},{10,11... | collective-permute-start | bytes 2359304 | tf_op jit(solution)/shard_map/ppermute | solution.py:1288
  210.1 7.3 %copy-start.6 = (f32[512,768]{1,0:T(8,128)S(1)}, f32[512,768]{1,0:T(8,128)}, u32[]{:S(2)}) copy-start(f32[512,768]{1,0:T(8,128)} %copy-done.5) | copy-start | bytes 4718596
  223.6 1.3 copy-start.19
  238.3 2.0 copy-start.16
  240.3 2.0 copy-start.9
  242.4 14.7 %collective-permute-start.4 = (bf16[512,384]{1,0:T(8,128)(2,1)S(1)}, bf16[512,384]{1,0:T(8,128)(2,1)S(1)}, u32[]{:S(2)}, u32[]{:S(2)}) collective-permute-start(bf16[512,384]{1,0:T(8,128)(2,1)S(1)} %constant_dynamic-slice_fusion.5), channel_id=1, source_target_pairs={{0,1},{1,0},{2,3},{3,2},{4,5},{5,4},{6,7},{7,6},{8,9},{9,8},{10,11... | collective-permute-start | bytes 1179656 | tf_op jit(solution)/shard_map/ppermute | solution.py:1288
  254.0 3.9 copy-start.7
  258.6 18.8 %collective-permute-start.7 = (bf16[512,768]{1,0:T(8,128)(2,1)S(1)}, bf16[512,768]{1,0:T(8,128)(2,1)S(1)}, u32[]{:S(2)}, u32[]{:S(2)}) collective-permute-start(bf16[512,768]{1,0:T(8,128)(2,1)S(1)} %get-tuple-element.110.refs_1_), channel_id=1, source_target_pairs={{0,1},{1,0},{2,3},{3,2},{4,5},{5,4},{6,7},{7,6},{8,9},{9,8},{10,11... | collective-permute-start | bytes 2359304 | tf_op jit(solution)/shard_map/ppermute | solution.py:1288
  266.6 1.6 copy-start.14
  274.5 9.2 %copy-start = (f32[1,4,3072,128]{3,2,1,0:T(8,128)}, f32[1,4,3072,128]{3,2,1,0:T(8,128)S(1)}, u32[]{:S(2)}) copy-start(f32[1,4,3072,128]{3,2,1,0:T(8,128)S(1)} %grad_down_last.1) | copy-start | bytes 18874372
  283.8 2.6 copy-start.1
  286.4 196.1 %copy-start.11 = (f32[458878]{0:T(1024)S(1)}, f32[458878]{0:T(1024)}, u32[]{:S(2)}) copy-start(f32[458878]{0:T(1024)} %param.21) | copy-start | bytes 5506540
  480.6 1.9 copy-start.4
  480.6 2.0 copy-start.10
